TPU v7x, 512 devices: a whole 4x4x16 slice. The times are simulated.
512 devices in a mesh: dp: 32 (over y, x, core), fsdp: 16 (over z).
Axes of the slice: x: 4, y: 4, z: 16, core: 2. Of those that a mesh axis runs over, the one named last changes fastest.
Arguments:
- patches: bfloat16 [1536, 1280, 128], P('dp', 'fsdp'), as said below
- patch_count: int32 [32, 48], P('dp'), may hold values from 0 to 128, as said below
- dest_rank: int32 [32, 48], P('dp'), may hold values from 0 to 31, as said below
- dest_slot: int32 [32, 48], P('dp'), may hold values from 0 to 23, as said below
- ln_gain: float32 [1280], replicated, may hold values from 0.5 to 1.5
- ln_bias: float32 [1280], replicated, may hold values from -3 to 3
- w_qkv: bfloat16 [3840, 1280], P('fsdp'), may hold values from -0.15625 to 0.15625
- b_qkv: bfloat16 [3840], P('fsdp'), may hold values from -3 to 3
Outputs:
- work_out: bfloat16 [768, 1280, 128], P('dp', 'fsdp')
Inputs may be any that keep to these rules, and one draw needn't show every extreme that they name: `patches`: rows beyond a block's patch count hold arbitrary values. `patch_count`: the nonempty blocks of all ranks number 32 * 24 in all. `dest_rank`: read only where patch_count > 0: each nonempty block goes to its home rank or to the rank whose index differs by 32 / 2 (modulo 32); every rank receives exactly 24 nonempty blocks, and a rank sends at most 24 blocks away. `dest_slot`: read only where patch_count > 0: the nonempty blocks that one rank receives have distinct slots.
All inputs are finite; a program needn't handle non-finite values.
Results may differ from a plain program's by a relative error of at most 0.0059.
Values may be sent and summed in bfloat16 or wider, within the bound.
No kernel may reach another device: no remote copies, remote signals or barrier semaphores. Data moves between devices by JAX's collectives and lax.ppermute only.
A program may use at most 64 MiB of HBM per device.

v0:
```python
import math

import jax
import jax.numpy as jnp
from jax import lax
from jax.sharding import PartitionSpec as P

HEAD_DIM = 80


def passed_along(value, axis, steps):
    count = lax.axis_size(axis)
    pairs = [(source, (source + steps) % count) for source in range(count)]
    return lax.ppermute(value, axis, pairs)


def attend(qkv_rows, counts, head_total):
    blocks_n, block_rows, _ = qkv_rows.shape
    divided = qkv_rows.reshape(blocks_n, block_rows, head_total, 3, HEAD_DIM)
    query_part = divided[:, :, :, 0]
    key_part = divided[:, :, :, 1]
    value_part = divided[:, :, :, 2]
    scores = jnp.einsum(
        "bqhd,bkhd->bhqk", query_part, key_part, preferred_element_type=jnp.float32
    ) / math.sqrt(HEAD_DIM)
    places = jnp.arange(block_rows, dtype=jnp.int32)
    inside = (places[None, :] < counts[:, None]).astype(jnp.float32)
    raised = jnp.exp(scores) * inside[:, None, None, :]
    totals = jnp.sum(raised, axis=-1, keepdims=True)
    totals = jnp.where(counts[:, None, None, None] > 0, totals, 1.0)
    weights = (raised / totals).astype(jnp.bfloat16)
    mixed = jnp.einsum("bhqk,bkhd->bhdq", weights, value_part, preferred_element_type=jnp.float32)
    mixed = mixed * inside[:, None, None, :]
    return mixed.reshape(blocks_n, head_total * HEAD_DIM, block_rows).astype(jnp.bfloat16)


def encode(blocks, counts, ln_gain, ln_bias, w_qkv, b_qkv):
    blocks_n, feat_share, block_rows = blocks.shape
    head_local = w_qkv.shape[0] // (3 * HEAD_DIM)
    values = blocks.astype(jnp.float32)
    moment_one = jnp.sum(values, axis=1)
    moment_two = jnp.sum(values * values, axis=1)
    total_one, total_two = lax.psum((moment_one, moment_two), "fsdp")
    feat_total = feat_share * lax.axis_size("fsdp")
    center = total_one / feat_total
    spread = total_two / feat_total - center * center
    feat_start = lax.axis_index("fsdp") * feat_share
    gain_local = lax.dynamic_slice_in_dim(ln_gain, feat_start, feat_share)
    bias_local = lax.dynamic_slice_in_dim(ln_bias, feat_start, feat_share)
    scaled = (values - center[:, None, :]) * lax.rsqrt(spread + 1e-06)[:, None, :]
    normed = (scaled * gain_local[:, None] + bias_local[:, None]).astype(jnp.bfloat16)
    projected = jnp.einsum(
        "bfr,cf->brc",
        lax.all_gather(normed, "fsdp", axis=1, tiled=True),
        w_qkv,
        preferred_element_type=jnp.float32,
    )
    qkv_rows = (projected + b_qkv.astype(jnp.float32)).astype(jnp.bfloat16)
    return attend(qkv_rows, counts, head_local)


def shards(patches, patch_count, dest_rank, dest_slot, ln_gain, ln_bias, w_qkv, b_qkv):
    rank_total = lax.axis_size("dp")
    own_rank = lax.axis_index("dp")
    home_blocks, feat_share, block_rows = patches.shape
    work_blocks = home_blocks // 2
    counts = patch_count[0]
    dest_ranks = dest_rank[0]
    dest_slots = dest_slot[0]
    occupied = counts > 0
    staying = occupied & (dest_ranks == own_rank)
    leaving = occupied & (dest_ranks != own_rank)
    positions = jnp.arange(home_blocks, dtype=jnp.int32)
    earlier = leaving[None, :] & (positions[None, :] < positions[:, None])
    leave_order = jnp.sum(earlier.astype(jnp.int32), axis=1)
    target = jnp.where(leaving, leave_order, work_blocks)
    matches = target[None, :] == jnp.arange(work_blocks, dtype=jnp.int32)[:, None]
    filled = jnp.any(matches, axis=1)
    chosen = jnp.sum(jnp.where(matches, positions[None, :], 0), axis=1)
    label_pack = jnp.stack(
        (jnp.where(filled, counts[chosen], 0), jnp.where(filled, dest_slots[chosen], 0)), axis=-1
    )
    label_pack = label_pack.astype(jnp.bfloat16)
    arrived, arrived_labels = passed_along(
        (patches[chosen] * filled[:, None, None].astype(patches.dtype), label_pack),
        "dp",
        rank_total // 2,
    )
    pool = jnp.concatenate([patches, arrived], axis=0)
    pool_counts = jnp.concatenate(
        [jnp.where(staying, counts, 0), arrived_labels[:, 0].astype(jnp.int32)]
    )
    pool_slots = jnp.concatenate([dest_slots, arrived_labels[:, 1].astype(jnp.int32)])
    pool_size = pool.shape[0]
    landing = (pool_slots[None, :] == jnp.arange(work_blocks, dtype=jnp.int32)[:, None]) & (
        pool_counts[None, :] > 0
    )
    present = jnp.any(landing, axis=1)
    source_index = jnp.sum(
        jnp.where(landing, jnp.arange(pool_size, dtype=jnp.int32)[None, :], 0), axis=1
    )
    work_rows = pool[source_index] * present[:, None, None].astype(pool.dtype)
    work_counts = jnp.sum(jnp.where(landing, pool_counts[None, :], 0), axis=1)
    work_rows, work_counts = (work_rows, work_counts)
    return encode(work_rows, work_counts, ln_gain, ln_bias, w_qkv, b_qkv)


def solution(mesh):
    placed = (
        P("dp", "fsdp", None),
        P("dp", None),
        P("dp", None),
        P("dp", None),
        P(),
        P(),
        P("fsdp", None),
        P("fsdp"),
    )
    return jax.shard_map(
        shards, mesh=mesh, in_specs=placed, out_specs=P("dp", "fsdp", None), check_vma=False
    )
```

profile of v0, /device:TPU:6, one launch (start us, length us, event | category | flops | bytes accessed | tf_op | source)
XLA Modules:
  0.0 209.1 jit_solution(18410961316031298741)
XLA Ops:
  6.5 0.0 copy-start
  6.5 0.0 copy-start.3
  6.5 0.0 copy-start.1
  6.5 0.0 copy-start.2
  6.5 0.0 all-gather.2.cloned.1.call-start
  6.6 0.7 fusion.17
  7.3 0.1 convert_reduce_fusion.1
  7.4 0.7 fusion.16
  8.1 0.1 select_reduce_fusion.2
  8.2 0.1 fusion.8
  8.4 1.4 gather_fusion.2
  9.7 1.4 gather_fusion.1
  11.1 5.1 %collective-permute-start.1 = (bf16[24,2]{0,1:T(2,128)(2,1)S(1)}, bf16[24,2]{0,1:T(2,128)(2,1)S(1)}, u32[]{:S(2)}, u32[]{:S(2)}) collective-permute-start(bf16[24,2]{0,1:T(2,128)(2,1)S(1)} %pad_maximum_fusion.1), channel_id=1, source_target_pairs={{0,256},{16,272},{32,288},{48,304},{64,320},{80,336},{96,352},{112... | collective-permute-start | bytes 296 | tf_op jit(solution)/shard_map/ppermute | solution.py:14
  16.2 1.8 gather_fusion
  18.1 0.1 broadcast_multiply_fusion
  18.2 2.2 %collective-permute-start = (bf16[24,80,128]{2,1,0:T(8,128)(2,1)S(1)}, bf16[24,80,128]{2,1,0:T(8,128)(2,1)S(1)}, u32[]{:S(2)}, u32[]{:S(2)}) collective-permute-start(bf16[24,80,128]{2,1,0:T(8,128)(2,1)S(1)} %broadcast_multiply_fusion), channel_id=1, source_target_pairs={{0,256},{16,272},{32,288},{48,304},{64,320},{80,336},{96,352},{112... | collective-permute-start | bytes 1474568 | tf_op jit(solution)/shard_map/ppermute | solution.py:14
  20.5 0.0 copy-done.3
  20.5 0.0 copy-done.1
  20.5 0.8 dynamic_slice.6
  21.3 0.8 dynamic_slice.7
  22.0 0.0 collective-permute-done.1
  22.1 0.1 add_compare_fusion
  22.1 0.0 copy-done.2
  22.1 0.1 pad_add_fusion
  22.2 0.1 fusion.10
  22.3 0.1 select_reduce_fusion.1
  22.5 11.8 %collective-permute-done = bf16[24,80,128]{2,1,0:T(8,128)(2,1)S(1)} collective-permute-done((bf16[24,80,128]{2,1,0:T(8,128)(2,1)S(1)}, bf16[24,80,128]{2,1,0:T(8,128)(2,1)S(1)}, u32[]{:S(2)}, u32[]{:S(2)}) %collective-permute-start) | collective-permute-done | bytes 491552 | tf_op jit(solution)/shard_map/ppermute | solution.py:14
  34.3 1.3 pad_maximum_fusion
  35.6 0.0 copy-start.4
  35.6 0.6 gather_fusion.3
  36.3 0.3 convert_reduce_fusion
  36.6 62.0 %all-reduce = (f32[24,128]{1,0:T(8,128)S(1)}, f32[24,128]{1,0:T(8,128)S(1)}) all-reduce(f32[24,128]{1,0:T(8,128)S(1)} %get-tuple-element.6, f32[24,128]{1,0:T(8,128)S(1)} %get-tuple-element.5), channel_id=1, replica_groups=mesh['dp'=32,'fsdp'=16] {'fsdp'}, use_global_device_ids=true, to_apply=%region_8.9 | all-reduce | flops 6144 | bytes 49152 | tf_op jit(solution)/shard_map/psum | solution.py:43
  98.6 1.3 fusion.4
  99.9 0.0 all-gather.2.cloned.1.call-update
  99.9 0.0 copy-done.4
  99.9 0.1 fusion.11
  100.0 94.6 %all-gather.2.cloned.1.call-done = bf16[24,1280,128]{2,1,0:T(8,128)(2,1)} async-done(((bf16[24,80,128]{2,1,0:T(8,128)(2,1)}), bf16[24,1280,128]{2,1,0:T(8,128)(2,1)}) %all-gather.2.cloned.1.call-update) | async-done | bytes 7864336 | tf_op jit(solution)/shard_map/all_gather | solution.py:54
  194.6 0.0 copy-done
  194.6 5.3 %add_convert_fusion = bf16[24,128,240]{1,2,0:T(8,128)(2,1)S(1)} fusion(bf16[24,1280,128]{2,1,0:T(8,128)(2,1)} %all-gather.2.cloned.1.call-done, f32[240]{0:T(256)S(1)} %convert_element_type.69, bf16[240,1280]{1,0:T(8,128)(2,1)S(1)} %copy-done), kind=kOutput, calls=%fused_computation.4 | convolution fusion | flops 1888911360 | bytes 9954240 | tf_op jit(solution)/shard_map/bfr,cf->brc/dot_general | solution.py:52
  199.9 1.0 fusion.18
  201.0 0.1 broadcast_select_fusion
  201.0 1.2 fusion
  (13 shorter events, 0.1 us)
Async XLA Ops:
  6.5 188.1 %copy-start = (bf16[240,1280]{1,0:T(8,128)(2,1)S(1)}, bf16[240,1280]{1,0:T(8,128)(2,1)}, u32[]{:S(2)}) copy-start(bf16[240,1280]{1,0:T(8,128)(2,1)} %param.14) | copy-start | bytes 1843204
  6.5 13.9 %copy-start.3 = (s32[1,48]{1,0:T(1,128)S(1)}, s32[1,48]{1,0:T(1,128)}, u32[]{:S(2)}) copy-start(s32[1,48]{1,0:T(1,128)} %param.10) | copy-start | bytes 580
  6.5 13.9 %copy-start.1 = (s32[1,48]{1,0:T(1,128)S(1)}, s32[1,48]{1,0:T(1,128)}, u32[]{:S(2)}) copy-start(s32[1,48]{1,0:T(1,128)} %param.9) | copy-start | bytes 580
  6.5 15.6 %copy-start.2 = (s32[1,48]{1,0:T(1,128)S(1)}, s32[1,48]{1,0:T(1,128)}, u32[]{:S(2)}) copy-start(s32[1,48]{1,0:T(1,128)} %param.11) | copy-start | bytes 580
  6.5 188.1 %all-gather.2.cloned.1.call-start = ((), (), s32[]{:S(2)}) async-start(), calls=%async_computation | async-start | bytes 8355840 | tf_op jit(solution)/shard_map/all_gather | solution.py:54
  11.1 10.9 %collective-permute-start.1 = (bf16[24,2]{0,1:T(2,128)(2,1)S(1)}, bf16[24,2]{0,1:T(2,128)(2,1)S(1)}, u32[]{:S(2)}, u32[]{:S(2)}) collective-permute-start(bf16[24,2]{0,1:T(2,128)(2,1)S(1)} %pad_maximum_fusion.1), channel_id=1, source_target_pairs={{0,256},{16,272},{32,288},{48,304},{64,320},{80,336},{96,352},{112... | collective-permute-start | bytes 296 | tf_op jit(solution)/shard_map/ppermute | solution.py:14
  18.2 16.1 %collective-permute-start = (bf16[24,80,128]{2,1,0:T(8,128)(2,1)S(1)}, bf16[24,80,128]{2,1,0:T(8,128)(2,1)S(1)}, u32[]{:S(2)}, u32[]{:S(2)}) collective-permute-start(bf16[24,80,128]{2,1,0:T(8,128)(2,1)S(1)} %broadcast_multiply_fusion), channel_id=1, source_target_pairs={{0,256},{16,272},{32,288},{48,304},{64,320},{80,336},{96,352},{112... | collective-permute-start | bytes 1474568 | tf_op jit(solution)/shard_map/ppermute | solution.py:14
  35.6 64.3 %copy-start.4 = (bf16[240]{0:T(256)(128)(2,1)S(1)}, bf16[240]{0:T(256)(128)(2,1)}, u32[]{:S(2)}) copy-start(bf16[240]{0:T(256)(128)(2,1)} %param.15) | copy-start | bytes 1444
Sparse Core Ops, SparseCore 0:
  100.0 94.5 all-gather.1
where the time goes:
time: 210 us; the launch traced here: 209 us
  waiting for transfers between devices  106 us (50%)
  blocking collectives  62 us (30%)
  between operations  13.6 us (6%)
  matrix products  7.56 us (4%)
  starting transfers between devices  7.38 us (4%)
  local copies, waits for them, and re-layouts  6.77 us (3%)
  other arithmetic  5.35 us (3%)
    all_gather x1, waiting for transfers between devices, encode(): lax.all_gather(normed, 'fsdp', axis=1, tiled=True)  94.6 us
    psum x1, blocking collectives, encode(): total_one, total_two = lax.psum((moment_one, moment_two), 'fsdp')  62 us
    ppermute x2, waiting for transfers between devices, passed_along(): return lax.ppermute(value, axis, pairs)  11.8 us
    ppermute x2, starting transfers between devices, passed_along(): return lax.ppermute(value, axis, pairs)  7.35 us
    dot_general x1, matrix products, encode(): jnp.einsum('bfr,cf->brc', lax.all_gather(normed, 'fsdp', axis=1, tiled=Tr...  5.3 us
  transfers between devices with their start and end apart: 3, of which 2 were waited for; matrix products, arithmetic and copies ran while one was open for 2% of the time, Pallas kernels for 0%

commit v1 on v0

--- a/solution.py
+++ b/solution.py
@@ -35,23 +35,17 @@
 
 
 def encode(blocks, counts, ln_gain, ln_bias, w_qkv, b_qkv):
-    blocks_n, feat_share, block_rows = blocks.shape
     head_local = w_qkv.shape[0] // (3 * HEAD_DIM)
-    values = blocks.astype(jnp.float32)
-    moment_one = jnp.sum(values, axis=1)
-    moment_two = jnp.sum(values * values, axis=1)
-    total_one, total_two = lax.psum((moment_one, moment_two), "fsdp")
-    feat_total = feat_share * lax.axis_size("fsdp")
-    center = total_one / feat_total
-    spread = total_two / feat_total - center * center
-    feat_start = lax.axis_index("fsdp") * feat_share
-    gain_local = lax.dynamic_slice_in_dim(ln_gain, feat_start, feat_share)
-    bias_local = lax.dynamic_slice_in_dim(ln_bias, feat_start, feat_share)
+    gathered = lax.all_gather(blocks, "fsdp", axis=1, tiled=True)
+    values = gathered.astype(jnp.float32)
+    feat_total = values.shape[1]
+    center = jnp.sum(values, axis=1) / feat_total
+    spread = jnp.sum(values * values, axis=1) / feat_total - center * center
     scaled = (values - center[:, None, :]) * lax.rsqrt(spread + 1e-06)[:, None, :]
-    normed = (scaled * gain_local[:, None] + bias_local[:, None]).astype(jnp.bfloat16)
+    normed = (scaled * ln_gain[:, None] + ln_bias[:, None]).astype(jnp.bfloat16)
     projected = jnp.einsum(
         "bfr,cf->brc",
-        lax.all_gather(normed, "fsdp", axis=1, tiled=True),
+        normed,
         w_qkv,
         preferred_element_type=jnp.float32,
     )

time: 210 us -> 159 us (0.76)
  blocking collectives: 62 us -> 0 us
  waiting for transfers between devices: 106 us -> 116 us
  other arithmetic: 5.35 us -> 9 us
    psum x1 -> x0, blocking collectives: 62 us -> none  [encode(): total_one, total_two = lax.psum((moment_one, moment_two), 'fsdp')]
    all_gather x1, waiting for transfers between devices: 94.6 us -> 103 us  [encode(): gathered = lax.all_gather(blocks, 'fsdp', axis=1, tiled=True)]
    reduce_sum x1, other arithmetic: 0.27 us -> 5.45 us  [encode(): center = jnp.sum(values, axis=1) / feat_total]
where the time goes in v1:
time: 159 us; the launch traced here: 158 us
  waiting for transfers between devices  116 us (73%)
  between operations  13.6 us (9%)
  other arithmetic  9 us (6%)
  starting transfers between devices  7.38 us (5%)
  matrix products  6.25 us (4%)
  local copies, waits for them, and re-layouts  5.24 us (3%)
    all_gather x1, waiting for transfers between devices, encode(): gathered = lax.all_gather(blocks, 'fsdp', axis=1, tiled=True)  103 us
    ppermute x2, waiting for transfers between devices, passed_along(): return lax.ppermute(value, axis, pairs)  13.3 us
    ppermute x2, starting transfers between devices, passed_along(): return lax.ppermute(value, axis, pairs)  7.35 us
    reduce_sum x1, other arithmetic, encode(): center = jnp.sum(values, axis=1) / feat_total  5.45 us
    dot_general x1, matrix products, encode(): jnp.einsum('bfr,cf->brc', normed, w_qkv, preferred_element_type=jnp.float32)  3.99 us
  transfers between devices with their start and end apart: 3, of which 2 were waited for; matrix products, arithmetic and copies ran while one was open for 2% of the time, Pallas kernels for 0%

profile of v1, /device:TPU:6, one launch (start us, length us, event | category | flops | bytes accessed | tf_op | source)
XLA Modules:
  0.0 157.8 jit_solution(7824315311612844439)
XLA Ops:
  6.5 0.0 copy-start
  6.5 0.0 copy-start.5
  6.5 0.0 copy-start.1
  6.5 0.0 copy-start.2
  6.5 0.0 copy-start.4
  6.6 0.0 all-gather.2.cloned.1.call-start
  6.6 0.8 fusion.21
  7.4 0.1 convert_reduce_fusion.1
  7.5 0.7 fusion.20
  8.2 0.1 select_reduce_fusion.2
  8.3 0.1 fusion.12
  8.4 1.4 gather_fusion.2
  9.8 1.4 gather_fusion.1
  11.2 5.1 %collective-permute-start.1 = (bf16[24,2]{0,1:T(2,128)(2,1)S(1)}, bf16[24,2]{0,1:T(2,128)(2,1)S(1)}, u32[]{:S(2)}, u32[]{:S(2)}) collective-permute-start(bf16[24,2]{0,1:T(2,128)(2,1)S(1)} %pad_maximum_fusion.1), channel_id=1, source_target_pairs={{0,256},{16,272},{32,288},{48,304},{64,320},{80,336},{96,352},{112... | collective-permute-start | bytes 296 | tf_op jit(solution)/shard_map/ppermute | solution.py:14
  16.3 1.8 %gather_fusion = bf16[24,80,128]{2,1,0:T(8,128)(2,1)S(1)} fusion(bf16[48,80,128]{2,1,0:T(8,128)(2,1)} %param.8, s32[1024]{0:T(1024)S(1)} %pad_clamp_fusion.1), kind=kCustom, calls=%fused_computation | custom fusion | bytes 983136 | tf_op jit(solution)/shard_map/gather | solution.py:79
  18.2 0.1 broadcast_multiply_fusion.1
  18.3 2.2 %collective-permute-start = (bf16[24,80,128]{2,1,0:T(8,128)(2,1)S(1)}, bf16[24,80,128]{2,1,0:T(8,128)(2,1)S(1)}, u32[]{:S(2)}, u32[]{:S(2)}) collective-permute-start(bf16[24,80,128]{2,1,0:T(8,128)(2,1)S(1)} %broadcast_multiply_fusion.1), channel_id=1, source_target_pairs={{0,256},{16,272},{32,288},{48,304},{64,320},{80,336},{96,352},{112... | collective-permute-start | bytes 1474568 | tf_op jit(solution)/shard_map/ppermute | solution.py:14
  20.5 0.0 copy-done.5
  20.5 0.0 copy-done.1
  20.6 0.0 collective-permute-done.1
  20.6 0.1 add_compare_fusion
  20.7 0.0 copy-done.2
  20.7 0.1 pad_add_fusion
  20.7 0.1 fusion.14
  20.9 0.1 select_reduce_fusion.1
  21.0 13.3 %collective-permute-done = bf16[24,80,128]{2,1,0:T(8,128)(2,1)S(1)} collective-permute-done((bf16[24,80,128]{2,1,0:T(8,128)(2,1)S(1)}, bf16[24,80,128]{2,1,0:T(8,128)(2,1)S(1)}, u32[]{:S(2)}, u32[]{:S(2)}) %collective-permute-start) | collective-permute-done | bytes 491552 | tf_op jit(solution)/shard_map/ppermute | solution.py:14
  34.3 0.0 copy-done.4
  34.4 0.1 pad_maximum_fusion
  34.5 0.0 copy-start.8
  34.5 0.6 gather_fusion.3
  35.1 0.9 broadcast_multiply_fusion
  36.0 0.0 all-gather.2.cloned.1.call-update
  36.1 0.0 copy-done.8
  36.1 0.1 fusion.15
  36.2 0.0 copy-start.6
  36.2 0.0 copy-start.7
  36.2 103.0 %all-gather.2.cloned.1.call-done = bf16[24,1280,128]{2,1,0:T(8,128)(2,1)} async-done(((bf16[24,80,128]{2,1,0:T(8,128)(2,1)}), bf16[24,1280,128]{2,1,0:T(8,128)(2,1)}) %all-gather.2.cloned.1.call-update) | async-done | bytes 7864336 | tf_op jit(solution)/shard_map/all_gather | solution.py:39
  139.2 0.0 copy-start.3
  139.2 5.5 %convert_reduce_fusion = (f32[24,128]{1,0:T(8,128)S(1)}, f32[24,128]{1,0:T(8,128)S(1)}) fusion(bf16[24,1280,128]{2,1,0:T(8,128)(2,1)} %all-gather.2.cloned.1.call-done), kind=kLoop, calls=%fused_computation.6 | loop fusion | flops 15722496 | bytes 7888896 | tf_op jit(solution)/shard_map/reduce_sum | solution.py:42
  144.6 0.0 copy-done
  144.6 0.0 copy-done.6
  144.6 0.0 copy-done.7
  144.7 0.0 copy-done.3
  144.7 4.0 %add_convert_fusion = bf16[24,128,240]{1,2,0:T(8,128)(2,1)S(1)} fusion(bf16[24,1280,128]{2,1,0:T(8,128)(2,1)S(1)} %copy-done.3, f32[1280]{0:T(1024)S(1)} %copy-done.6, f32[1280]{0:T(1024)S(1)} %copy-done.7, f32[24,128]{1,0:T(8,128)S(1)} %get-tuple-element.10, f32[24,128]{1,0:T(8,128)S(1)} %get-tuple-element.9, f32[240]{0:T(256)S(1)} %convert_element_type.69, ...), kind=kOutput, calls=%fused_computation.13 | convolution fusion | flops 1912504320 | bytes 9989056 | tf_op jit(solution)/shard_map/bfr,cf->brc/dot_general | solution.py:46
  148.7 1.0 fusion.22
  149.7 0.1 broadcast_select_fusion
  149.8 1.2 fusion.9
  (13 shorter events, 0.1 us)
Async XLA Ops:
  6.5 138.1 %copy-start = (bf16[240,1280]{1,0:T(8,128)(2,1)S(1)}, bf16[240,1280]{1,0:T(8,128)(2,1)}, u32[]{:S(2)}) copy-start(bf16[240,1280]{1,0:T(8,128)(2,1)} %param.14) | copy-start | bytes 1843204
  6.5 14.0 %copy-start.5 = (s32[1,48]{1,0:T(1,128)S(1)}, s32[1,48]{1,0:T(1,128)}, u32[]{:S(2)}) copy-start(s32[1,48]{1,0:T(1,128)} %param.10) | copy-start | bytes 580
  6.5 14.0 %copy-start.1 = (s32[1,48]{1,0:T(1,128)S(1)}, s32[1,48]{1,0:T(1,128)}, u32[]{:S(2)}) copy-start(s32[1,48]{1,0:T(1,128)} %param.9) | copy-start | bytes 580
  6.5 14.1 %copy-start.2 = (s32[1,48]{1,0:T(1,128)S(1)}, s32[1,48]{1,0:T(1,128)}, u32[]{:S(2)}) copy-start(s32[1,48]{1,0:T(1,128)} %param.11) | copy-start | bytes 580
  6.5 27.8 %copy-start.4 = (bf16[48,80,128]{2,1,0:T(8,128)(2,1)S(1)}, bf16[48,80,128]{2,1,0:T(8,128)(2,1)}, u32[]{:S(2)}) copy-start(bf16[48,80,128]{2,1,0:T(8,128)(2,1)} %param.8) | copy-start | bytes 2949124
  6.6 132.6 %all-gather.2.cloned.1.call-start = ((), (), s32[]{:S(2)}) async-start(), calls=%async_computation | async-start | bytes 8355840 | tf_op jit(solution)/shard_map/all_gather | solution.py:39
  11.2 9.4 %collective-permute-start.1 = (bf16[24,2]{0,1:T(2,128)(2,1)S(1)}, bf16[24,2]{0,1:T(2,128)(2,1)S(1)}, u32[]{:S(2)}, u32[]{:S(2)}) collective-permute-start(bf16[24,2]{0,1:T(2,128)(2,1)S(1)} %pad_maximum_fusion.1), channel_id=1, source_target_pairs={{0,256},{16,272},{32,288},{48,304},{64,320},{80,336},{96,352},{112... | collective-permute-start | bytes 296 | tf_op jit(solution)/shard_map/ppermute | solution.py:14
  18.3 16.1 %collective-permute-start = (bf16[24,80,128]{2,1,0:T(8,128)(2,1)S(1)}, bf16[24,80,128]{2,1,0:T(8,128)(2,1)S(1)}, u32[]{:S(2)}, u32[]{:S(2)}) collective-permute-start(bf16[24,80,128]{2,1,0:T(8,128)(2,1)S(1)} %broadcast_multiply_fusion.1), channel_id=1, source_target_pairs={{0,256},{16,272},{32,288},{48,304},{64,320},{80,336},{96,352},{112... | collective-permute-start | bytes 1474568 | tf_op jit(solution)/shard_map/ppermute | solution.py:14
  34.5 1.6 copy-start.8
  36.2 108.5 %copy-start.6 = (f32[1280]{0:T(1024)S(1)}, f32[1280]{0:T(1024)}, u32[]{:S(2)}) copy-start(f32[1280]{0:T(1024)} %param.13) | copy-start | bytes 15364
  36.2 108.5 %copy-start.7 = (f32[1280]{0:T(1024)S(1)}, f32[1280]{0:T(1024)}, u32[]{:S(2)}) copy-start(f32[1280]{0:T(1024)} %param.12) | copy-start | bytes 15364
  139.2 5.5 %copy-start.3 = (bf16[24,1280,128]{2,1,0:T(8,128)(2,1)S(1)}, bf16[24,1280,128]{2,1,0:T(8,128)(2,1)}, u32[]{:S(2)}) copy-start(bf16[24,1280,128]{2,1,0:T(8,128)(2,1)} %all-gather.2.cloned.1.call-done) | copy-start | bytes 23592964
Sparse Core Ops, SparseCore 0:
  36.2 102.9 all-gather.1

commit v2 on v1

v2 whole, which is shorter than its diff:
```python
import math

import jax
import jax.numpy as jnp
from jax import lax
from jax.experimental import pallas as pl
from jax.experimental.pallas import tpu as pltpu
from jax.sharding import PartitionSpec as P

HEAD_DIM = 80
GROUP = 4


def encode_kernel(starts, counts, weight, column_sum, shift, *refs):
    pieces, out, rows, qkv = refs[:-3], refs[-3], refs[-2], refs[-1]
    feat_share, block_rows = out.shape[1], out.shape[2]
    columns_n = qkv.shape[0]
    feat_total = feat_share * len(pieces)
    step = pl.program_id(0)
    squares = []
    for block in range(GROUP):
        columns = slice(block * block_rows, (block + 1) * block_rows)
        sum_two = jnp.zeros((feat_share, block_rows), jnp.float32)
        for index, piece in enumerate(pieces):
            raw = piece[block]
            rows[pl.ds(pl.multiple_of(starts[index], 16), feat_share), columns] = raw
            values = raw.astype(jnp.float32)
            sum_two += values * values
        squares.append(jnp.sum(sum_two, axis=0, keepdims=True))
    product = jnp.dot(weight[...], rows[...], preferred_element_type=jnp.float32)
    center = product[columns_n : columns_n + 1] / feat_total
    spread = jnp.concatenate(squares, axis=1) / feat_total - center * center
    scale = lax.rsqrt(spread + 1e-06)
    projected = (product[:columns_n] - column_sum[...] * center) * scale + shift[...]
    qkv[...] = projected.astype(jnp.bfloat16)
    key_place = lax.broadcasted_iota(jnp.int32, (block_rows, block_rows), 0)
    row_place = lax.broadcasted_iota(jnp.int32, (feat_share, block_rows), 1)
    for block in range(GROUP):
        count = counts[step * GROUP + block]
        columns = slice(block * block_rows, (block + 1) * block_rows)
        query_part = qkv[0:HEAD_DIM, columns]
        key_part = qkv[HEAD_DIM : 2 * HEAD_DIM, columns]
        value_part = qkv[2 * HEAD_DIM : 3 * HEAD_DIM, columns]
        scores = lax.dot_general(
            key_part, query_part, (((0,), (0,)), ((), ())), preferred_element_type=jnp.float32
        ) * (1.0 / math.sqrt(HEAD_DIM))
        raised = jnp.where(key_place < count, jnp.exp(scores), 0.0)
        totals = jnp.sum(raised, axis=0, keepdims=True)
        totals = jnp.where(count > 0, totals, 1.0)
        weights = (raised * (1.0 / totals)).astype(jnp.bfloat16)
        mixed = jnp.dot(value_part, weights, preferred_element_type=jnp.float32)
        out[block] = jnp.where(row_place < count, mixed, 0.0).astype(jnp.bfloat16)


def folded(ln_gain, ln_bias, w_qkv, b_qkv):
    wide = w_qkv.astype(jnp.float32)
    scaled = (wide * ln_gain[None, :]).astype(jnp.bfloat16)
    column_sum = jnp.sum(scaled.astype(jnp.float32), axis=1, keepdims=True)
    shift = jnp.sum(wide * ln_bias[None, :], axis=1) + b_qkv.astype(jnp.float32)
    ones = jnp.ones((16, w_qkv.shape[1]), jnp.bfloat16)
    return jnp.concatenate([scaled, ones], axis=0), column_sum, shift[:, None]


def encode(pieces, starts, counts, weight, column_sum, shift):
    blocks_n, feat_share, block_rows = pieces[0].shape
    feat_total = feat_share * len(pieces)
    columns_n = column_sum.shape[0]

    def whole(step, starts_ref, counts_ref):
        return (0, 0)

    def group(step, starts_ref, counts_ref):
        return (step, 0, 0)

    block_spec = pl.BlockSpec((GROUP, feat_share, block_rows), group)
    return pl.pallas_call(
        encode_kernel,
        grid_spec=pltpu.PrefetchScalarGridSpec(
            num_scalar_prefetch=2,
            grid=(blocks_n // GROUP,),
            in_specs=[
                pl.BlockSpec(weight.shape, whole),
                pl.BlockSpec((columns_n, 1), whole),
                pl.BlockSpec((columns_n, 1), whole),
            ]
            + [block_spec] * len(pieces),
            out_specs=block_spec,
            scratch_shapes=[
                pltpu.VMEM((feat_total, GROUP * block_rows), jnp.bfloat16),
                pltpu.VMEM((columns_n, GROUP * block_rows), jnp.bfloat16),
            ],
        ),
        out_shape=jax.ShapeDtypeStruct((blocks_n, feat_share, block_rows), jnp.bfloat16),
        compiler_params=pltpu.CompilerParams(vmem_limit_bytes=60 * 2**20),
        cost_estimate=pl.CostEstimate(
            flops=2 * blocks_n * block_rows * columns_n * feat_total,
            bytes_accessed=2 * feat_total * blocks_n * block_rows,
            transcendentals=blocks_n * block_rows * block_rows,
        ),
    )(starts, counts, weight, column_sum, shift, *pieces)


def rebalance(patches, counts, dest_ranks, dest_slots):
    rank_total = lax.axis_size("dp")
    own_rank = lax.axis_index("dp")
    home_blocks = patches.shape[0]
    work_blocks = home_blocks // 2
    occupied = counts > 0
    staying = occupied & (dest_ranks == own_rank)
    leaving = occupied & (dest_ranks != own_rank)
    positions = jnp.arange(home_blocks, dtype=jnp.int32)
    work_slots = jnp.arange(work_blocks, dtype=jnp.int32)
    earlier = leaving[None, :] & (positions[None, :] < positions[:, None])
    leave_order = jnp.sum(earlier.astype(jnp.int32), axis=1)
    target = jnp.where(leaving, leave_order, work_blocks)
    matches = target[None, :] == work_slots[:, None]

    def picked(values):
        return jnp.sum(jnp.where(matches, values[None, :], 0), axis=1)

    pairs = [(source, (source + rank_total // 2) % rank_total) for source in range(rank_total)]
    labels = jnp.stack((picked(counts), picked(dest_slots)), axis=0).astype(patches.dtype)
    label_block = jnp.zeros((1,) + patches.shape[1:], patches.dtype)
    label_block = lax.dynamic_update_slice(label_block, labels[None], (0, 0, 0))
    message = jnp.concatenate([patches[picked(positions)], label_block], axis=0)
    arrived = lax.ppermute(message, "dp", pairs)
    arrived_labels = arrived[work_blocks, :2, :work_blocks].astype(jnp.int32)
    arrived = arrived[:work_blocks]
    pool = jnp.concatenate([patches, arrived], axis=0)
    pool_counts = jnp.concatenate([jnp.where(staying, counts, 0), arrived_labels[0]])
    pool_slots = jnp.concatenate([dest_slots, arrived_labels[1]])
    landing = (pool_slots[None, :] == work_slots[:, None]) & (pool_counts[None, :] > 0)
    pool_places = jnp.arange(pool.shape[0], dtype=jnp.int32)
    source_index = jnp.sum(jnp.where(landing, pool_places[None, :], 0), axis=1)
    work_counts = jnp.sum(jnp.where(landing, pool_counts[None, :], 0), axis=1)
    return pool[source_index], work_counts


def gather_pieces(own):
    rank_total, ring = lax.axis_size("dp"), lax.axis_size("fsdp")
    swaps = [(rank, rank ^ 1) for rank in range(rank_total)]
    hops = [
        (rank * ring + place, rank * ring + (place + 1 - 2 * (rank % 2)) % ring)
        for rank in range(rank_total)
        for place in range(ring)
    ]

    def swap(value):
        return lax.ppermute(value, "dp", swaps)

    def hop(value):
        return lax.ppermute(value, ("dp", "fsdp"), hops)

    place = lax.axis_index("fsdp")
    sense = 1 - 2 * (lax.axis_index("dp") % 2)
    pieces, origins = [own], [place]
    mine, other = hop(own), swap(own)
    swaps_done = []
    for step in range(1, ring // 2 + 1):
        pieces.append(mine)
        origins.append((place - sense * step) % ring)
        if step < ring // 2:
            received = other = hop(other)
            if step > 2:
                other, swaps_done[step - 3] = lax.optimization_barrier((other, swaps_done[step - 3]))
            mine = hop(mine)
            swaps_done.append(swap(received))
            origins.append((place + sense * step) % ring)
    first, rest = pieces[0], pieces[1:]
    pieces = [first]
    for step in range(len(rest)):
        pieces.append(rest[step])
        if step < len(swaps_done):
            pieces.append(swaps_done[step])
    return pieces, jnp.stack(origins).astype(jnp.int32)


def shards(patches, patch_count, dest_rank, dest_slot, ln_gain, ln_bias, w_qkv, b_qkv):
    work_rows, work_counts = rebalance(patches, patch_count[0], dest_rank[0], dest_slot[0])
    weight, column_sum, shift = folded(ln_gain, ln_bias, w_qkv, b_qkv)
    work_rows, weight, column_sum, shift = lax.optimization_barrier(
        (work_rows, weight, column_sum, shift)
    )
    pieces, origins = gather_pieces(work_rows)
    starts = origins * patches.shape[1]
    return encode(pieces, starts, work_counts, weight, column_sum, shift)


def solution(mesh):
    placed = (
        P("dp", "fsdp", None),
        P("dp", None),
        P("dp", None),
        P("dp", None),
        P(),
        P(),
        P("fsdp", None),
        P("fsdp"),
    )
    return jax.shard_map(
        shards, mesh=mesh, in_specs=placed, out_specs=P("dp", "fsdp", None), check_vma=False
    )
```

time: 159 us -> 142 us (0.89)
  waiting for transfers between devices: 116 us -> 59.3 us
  starting transfers between devices: 7.38 us -> 57.6 us
  between operations: 13.6 us -> 0.79 us
  Pallas kernels: 0 us -> 11.9 us
  matrix products: 6.25 us -> 0 us
  other arithmetic: 9 us -> 4.32 us
    all_gather x1 -> x0, waiting for transfers between devices: 103 us -> none  [encode(): gathered = lax.all_gather(blocks, 'fsdp', axis=1, tiled=True)]
    ppermute x2 -> x24, starting transfers between devices: 7.35 us -> 57.6 us  [the longest x15 32.5 us: hop(): return lax.ppermute(value, ('dp', 'fsdp'), hops)]
    ppermute x2 -> x24, waiting for transfers between devices: 13.3 us -> 59.3 us  [the longest x15 48.9 us: hop(): return lax.ppermute(value, ('dp', 'fsdp'), hops)]
    pallas_call x0 -> x1, Pallas kernels: none -> 11.9 us  [encode(): pl.pallas_call(encode_kernel, grid_spec=pltpu.PrefetchScalarGridSpec(num_...]
    dot_general x3 -> x0, matrix products: 6.25 us -> none  [the longest x1 3.99 us: encode(): jnp.einsum('bfr,cf->brc', normed, w_qkv, preferred_element_type=jnp.float32)]
    reduce_sum x4, other arithmetic: 5.79 us -> 1.9 us  [the longest x1 0.82 us: picked(): return jnp.sum(jnp.where(matches, values[None, :], 0), axis=1)]
    gather x4 -> x2, local copies, waits for them, and re-layouts: 5.2 us -> 2.49 us  [the longest x1 1.84 us: rebalance(): message = jnp.concatenate([patches[picked(positions)], label_block], axis=0)]
    unnamed x18 -> x34, local copies, waits for them, and re-layouts: 0.04 us -> 1.66 us
  transfers between devices with their start and end apart: 3 -> 24, of which waited for: 2 -> 16; matrix products, arithmetic and copies ran while one was open for 2% -> 2% of each run, Pallas kernels for 0% -> 0%
where the time goes in v2:
time: 142 us; the launch traced here: 141 us
  waiting for transfers between devices  59.3 us (42%)
  starting transfers between devices  57.6 us (41%)
  Pallas kernels  11.9 us (8%)
  local copies, waits for them, and re-layouts  6.75 us (5%)
  other arithmetic  4.32 us (3%)
    ppermute x15, waiting for transfers between devices, hop(): return lax.ppermute(value, ('dp', 'fsdp'), hops)  48.9 us
    ppermute x15, starting transfers between devices, hop(): return lax.ppermute(value, ('dp', 'fsdp'), hops)  32.5 us
    ppermute x8, starting transfers between devices, swap(): return lax.ppermute(value, 'dp', swaps)  19.9 us
    pallas_call x1, Pallas kernels, encode(): pl.pallas_call(encode_kernel, grid_spec=pltpu.PrefetchScalarGridSpec(num_...  11.9 us
    ppermute x1, waiting for transfers between devices, rebalance(): arrived = lax.ppermute(message, 'dp', pairs)  10.3 us
    ppermute x1, starting transfers between devices, rebalance(): arrived = lax.ppermute(message, 'dp', pairs)  5.23 us
  transfers between devices with their start and end apart: 24, of which 16 were waited for; matrix products, arithmetic and copies ran while one was open for 2% of the time, Pallas kernels for 0%

profile of v2, /device:TPU:6, one launch (start us, length us, event | category | flops | bytes accessed | tf_op | source)
XLA Modules:
  0.0 140.6 jit_solution(14125764399661318146)
XLA Ops:
  0.0 0.7 fusion.15
  1.6 0.8 select_reduce_fusion.4
  2.4 1.8 %gather_fusion = bf16[24,80,128]{2,1,0:T(8,128)(2,1)S(1)} fusion(bf16[48,80,128]{2,1,0:T(8,128)(2,1)} %param.8, s32[1024]{0:T(1024)S(1)} %pad_clamp_fusion.1), kind=kCustom, calls=%fused_computation | custom fusion | bytes 983136 | tf_op jit(solution)/shard_map/gather | solution.py:125
  4.4 5.2 %collective-permute-start = (bf16[25,80,128]{2,1,0:T(8,128)(2,1)S(1)}, bf16[25,80,128]{2,1,0:T(8,128)(2,1)S(1)}, u32[]{:S(2)}, u32[]{:S(2)}) collective-permute-start(bf16[25,80,128]{2,1,0:T(8,128)(2,1)S(1)} %pad_maximum_fusion.1), channel_id=1, source_target_pairs={{0,256},{16,272},{32,288},{48,304},{64,320},{80,336},{96,352},{112... | collective-permute-start | bytes 1536008 | tf_op jit(solution)/shard_map/ppermute | solution.py:126
  10.0 0.9 concatenate.40.weight
  11.0 10.3 %collective-permute-done = bf16[25,80,128]{2,1,0:T(8,128)(2,1)S(1)} collective-permute-done((bf16[25,80,128]{2,1,0:T(8,128)(2,1)S(1)}, bf16[25,80,128]{2,1,0:T(8,128)(2,1)S(1)}, u32[]{:S(2)}, u32[]{:S(2)}) %collective-permute-start) | collective-permute-done | bytes 512032 | tf_op jit(solution)/shard_map/ppermute | solution.py:126
  23.0 1.9 %collective-permute-start.2 = (bf16[24,80,128]{2,1,0:T(8,128)(2,1)S(1)}, bf16[24,80,128]{2,1,0:T(8,128)(2,1)S(1)}, u32[]{:S(2)}, u32[]{:S(2)}) collective-permute-start(bf16[24,80,128]{2,1,0:T(8,128)(2,1)S(1)} %gather_fusion.1), channel_id=1, source_target_pairs={{0,16},{16,0},{32,48},{48,32},{64,80},{80,64},{96,112},{112,96},{1... | collective-permute-start | bytes 1474568 | tf_op jit(solution)/shard_map/ppermute | solution.py:149
  24.9 3.8 %collective-permute-start.1 = (bf16[24,80,128]{2,1,0:T(8,128)(2,1)S(1)}, bf16[24,80,128]{2,1,0:T(8,128)(2,1)S(1)}, u32[]{:S(2)}, u32[]{:S(2)}) collective-permute-start(bf16[24,80,128]{2,1,0:T(8,128)(2,1)S(1)} %gather_fusion.1), channel_id=1, source_target_pairs={{0,1},{1,2},{2,3},{3,4},{4,5},{5,6},{6,7},{7,8},{8,9},{9,10},{10,1... | collective-permute-start | bytes 1474568 | tf_op jit(solution)/shard_map/ppermute | solution.py:152
  28.8 3.8 %collective-permute-start.3 = (bf16[24,80,128]{2,1,0:T(8,128)(2,1)S(1)}, bf16[24,80,128]{2,1,0:T(8,128)(2,1)S(1)}, u32[]{:S(2)}, u32[]{:S(2)}) collective-permute-start(bf16[24,80,128]{2,1,0:T(8,128)(2,1)S(1)} %collective-permute-done.2), channel_id=1, source_target_pairs={{0,1},{1,2},{2,3},{3,4},{4,5},{5,6},{6,7},{7,8},{8,9},{9,10},{10,1... | collective-permute-start | bytes 1474568 | tf_op jit(solution)/shard_map/ppermute | solution.py:152
  32.6 10.5 %collective-permute-done.1.refs_1_ = bf16[24,80,128]{2,1,0:T(8,128)(2,1)S(1)} collective-permute-done((bf16[24,80,128]{2,1,0:T(8,128)(2,1)S(1)}, bf16[24,80,128]{2,1,0:T(8,128)(2,1)S(1)}, u32[]{:S(2)}, u32[]{:S(2)}) %collective-permute-start.1) | collective-permute-done | bytes 491552 | tf_op jit(solution)/shard_map/ppermute | solution.py:152
  43.2 1.9 %collective-permute-start.7 = (bf16[24,80,128]{2,1,0:T(8,128)(2,1)S(1)}, bf16[24,80,128]{2,1,0:T(8,128)(2,1)S(1)}, u32[]{:S(2)}, u32[]{:S(2)}) collective-permute-start(bf16[24,80,128]{2,1,0:T(8,128)(2,1)S(1)} %collective-permute-done.1.refs_1_), channel_id=1, source_target_pairs={{0,1},{1,2},{2,3},{3,4},{4,5},{5,6},{6,7},{7,8},{8,9},{9,10},{10,1... | collective-permute-start | bytes 1474568 | tf_op jit(solution)/shard_map/ppermute | solution.py:152
  45.1 3.3 %collective-permute-done.3 = bf16[24,80,128]{2,1,0:T(8,128)(2,1)S(1)} collective-permute-done((bf16[24,80,128]{2,1,0:T(8,128)(2,1)S(1)}, bf16[24,80,128]{2,1,0:T(8,128)(2,1)S(1)}, u32[]{:S(2)}, u32[]{:S(2)}) %collective-permute-start.3) | collective-permute-done | bytes 491552 | tf_op jit(solution)/shard_map/ppermute | solution.py:152
  48.4 1.9 %collective-permute-start.4 = (bf16[24,80,128]{2,1,0:T(8,128)(2,1)S(1)}, bf16[24,80,128]{2,1,0:T(8,128)(2,1)S(1)}, u32[]{:S(2)}, u32[]{:S(2)}) collective-permute-start(bf16[24,80,128]{2,1,0:T(8,128)(2,1)S(1)} %collective-permute-done.3), channel_id=1, source_target_pairs={{0,1},{1,2},{2,3},{3,4},{4,5},{5,6},{6,7},{7,8},{8,9},{9,10},{10,1... | collective-permute-start | bytes 1474568 | tf_op jit(solution)/shard_map/ppermute | solution.py:152
  50.3 4.7 %collective-permute-done.7.refs_3_ = bf16[24,80,128]{2,1,0:T(8,128)(2,1)S(1)} collective-permute-done((bf16[24,80,128]{2,1,0:T(8,128)(2,1)S(1)}, bf16[24,80,128]{2,1,0:T(8,128)(2,1)S(1)}, u32[]{:S(2)}, u32[]{:S(2)}) %collective-permute-start.7) | collective-permute-done | bytes 491552 | tf_op jit(solution)/shard_map/ppermute | solution.py:152
  55.1 1.9 %collective-permute-start.10 = (bf16[24,80,128]{2,1,0:T(8,128)(2,1)S(1)}, bf16[24,80,128]{2,1,0:T(8,128)(2,1)S(1)}, u32[]{:S(2)}, u32[]{:S(2)}) collective-permute-start(bf16[24,80,128]{2,1,0:T(8,128)(2,1)S(1)} %collective-permute-done.7.refs_3_), channel_id=1, source_target_pairs={{0,1},{1,2},{2,3},{3,4},{4,5},{5,6},{6,7},{7,8},{8,9},{9,10},{10,1... | collective-permute-start | bytes 1474568 | tf_op jit(solution)/shard_map/ppermute | solution.py:152
  57.0 3.0 %collective-permute-start.6 = (bf16[24,80,128]{2,1,0:T(8,128)(2,1)S(1)}, bf16[24,80,128]{2,1,0:T(8,128)(2,1)S(1)}, u32[]{:S(2)}, u32[]{:S(2)}) collective-permute-start(bf16[24,80,128]{2,1,0:T(8,128)(2,1)S(1)} %collective-permute-done.3), channel_id=1, source_target_pairs={{0,16},{16,0},{32,48},{48,32},{64,80},{80,64},{96,112},{112,96},{1... | collective-permute-start | bytes 1474568 | tf_op jit(solution)/shard_map/ppermute | solution.py:149
  60.3 1.9 %collective-permute-start.5 = (bf16[24,80,128]{2,1,0:T(8,128)(2,1)S(1)}, bf16[24,80,128]{2,1,0:T(8,128)(2,1)S(1)}, u32[]{:S(2)}, u32[]{:S(2)}) collective-permute-start(bf16[24,80,128]{2,1,0:T(8,128)(2,1)S(1)} %collective-permute-done.4), channel_id=1, source_target_pairs={{0,1},{1,2},{2,3},{3,4},{4,5},{5,6},{6,7},{7,8},{8,9},{9,10},{10,1... | collective-permute-start | bytes 1474568 | tf_op jit(solution)/shard_map/ppermute | solution.py:152
  62.3 3.9 %collective-permute-start.9 = (bf16[24,80,128]{2,1,0:T(8,128)(2,1)S(1)}, bf16[24,80,128]{2,1,0:T(8,128)(2,1)S(1)}, u32[]{:S(2)}, u32[]{:S(2)}) collective-permute-start(bf16[24,80,128]{2,1,0:T(8,128)(2,1)S(1)} %collective-permute-done.4), channel_id=1, source_target_pairs={{0,16},{16,0},{32,48},{48,32},{64,80},{80,64},{96,112},{112,96},{1... | collective-permute-start | bytes 1474568 | tf_op jit(solution)/shard_map/ppermute | solution.py:149
  66.2 0.8 collective-permute-done.10.refs_5_
  67.0 1.9 %collective-permute-start.13 = (bf16[24,80,128]{2,1,0:T(8,128)(2,1)S(1)}, bf16[24,80,128]{2,1,0:T(8,128)(2,1)S(1)}, u32[]{:S(2)}, u32[]{:S(2)}) collective-permute-start(bf16[24,80,128]{2,1,0:T(8,128)(2,1)S(1)} %collective-permute-done.10.refs_5_), channel_id=1, source_target_pairs={{0,1},{1,2},{2,3},{3,4},{4,5},{5,6},{6,7},{7,8},{8,9},{9,10},{10,1... | collective-permute-start | bytes 1474568 | tf_op jit(solution)/shard_map/ppermute | solution.py:152
  68.9 3.3 %collective-permute-done.5 = bf16[24,80,128]{2,1,0:T(8,128)(2,1)S(1)} collective-permute-done((bf16[24,80,128]{2,1,0:T(8,128)(2,1)S(1)}, bf16[24,80,128]{2,1,0:T(8,128)(2,1)S(1)}, u32[]{:S(2)}, u32[]{:S(2)}) %collective-permute-start.5) | collective-permute-done | bytes 491552 | tf_op jit(solution)/shard_map/ppermute | solution.py:152
  72.3 1.9 %collective-permute-start.8 = (bf16[24,80,128]{2,1,0:T(8,128)(2,1)S(1)}, bf16[24,80,128]{2,1,0:T(8,128)(2,1)S(1)}, u32[]{:S(2)}, u32[]{:S(2)}) collective-permute-start(bf16[24,80,128]{2,1,0:T(8,128)(2,1)S(1)} %collective-permute-done.5), channel_id=1, source_target_pairs={{0,1},{1,2},{2,3},{3,4},{4,5},{5,6},{6,7},{7,8},{8,9},{9,10},{10,1... | collective-permute-start | bytes 1474568 | tf_op jit(solution)/shard_map/ppermute | solution.py:152
  74.2 2.8 %collective-permute-start.12 = (bf16[24,80,128]{2,1,0:T(8,128)(2,1)S(1)}, bf16[24,80,128]{2,1,0:T(8,128)(2,1)}, u32[]{:S(2)}, u32[]{:S(2)}) collective-permute-start(bf16[24,80,128]{2,1,0:T(8,128)(2,1)S(1)} %collective-permute-done.5), channel_id=1, source_target_pairs={{0,16},{16,0},{32,48},{48,32},{64,80},{80,64},{96,112},{112,96},{1... | collective-permute-start | bytes 1474568 | tf_op jit(solution)/shard_map/ppermute | solution.py:149
  77.0 1.9 %collective-permute-done.13.refs_7_ = bf16[24,80,128]{2,1,0:T(8,128)(2,1)S(1)} collective-permute-done((bf16[24,80,128]{2,1,0:T(8,128)(2,1)S(1)}, bf16[24,80,128]{2,1,0:T(8,128)(2,1)S(1)}, u32[]{:S(2)}, u32[]{:S(2)}) %collective-permute-start.13) | collective-permute-done | bytes 491552 | tf_op jit(solution)/shard_map/ppermute | solution.py:152
  78.9 1.9 %collective-permute-start.16 = (bf16[24,80,128]{2,1,0:T(8,128)(2,1)S(1)}, bf16[24,80,128]{2,1,0:T(8,128)(2,1)S(1)}, u32[]{:S(2)}, u32[]{:S(2)}) collective-permute-start(bf16[24,80,128]{2,1,0:T(8,128)(2,1)S(1)} %collective-permute-done.13.refs_7_), channel_id=1, source_target_pairs={{0,1},{1,2},{2,3},{3,4},{4,5},{5,6},{6,7},{7,8},{8,9},{9,10},{10,1... | collective-permute-start | bytes 1474568 | tf_op jit(solution)/shard_map/ppermute | solution.py:152
  80.9 3.3 %collective-permute-done.8 = bf16[24,80,128]{2,1,0:T(8,128)(2,1)S(1)} collective-permute-done((bf16[24,80,128]{2,1,0:T(8,128)(2,1)S(1)}, bf16[24,80,128]{2,1,0:T(8,128)(2,1)S(1)}, u32[]{:S(2)}, u32[]{:S(2)}) %collective-permute-start.8) | collective-permute-done | bytes 491552 | tf_op jit(solution)/shard_map/ppermute | solution.py:152
  84.2 1.9 %collective-permute-start.11 = (bf16[24,80,128]{2,1,0:T(8,128)(2,1)S(1)}, bf16[24,80,128]{2,1,0:T(8,128)(2,1)}, u32[]{:S(2)}, u32[]{:S(2)}) collective-permute-start(bf16[24,80,128]{2,1,0:T(8,128)(2,1)S(1)} %collective-permute-done.8), channel_id=1, source_target_pairs={{0,1},{1,2},{2,3},{3,4},{4,5},{5,6},{6,7},{7,8},{8,9},{9,10},{10,1... | collective-permute-start | bytes 1474568 | tf_op jit(solution)/shard_map/ppermute | solution.py:152
  86.1 1.9 %collective-permute-start.15 = (bf16[24,80,128]{2,1,0:T(8,128)(2,1)S(1)}, bf16[24,80,128]{2,1,0:T(8,128)(2,1)}, u32[]{:S(2)}, u32[]{:S(2)}) collective-permute-start(bf16[24,80,128]{2,1,0:T(8,128)(2,1)S(1)} %collective-permute-done.8), channel_id=1, source_target_pairs={{0,16},{16,0},{32,48},{48,32},{64,80},{80,64},{96,112},{112,96},{1... | collective-permute-start | bytes 1474568 | tf_op jit(solution)/shard_map/ppermute | solution.py:149
  88.0 2.8 %collective-permute-done.16.refs_9_ = bf16[24,80,128]{2,1,0:T(8,128)(2,1)S(1)} collective-permute-done((bf16[24,80,128]{2,1,0:T(8,128)(2,1)S(1)}, bf16[24,80,128]{2,1,0:T(8,128)(2,1)S(1)}, u32[]{:S(2)}, u32[]{:S(2)}) %collective-permute-start.16) | collective-permute-done | bytes 491552 | tf_op jit(solution)/shard_map/ppermute | solution.py:152
  90.9 0.8 copy-done.9
  91.7 1.9 %collective-permute-start.19 = (bf16[24,80,128]{2,1,0:T(8,128)(2,1)S(1)}, bf16[24,80,128]{2,1,0:T(8,128)(2,1)S(1)}, u32[]{:S(2)}, u32[]{:S(2)}) collective-permute-start(bf16[24,80,128]{2,1,0:T(8,128)(2,1)S(1)} %collective-permute-done.16.refs_9_), channel_id=1, source_target_pairs={{0,1},{1,2},{2,3},{3,4},{4,5},{5,6},{6,7},{7,8},{8,9},{9,10},{10,1... | collective-permute-start | bytes 1474568 | tf_op jit(solution)/shard_map/ppermute | solution.py:152
  93.6 2.6 %collective-permute-done.11 = bf16[24,80,128]{2,1,0:T(8,128)(2,1)} collective-permute-done((bf16[24,80,128]{2,1,0:T(8,128)(2,1)S(1)}, bf16[24,80,128]{2,1,0:T(8,128)(2,1)}, u32[]{:S(2)}, u32[]{:S(2)}) %collective-permute-start.11) | collective-permute-done | bytes 491552 | tf_op jit(solution)/shard_map/ppermute | solution.py:152
  96.2 1.9 %collective-permute-start.14 = (bf16[24,80,128]{2,1,0:T(8,128)(2,1)}, bf16[24,80,128]{2,1,0:T(8,128)(2,1)}, u32[]{:S(2)}, u32[]{:S(2)}) collective-permute-start(bf16[24,80,128]{2,1,0:T(8,128)(2,1)} %collective-permute-done.11), channel_id=1, source_target_pairs={{0,1},{1,2},{2,3},{3,4},{4,5},{5,6},{6,7},{7,8},{8,9},{9,10},{10,1... | collective-permute-start | bytes 1474568 | tf_op jit(solution)/shard_map/ppermute | solution.py:152
  98.1 5.5 %collective-permute-done.19.refs_11_ = bf16[24,80,128]{2,1,0:T(8,128)(2,1)S(1)} collective-permute-done((bf16[24,80,128]{2,1,0:T(8,128)(2,1)S(1)}, bf16[24,80,128]{2,1,0:T(8,128)(2,1)S(1)}, u32[]{:S(2)}, u32[]{:S(2)}) %collective-permute-start.19) | collective-permute-done | bytes 491552 | tf_op jit(solution)/shard_map/ppermute | solution.py:152
  103.6 0.8 copy-done.10
  104.4 1.9 %collective-permute-start.21 = (bf16[24,80,128]{2,1,0:T(8,128)(2,1)S(1)}, bf16[24,80,128]{2,1,0:T(8,128)(2,1)}, u32[]{:S(2)}, u32[]{:S(2)}) collective-permute-start(bf16[24,80,128]{2,1,0:T(8,128)(2,1)S(1)} %collective-permute-done.19.refs_11_), channel_id=1, source_target_pairs={{0,1},{1,2},{2,3},{3,4},{4,5},{5,6},{6,7},{7,8},{8,9},{9,10},{10,1... | collective-permute-start | bytes 1474568 | tf_op jit(solution)/shard_map/ppermute | solution.py:152
  106.3 2.7 %collective-permute-done.14 = bf16[24,80,128]{2,1,0:T(8,128)(2,1)} collective-permute-done((bf16[24,80,128]{2,1,0:T(8,128)(2,1)}, bf16[24,80,128]{2,1,0:T(8,128)(2,1)}, u32[]{:S(2)}, u32[]{:S(2)}) %collective-permute-start.14) | collective-permute-done | bytes 491552 | tf_op jit(solution)/shard_map/ppermute | solution.py:152
  109.0 1.9 %collective-permute-start.17 = (bf16[24,80,128]{2,1,0:T(8,128)(2,1)}, bf16[24,80,128]{2,1,0:T(8,128)(2,1)}, u32[]{:S(2)}, u32[]{:S(2)}) collective-permute-start(bf16[24,80,128]{2,1,0:T(8,128)(2,1)} %collective-permute-done.14), channel_id=1, source_target_pairs={{0,1},{1,2},{2,3},{3,4},{4,5},{5,6},{6,7},{7,8},{8,9},{9,10},{10,1... | collective-permute-start | bytes 1474568 | tf_op jit(solution)/shard_map/ppermute | solution.py:152
  110.9 1.9 %collective-permute-start.18 = (bf16[24,80,128]{2,1,0:T(8,128)(2,1)}, bf16[24,80,128]{2,1,0:T(8,128)(2,1)}, u32[]{:S(2)}, u32[]{:S(2)}) collective-permute-start(bf16[24,80,128]{2,1,0:T(8,128)(2,1)} %collective-permute-done.11), channel_id=1, source_target_pairs={{0,16},{16,0},{32,48},{48,32},{64,80},{80,64},{96,112},{112,96},{1... | collective-permute-start | bytes 1474568 | tf_op jit(solution)/shard_map/ppermute | solution.py:149
  112.8 2.4 %collective-permute-start.20 = (bf16[24,80,128]{2,1,0:T(8,128)(2,1)}, bf16[24,80,128]{2,1,0:T(8,128)(2,1)}, u32[]{:S(2)}, u32[]{:S(2)}) collective-permute-start(bf16[24,80,128]{2,1,0:T(8,128)(2,1)} %collective-permute-done.14), channel_id=1, source_target_pairs={{0,16},{16,0},{32,48},{48,32},{64,80},{80,64},{96,112},{112,96},{1... | collective-permute-start | bytes 1474568 | tf_op jit(solution)/shard_map/ppermute | solution.py:149
  115.2 1.2 collective-permute-done.21.refs_13_
  116.4 1.9 %collective-permute-start.23 = (bf16[24,80,128]{2,1,0:T(8,128)(2,1)}, bf16[24,80,128]{2,1,0:T(8,128)(2,1)}, u32[]{:S(2)}, u32[]{:S(2)}) collective-permute-start(bf16[24,80,128]{2,1,0:T(8,128)(2,1)} %collective-permute-done.21.refs_13_), channel_id=1, source_target_pairs={{0,1},{1,2},{2,3},{3,4},{4,5},{5,6},{6,7},{7,8},{8,9},{9,10},{10,1... | collective-permute-start | bytes 1474568 | tf_op jit(solution)/shard_map/ppermute | solution.py:152
  118.3 3.3 %collective-permute-done.17 = bf16[24,80,128]{2,1,0:T(8,128)(2,1)} collective-permute-done((bf16[24,80,128]{2,1,0:T(8,128)(2,1)}, bf16[24,80,128]{2,1,0:T(8,128)(2,1)}, u32[]{:S(2)}, u32[]{:S(2)}) %collective-permute-start.17) | collective-permute-done | bytes 491552 | tf_op jit(solution)/shard_map/ppermute | solution.py:152
  121.7 1.9 %collective-permute-start.22 = (bf16[24,80,128]{2,1,0:T(8,128)(2,1)}, bf16[24,80,128]{2,1,0:T(8,128)(2,1)}, u32[]{:S(2)}, u32[]{:S(2)}) collective-permute-start(bf16[24,80,128]{2,1,0:T(8,128)(2,1)} %collective-permute-done.17), channel_id=1, source_target_pairs={{0,16},{16,0},{32,48},{48,32},{64,80},{80,64},{96,112},{112,96},{1... | collective-permute-start | bytes 1474568 | tf_op jit(solution)/shard_map/ppermute | solution.py:149
  124.5 0.8 copy.11.column_sum
  125.3 0.8 copy.12.shift
  126.1 2.6 %collective-permute-done.23.refs_15_ = bf16[24,80,128]{2,1,0:T(8,128)(2,1)} collective-permute-done((bf16[24,80,128]{2,1,0:T(8,128)(2,1)}, bf16[24,80,128]{2,1,0:T(8,128)(2,1)}, u32[]{:S(2)}, u32[]{:S(2)}) %collective-permute-start.23) | collective-permute-done | bytes 491552 | tf_op jit(solution)/shard_map/ppermute | solution.py:152
  128.7 11.9 %shard_map.82 = bf16[24,80,128]{2,1,0:T(8,128)(2,1)} custom-call(s32[16]{0:T(128)} %broadcast_multiply_fusion.starts, s32[24]{0:T(128)} %get-tuple-element.32.counts, bf16[256,1280]{1,0:T(8,128)(2,1)} %concatenate.40.weight, f32[240,1]{1,0:T(8,128)} %copy.11.column_sum, f32[240,1]{1,0:T(8,128)} %copy.12.shift, bf16[24,80,128]{2,1,0:T(8,128)(2,1)} %copy-done.1, ...), custom_call_target="tpu_custom_call" | custom-call | flops 1887436800 | bytes 7864320 | tf_op jit(solution)/shard_map/pallas_call | solution.py:76
  (64 shorter events, 3.9 us)
Async XLA Ops:
  0.0 9.6 %copy-start.2 = (bf16[240,1280]{1,0:T(8,128)(2,1)S(1)}, bf16[240,1280]{1,0:T(8,128)(2,1)}, u32[]{:S(2)}) copy-start(bf16[240,1280]{1,0:T(8,128)(2,1)} %param.14) | copy-start | bytes 1843204
  0.0 9.6 %copy-start.12 = (f32[1280]{0:T(1024)S(1)}, f32[1280]{0:T(1024)}, u32[]{:S(2)}) copy-start(f32[1280]{0:T(1024)} %param.13) | copy-start | bytes 15364
  0.0 9.6 %copy-start.11 = (f32[1280]{0:T(1024)S(1)}, f32[1280]{0:T(1024)}, u32[]{:S(2)}) copy-start(f32[1280]{0:T(1024)} %param.12) | copy-start | bytes 15364
  4.3 6.6 %copy-start.13 = (s32[1,48]{1,0:T(1,128)S(1)}, s32[1,48]{1,0:T(1,128)}, u32[]{:S(2)}) copy-start(s32[1,48]{1,0:T(1,128)} %param.9) | copy-start | bytes 580
  4.3 6.6 %copy-start.14 = (s32[1,48]{1,0:T(1,128)S(1)}, s32[1,48]{1,0:T(1,128)}, u32[]{:S(2)}) copy-start(s32[1,48]{1,0:T(1,128)} %param.10) | copy-start | bytes 580
  4.4 6.6 %copy-start.15 = (bf16[240]{0:T(256)(128)(2,1)S(1)}, bf16[240]{0:T(256)(128)(2,1)}, u32[]{:S(2)}) copy-start(bf16[240]{0:T(256)(128)(2,1)} %param.15) | copy-start | bytes 1444
  4.4 17.0 %copy-start.16 = (s32[1,48]{1,0:T(1,128)S(1)}, s32[1,48]{1,0:T(1,128)}, u32[]{:S(2)}) copy-start(s32[1,48]{1,0:T(1,128)} %param.11) | copy-start | bytes 580
  4.4 16.9 %collective-permute-start = (bf16[25,80,128]{2,1,0:T(8,128)(2,1)S(1)}, bf16[25,80,128]{2,1,0:T(8,128)(2,1)S(1)}, u32[]{:S(2)}, u32[]{:S(2)}) collective-permute-start(bf16[25,80,128]{2,1,0:T(8,128)(2,1)S(1)} %pad_maximum_fusion.1), channel_id=1, source_target_pairs={{0,256},{16,272},{32,288},{48,304},{64,320},{80,336},{96,352},{112... | collective-permute-start | bytes 1536008 | tf_op jit(solution)/shard_map/ppermute | solution.py:126
  10.0 12.2 %copy-start = (bf16[48,80,128]{2,1,0:T(8,128)(2,1)S(1)}, bf16[48,80,128]{2,1,0:T(8,128)(2,1)}, u32[]{:S(2)}) copy-start(bf16[48,80,128]{2,1,0:T(8,128)(2,1)} %param.8) | copy-start | bytes 2949124
  23.0 105.6 %copy-start.1 = (bf16[24,80,128]{2,1,0:T(8,128)(2,1)}, bf16[24,80,128]{2,1,0:T(8,128)(2,1)S(1)}, u32[]{:S(2)}) copy-start(bf16[24,80,128]{2,1,0:T(8,128)(2,1)S(1)} %gather_fusion.1) | copy-start | bytes 1474564
  23.0 5.8 %collective-permute-start.2 = (bf16[24,80,128]{2,1,0:T(8,128)(2,1)S(1)}, bf16[24,80,128]{2,1,0:T(8,128)(2,1)S(1)}, u32[]{:S(2)}, u32[]{:S(2)}) collective-permute-start(bf16[24,80,128]{2,1,0:T(8,128)(2,1)S(1)} %gather_fusion.1), channel_id=1, source_target_pairs={{0,16},{16,0},{32,48},{48,32},{64,80},{80,64},{96,112},{112,96},{1... | collective-permute-start | bytes 1474568 | tf_op jit(solution)/shard_map/ppermute | solution.py:149
  24.9 18.2 %collective-permute-start.1 = (bf16[24,80,128]{2,1,0:T(8,128)(2,1)S(1)}, bf16[24,80,128]{2,1,0:T(8,128)(2,1)S(1)}, u32[]{:S(2)}, u32[]{:S(2)}) collective-permute-start(bf16[24,80,128]{2,1,0:T(8,128)(2,1)S(1)} %gather_fusion.1), channel_id=1, source_target_pairs={{0,1},{1,2},{2,3},{3,4},{4,5},{5,6},{6,7},{7,8},{8,9},{9,10},{10,1... | collective-permute-start | bytes 1474568 | tf_op jit(solution)/shard_map/ppermute | solution.py:152
  28.8 19.6 %collective-permute-start.3 = (bf16[24,80,128]{2,1,0:T(8,128)(2,1)S(1)}, bf16[24,80,128]{2,1,0:T(8,128)(2,1)S(1)}, u32[]{:S(2)}, u32[]{:S(2)}) collective-permute-start(bf16[24,80,128]{2,1,0:T(8,128)(2,1)S(1)} %collective-permute-done.2), channel_id=1, source_target_pairs={{0,1},{1,2},{2,3},{3,4},{4,5},{5,6},{6,7},{7,8},{8,9},{9,10},{10,1... | collective-permute-start | bytes 1474568 | tf_op jit(solution)/shard_map/ppermute | solution.py:152
  43.2 85.5 %copy-start.3 = (bf16[24,80,128]{2,1,0:T(8,128)(2,1)}, bf16[24,80,128]{2,1,0:T(8,128)(2,1)S(1)}, u32[]{:S(2)}) copy-start(bf16[24,80,128]{2,1,0:T(8,128)(2,1)S(1)} %collective-permute-done.1.refs_1_) | copy-start | bytes 1474564
  43.2 11.9 %collective-permute-start.7 = (bf16[24,80,128]{2,1,0:T(8,128)(2,1)S(1)}, bf16[24,80,128]{2,1,0:T(8,128)(2,1)S(1)}, u32[]{:S(2)}, u32[]{:S(2)}) collective-permute-start(bf16[24,80,128]{2,1,0:T(8,128)(2,1)S(1)} %collective-permute-done.1.refs_1_), channel_id=1, source_target_pairs={{0,1},{1,2},{2,3},{3,4},{4,5},{5,6},{6,7},{7,8},{8,9},{9,10},{10,1... | collective-permute-start | bytes 1474568 | tf_op jit(solution)/shard_map/ppermute | solution.py:152
  48.4 11.9 %collective-permute-start.4 = (bf16[24,80,128]{2,1,0:T(8,128)(2,1)S(1)}, bf16[24,80,128]{2,1,0:T(8,128)(2,1)S(1)}, u32[]{:S(2)}, u32[]{:S(2)}) collective-permute-start(bf16[24,80,128]{2,1,0:T(8,128)(2,1)S(1)} %collective-permute-done.3), channel_id=1, source_target_pairs={{0,1},{1,2},{2,3},{3,4},{4,5},{5,6},{6,7},{7,8},{8,9},{9,10},{10,1... | collective-permute-start | bytes 1474568 | tf_op jit(solution)/shard_map/ppermute | solution.py:152
  55.1 73.6 %copy-start.4 = (bf16[24,80,128]{2,1,0:T(8,128)(2,1)}, bf16[24,80,128]{2,1,0:T(8,128)(2,1)S(1)}, u32[]{:S(2)}) copy-start(bf16[24,80,128]{2,1,0:T(8,128)(2,1)S(1)} %collective-permute-done.7.refs_3_) | copy-start | bytes 1474564
  55.1 11.9 %collective-permute-start.10 = (bf16[24,80,128]{2,1,0:T(8,128)(2,1)S(1)}, bf16[24,80,128]{2,1,0:T(8,128)(2,1)S(1)}, u32[]{:S(2)}, u32[]{:S(2)}) collective-permute-start(bf16[24,80,128]{2,1,0:T(8,128)(2,1)S(1)} %collective-permute-done.7.refs_3_), channel_id=1, source_target_pairs={{0,1},{1,2},{2,3},{3,4},{4,5},{5,6},{6,7},{7,8},{8,9},{9,10},{10,1... | collective-permute-start | bytes 1474568 | tf_op jit(solution)/shard_map/ppermute | solution.py:152
  57.0 11.9 %collective-permute-start.6 = (bf16[24,80,128]{2,1,0:T(8,128)(2,1)S(1)}, bf16[24,80,128]{2,1,0:T(8,128)(2,1)S(1)}, u32[]{:S(2)}, u32[]{:S(2)}) collective-permute-start(bf16[24,80,128]{2,1,0:T(8,128)(2,1)S(1)} %collective-permute-done.3), channel_id=1, source_target_pairs={{0,16},{16,0},{32,48},{48,32},{64,80},{80,64},{96,112},{112,96},{1... | collective-permute-start | bytes 1474568 | tf_op jit(solution)/shard_map/ppermute | solution.py:149
  60.3 11.9 %collective-permute-start.5 = (bf16[24,80,128]{2,1,0:T(8,128)(2,1)S(1)}, bf16[24,80,128]{2,1,0:T(8,128)(2,1)S(1)}, u32[]{:S(2)}, u32[]{:S(2)}) collective-permute-start(bf16[24,80,128]{2,1,0:T(8,128)(2,1)S(1)} %collective-permute-done.4), channel_id=1, source_target_pairs={{0,1},{1,2},{2,3},{3,4},{4,5},{5,6},{6,7},{7,8},{8,9},{9,10},{10,1... | collective-permute-start | bytes 1474568 | tf_op jit(solution)/shard_map/ppermute | solution.py:152
  62.3 18.6 %collective-permute-start.9 = (bf16[24,80,128]{2,1,0:T(8,128)(2,1)S(1)}, bf16[24,80,128]{2,1,0:T(8,128)(2,1)S(1)}, u32[]{:S(2)}, u32[]{:S(2)}) collective-permute-start(bf16[24,80,128]{2,1,0:T(8,128)(2,1)S(1)} %collective-permute-done.4), channel_id=1, source_target_pairs={{0,16},{16,0},{32,48},{48,32},{64,80},{80,64},{96,112},{112,96},{1... | collective-permute-start | bytes 1474568 | tf_op jit(solution)/shard_map/ppermute | solution.py:149
  67.0 61.7 %copy-start.5 = (bf16[24,80,128]{2,1,0:T(8,128)(2,1)}, bf16[24,80,128]{2,1,0:T(8,128)(2,1)S(1)}, u32[]{:S(2)}) copy-start(bf16[24,80,128]{2,1,0:T(8,128)(2,1)S(1)} %collective-permute-done.10.refs_5_) | copy-start | bytes 1474564
  67.0 11.9 %collective-permute-start.13 = (bf16[24,80,128]{2,1,0:T(8,128)(2,1)S(1)}, bf16[24,80,128]{2,1,0:T(8,128)(2,1)S(1)}, u32[]{:S(2)}, u32[]{:S(2)}) collective-permute-start(bf16[24,80,128]{2,1,0:T(8,128)(2,1)S(1)} %collective-permute-done.10.refs_5_), channel_id=1, source_target_pairs={{0,1},{1,2},{2,3},{3,4},{4,5},{5,6},{6,7},{7,8},{8,9},{9,10},{10,1... | collective-permute-start | bytes 1474568 | tf_op jit(solution)/shard_map/ppermute | solution.py:152
  68.9 59.7 %copy-start.6 = (bf16[24,80,128]{2,1,0:T(8,128)(2,1)}, bf16[24,80,128]{2,1,0:T(8,128)(2,1)S(1)}, u32[]{:S(2)}) copy-start(bf16[24,80,128]{2,1,0:T(8,128)(2,1)S(1)} %collective-permute-done.6.refs_2_) | copy-start | bytes 1474564
  72.3 11.9 %collective-permute-start.8 = (bf16[24,80,128]{2,1,0:T(8,128)(2,1)S(1)}, bf16[24,80,128]{2,1,0:T(8,128)(2,1)S(1)}, u32[]{:S(2)}, u32[]{:S(2)}) collective-permute-start(bf16[24,80,128]{2,1,0:T(8,128)(2,1)S(1)} %collective-permute-done.5), channel_id=1, source_target_pairs={{0,1},{1,2},{2,3},{3,4},{4,5},{5,6},{6,7},{7,8},{8,9},{9,10},{10,1... | collective-permute-start | bytes 1474568 | tf_op jit(solution)/shard_map/ppermute | solution.py:152
  74.2 19.4 %collective-permute-start.12 = (bf16[24,80,128]{2,1,0:T(8,128)(2,1)S(1)}, bf16[24,80,128]{2,1,0:T(8,128)(2,1)}, u32[]{:S(2)}, u32[]{:S(2)}) collective-permute-start(bf16[24,80,128]{2,1,0:T(8,128)(2,1)S(1)} %collective-permute-done.5), channel_id=1, source_target_pairs={{0,16},{16,0},{32,48},{48,32},{64,80},{80,64},{96,112},{112,96},{1... | collective-permute-start | bytes 1474568 | tf_op jit(solution)/shard_map/ppermute | solution.py:149
  78.9 49.8 %copy-start.8 = (bf16[24,80,128]{2,1,0:T(8,128)(2,1)}, bf16[24,80,128]{2,1,0:T(8,128)(2,1)S(1)}, u32[]{:S(2)}) copy-start(bf16[24,80,128]{2,1,0:T(8,128)(2,1)S(1)} %collective-permute-done.13.refs_7_) | copy-start | bytes 1474564
  78.9 11.9 %collective-permute-start.16 = (bf16[24,80,128]{2,1,0:T(8,128)(2,1)S(1)}, bf16[24,80,128]{2,1,0:T(8,128)(2,1)S(1)}, u32[]{:S(2)}, u32[]{:S(2)}) collective-permute-start(bf16[24,80,128]{2,1,0:T(8,128)(2,1)S(1)} %collective-permute-done.13.refs_7_), channel_id=1, source_target_pairs={{0,1},{1,2},{2,3},{3,4},{4,5},{5,6},{6,7},{7,8},{8,9},{9,10},{10,1... | collective-permute-start | bytes 1474568 | tf_op jit(solution)/shard_map/ppermute | solution.py:152
  80.9 47.8 %copy-start.7 = (bf16[24,80,128]{2,1,0:T(8,128)(2,1)}, bf16[24,80,128]{2,1,0:T(8,128)(2,1)S(1)}, u32[]{:S(2)}) copy-start(bf16[24,80,128]{2,1,0:T(8,128)(2,1)S(1)} %collective-permute-done.9.refs_4_) | copy-start | bytes 1474564
  84.2 12.0 %collective-permute-start.11 = (bf16[24,80,128]{2,1,0:T(8,128)(2,1)S(1)}, bf16[24,80,128]{2,1,0:T(8,128)(2,1)}, u32[]{:S(2)}, u32[]{:S(2)}) collective-permute-start(bf16[24,80,128]{2,1,0:T(8,128)(2,1)S(1)} %collective-permute-done.8), channel_id=1, source_target_pairs={{0,1},{1,2},{2,3},{3,4},{4,5},{5,6},{6,7},{7,8},{8,9},{9,10},{10,1... | collective-permute-start | bytes 1474568 | tf_op jit(solution)/shard_map/ppermute | solution.py:152
  86.1 20.2 %collective-permute-start.15 = (bf16[24,80,128]{2,1,0:T(8,128)(2,1)S(1)}, bf16[24,80,128]{2,1,0:T(8,128)(2,1)}, u32[]{:S(2)}, u32[]{:S(2)}) collective-permute-start(bf16[24,80,128]{2,1,0:T(8,128)(2,1)S(1)} %collective-permute-done.8), channel_id=1, source_target_pairs={{0,16},{16,0},{32,48},{48,32},{64,80},{80,64},{96,112},{112,96},{1... | collective-permute-start | bytes 1474568 | tf_op jit(solution)/shard_map/ppermute | solution.py:149
  90.9 0.8 copy-start.9
  91.7 11.9 %collective-permute-start.19 = (bf16[24,80,128]{2,1,0:T(8,128)(2,1)S(1)}, bf16[24,80,128]{2,1,0:T(8,128)(2,1)S(1)}, u32[]{:S(2)}, u32[]{:S(2)}) collective-permute-start(bf16[24,80,128]{2,1,0:T(8,128)(2,1)S(1)} %collective-permute-done.16.refs_9_), channel_id=1, source_target_pairs={{0,1},{1,2},{2,3},{3,4},{4,5},{5,6},{6,7},{7,8},{8,9},{9,10},{10,1... | collective-permute-start | bytes 1474568 | tf_op jit(solution)/shard_map/ppermute | solution.py:152
  96.2 12.7 %collective-permute-start.14 = (bf16[24,80,128]{2,1,0:T(8,128)(2,1)}, bf16[24,80,128]{2,1,0:T(8,128)(2,1)}, u32[]{:S(2)}, u32[]{:S(2)}) collective-permute-start(bf16[24,80,128]{2,1,0:T(8,128)(2,1)} %collective-permute-done.11), channel_id=1, source_target_pairs={{0,1},{1,2},{2,3},{3,4},{4,5},{5,6},{6,7},{7,8},{8,9},{9,10},{10,1... | collective-permute-start | bytes 1474568 | tf_op jit(solution)/shard_map/ppermute | solution.py:152
  103.6 0.8 copy-start.10
  104.4 12.0 %collective-permute-start.21 = (bf16[24,80,128]{2,1,0:T(8,128)(2,1)S(1)}, bf16[24,80,128]{2,1,0:T(8,128)(2,1)}, u32[]{:S(2)}, u32[]{:S(2)}) collective-permute-start(bf16[24,80,128]{2,1,0:T(8,128)(2,1)S(1)} %collective-permute-done.19.refs_11_), channel_id=1, source_target_pairs={{0,1},{1,2},{2,3},{3,4},{4,5},{5,6},{6,7},{7,8},{8,9},{9,10},{10,1... | collective-permute-start | bytes 1474568 | tf_op jit(solution)/shard_map/ppermute | solution.py:152
  109.0 12.7 %collective-permute-start.17 = (bf16[24,80,128]{2,1,0:T(8,128)(2,1)}, bf16[24,80,128]{2,1,0:T(8,128)(2,1)}, u32[]{:S(2)}, u32[]{:S(2)}) collective-permute-start(bf16[24,80,128]{2,1,0:T(8,128)(2,1)} %collective-permute-done.14), channel_id=1, source_target_pairs={{0,1},{1,2},{2,3},{3,4},{4,5},{5,6},{6,7},{7,8},{8,9},{9,10},{10,1... | collective-permute-start | bytes 1474568 | tf_op jit(solution)/shard_map/ppermute | solution.py:152
  110.9 15.2 %collective-permute-start.18 = (bf16[24,80,128]{2,1,0:T(8,128)(2,1)}, bf16[24,80,128]{2,1,0:T(8,128)(2,1)}, u32[]{:S(2)}, u32[]{:S(2)}) collective-permute-start(bf16[24,80,128]{2,1,0:T(8,128)(2,1)} %collective-permute-done.11), channel_id=1, source_target_pairs={{0,16},{16,0},{32,48},{48,32},{64,80},{80,64},{96,112},{112,96},{1... | collective-permute-start | bytes 1474568 | tf_op jit(solution)/shard_map/ppermute | solution.py:149
  112.8 13.3 %collective-permute-start.20 = (bf16[24,80,128]{2,1,0:T(8,128)(2,1)}, bf16[24,80,128]{2,1,0:T(8,128)(2,1)}, u32[]{:S(2)}, u32[]{:S(2)}) collective-permute-start(bf16[24,80,128]{2,1,0:T(8,128)(2,1)} %collective-permute-done.14), channel_id=1, source_target_pairs={{0,16},{16,0},{32,48},{48,32},{64,80},{80,64},{96,112},{112,96},{1... | collective-permute-start | bytes 1474568 | tf_op jit(solution)/shard_map/ppermute | solution.py:149
  116.4 12.2 %collective-permute-start.23 = (bf16[24,80,128]{2,1,0:T(8,128)(2,1)}, bf16[24,80,128]{2,1,0:T(8,128)(2,1)}, u32[]{:S(2)}, u32[]{:S(2)}) collective-permute-start(bf16[24,80,128]{2,1,0:T(8,128)(2,1)} %collective-permute-done.21.refs_13_), channel_id=1, source_target_pairs={{0,1},{1,2},{2,3},{3,4},{4,5},{5,6},{6,7},{7,8},{8,9},{9,10},{10,1... | collective-permute-start | bytes 1474568 | tf_op jit(solution)/shard_map/ppermute | solution.py:152
  121.7 7.0 %collective-permute-start.22 = (bf16[24,80,128]{2,1,0:T(8,128)(2,1)}, bf16[24,80,128]{2,1,0:T(8,128)(2,1)}, u32[]{:S(2)}, u32[]{:S(2)}) collective-permute-start(bf16[24,80,128]{2,1,0:T(8,128)(2,1)} %collective-permute-done.17), channel_id=1, source_target_pairs={{0,16},{16,0},{32,48},{48,32},{64,80},{80,64},{96,112},{112,96},{1... | collective-permute-start | bytes 1474568 | tf_op jit(solution)/shard_map/ppermute | solution.py:149

commit v3 on v1

v3 whole, which is shorter than its diff:
```python
import math

import jax
import jax.numpy as jnp
from jax import lax
from jax.experimental import pallas as pl
from jax.experimental.pallas import tpu as pltpu
from jax.sharding import PartitionSpec as P

HEAD_DIM = 80
GROUP = 8
SUMS = 16


def encode_kernel(counts, weight, column_sum, shift, *refs):
    pieces, out = refs[:-1], refs[-1]
    blocks_n, feat_share, block_rows = out.shape
    columns_n = column_sum.shape[0]
    feat_total = feat_share * len(pieces)
    key_place = lax.broadcasted_iota(jnp.int32, (block_rows, block_rows), 0)
    row_place = lax.broadcasted_iota(jnp.int32, (feat_share, block_rows), 1)

    def encode_group(first):
        blocks, squares = [], []
        for block in range(GROUP):
            raw = jnp.concatenate([piece[first + block] for piece in pieces], axis=0)
            values = raw.astype(jnp.float32)
            square = jnp.sum((values * values).reshape(feat_total // 8, 8, block_rows), axis=0)
            squares.append(jnp.sum(square, axis=0, keepdims=True))
            blocks.append(raw)
        product = jnp.dot(
            weight[...], jnp.concatenate(blocks, axis=1), preferred_element_type=jnp.float32
        )
        center = product[columns_n : columns_n + 1] / feat_total
        spread = jnp.concatenate(squares, axis=1) / feat_total - center * center
        scale = lax.rsqrt(spread + 1e-06)
        for block in range(GROUP):
            columns = slice(block * block_rows, (block + 1) * block_rows)
            part = (product[:columns_n, columns] - column_sum[...] * center[:, columns]) * scale[:, columns]
            qkv = (part + shift[...]).astype(jnp.bfloat16)
            count = counts[first + block]
            scores = lax.dot_general(
                qkv[HEAD_DIM : 2 * HEAD_DIM],
                qkv[:HEAD_DIM],
                (((0,), (0,)), ((), ())),
                preferred_element_type=jnp.float32,
            ) * (1.0 / math.sqrt(HEAD_DIM))
            raised = jnp.where(key_place < count, jnp.exp(scores), 0.0)
            totals = jnp.sum(raised, axis=0, keepdims=True)
            totals = jnp.where(count > 0, totals, 1.0)
            weights = (raised * (1.0 / totals)).astype(jnp.bfloat16)
            mixed = jnp.dot(qkv[2 * HEAD_DIM :], weights, preferred_element_type=jnp.float32)
            out[first + block] = jnp.where(row_place < count, mixed, 0.0).astype(jnp.bfloat16)

    @pl.loop(0, blocks_n // GROUP)
    def _(index):
        encode_group(index * GROUP)


def folded(ln_gain, ln_bias, w_qkv, b_qkv, origins, block_rows):
    columns_n, feat_total = w_qkv.shape
    wide = w_qkv.astype(jnp.float32)
    scaled = (wide * ln_gain[None, :]).astype(jnp.bfloat16)
    column_sum = jnp.sum(scaled.astype(jnp.float32), axis=1, keepdims=True)
    shift = jnp.sum(wide * ln_bias[None, :], axis=1) + b_qkv.astype(jnp.float32)
    ones = jnp.ones((SUMS, feat_total), jnp.bfloat16)
    weight = jnp.concatenate([scaled, ones], axis=0)
    share = feat_total // len(origins)
    inside = jnp.arange(share, dtype=jnp.int32)
    order = (jnp.stack(origins)[:, None] * share + inside[None, :]).reshape(-1)
    places = jnp.arange(feat_total, dtype=jnp.int32)
    moved = (places[:, None] == order[None, :]).astype(jnp.bfloat16)
    weight = jnp.dot(weight, moved, preferred_element_type=jnp.bfloat16)
    column_sum = jnp.broadcast_to(column_sum, (columns_n, block_rows))
    shift = jnp.broadcast_to(shift[:, None], (columns_n, block_rows))
    return weight, column_sum, shift


def encode(pieces, counts, weight, column_sum, shift):
    blocks_n, feat_share, block_rows = pieces[0].shape
    feat_total = feat_share * len(pieces)
    rows_n = blocks_n * block_rows
    vmem = pl.BlockSpec(memory_space=pltpu.VMEM)
    return pl.pallas_call(
        encode_kernel,
        in_specs=[pl.BlockSpec(memory_space=pltpu.SMEM), vmem, vmem, vmem]
        + [vmem] * len(pieces),
        out_specs=vmem,
        out_shape=jax.ShapeDtypeStruct((blocks_n, feat_share, block_rows), jnp.bfloat16),
        compiler_params=pltpu.CompilerParams(vmem_limit_bytes=24 * 2**20),
        cost_estimate=pl.CostEstimate(
            flops=2 * rows_n * weight.shape[0] * feat_total,
            bytes_accessed=2 * feat_total * rows_n,
            transcendentals=blocks_n * block_rows * block_rows,
        ),
    )(counts, weight, column_sum, shift, *pieces)


def rebalance(patches, counts, dest_ranks, dest_slots, ready):
    rank_total = lax.axis_size("dp")
    home_blocks = patches.shape[0]
    work_blocks = home_blocks // 2
    staying = dest_ranks == lax.axis_index("dp")
    positions = jnp.arange(home_blocks, dtype=jnp.int32)
    work_slots = jnp.arange(work_blocks, dtype=jnp.int32)
    filling = (dest_slots[None, :] == work_slots[:, None]) & (counts[None, :] > 0)

    def picked(which, values):
        return jnp.sum(jnp.where(filling & which[None, :], values[None, :], 0), axis=1)

    leaving_counts = picked(~staying, counts)
    staying_counts = picked(staying, counts)
    label_block = jnp.zeros((1,) + patches.shape[1:], patches.dtype)
    label_block = lax.dynamic_update_slice(
        label_block, leaving_counts.astype(patches.dtype)[None, None], (0, 0, 0)
    )
    message = jnp.concatenate([patches[picked(~staying, positions)], label_block], axis=0)
    pairs = [(source, (source + rank_total // 2) % rank_total) for source in range(rank_total)]
    arrived = lax.ppermute(message, "dp", pairs)
    sources = jnp.where(staying_counts > 0, picked(staying, positions), home_blocks + work_slots)
    arrived, sources, ready = lax.optimization_barrier((arrived, sources, ready))
    arrived_counts = arrived[work_blocks, 0, :work_blocks].astype(jnp.int32)
    pool = jnp.concatenate([patches, arrived], axis=0)
    work_counts = jnp.where(staying_counts > 0, staying_counts, arrived_counts)
    return pool[sources], work_counts, ready


def gather_pieces(own):
    rank_total, ring = lax.axis_size("dp"), lax.axis_size("fsdp")
    swaps = [(rank, rank ^ 1) for rank in range(rank_total)]
    hops = [
        (rank * ring + place, rank * ring + (place + 1 - 2 * (rank % 2)) % ring)
        for rank in range(rank_total)
        for place in range(ring)
    ]

    def swap(value):
        return lax.ppermute(value, "dp", swaps)

    def hop(value):
        return lax.ppermute(value, ("dp", "fsdp"), hops)

    half = ring // 2
    mine, other, swapped = [own, hop(own)], [swap(own)], {}
    for step in range(1, half):
        received = hop(other[-1])
        other.append(received)
        mine[-1], other[-2] = lax.optimization_barrier((mine[-1], other[-2]))
        if step > 2:
            other[-1], swapped[step - 2] = lax.optimization_barrier((received, swapped[step - 2]))
        mine.append(hop(mine[-1]))
        swapped[step] = swap(received)

    pieces = [own]
    for step in range(1, half + 1):
        pieces.append(mine[step])
        if step < half:
            pieces.append(swapped[step])
    return pieces


def shards(patches, patch_count, dest_rank, dest_slot, ln_gain, ln_bias, w_qkv, b_qkv):
    ring = lax.axis_size("fsdp")
    place = lax.axis_index("fsdp")
    sense = 1 - 2 * (lax.axis_index("dp") % 2)
    origins = [place]
    for step in range(1, ring // 2 + 1):
        origins.append((place - sense * step) % ring)
        if step < ring // 2:
            origins.append((place + sense * step) % ring)
    weight, column_sum, shift = folded(
        ln_gain, ln_bias, w_qkv, b_qkv, origins, patches.shape[2]
    )
    own, counts, ready = rebalance(
        patches, patch_count[0], dest_rank[0], dest_slot[0], (weight, column_sum, shift)
    )
    return encode(gather_pieces(own), counts, *ready)


def solution(mesh):
    placed = (
        P("dp", "fsdp", None),
        P("dp", None),
        P("dp", None),
        P("dp", None),
        P(),
        P(),
        P("fsdp", None),
        P("fsdp"),
    )
    return jax.shard_map(
        shards, mesh=mesh, in_specs=placed, out_specs=P("dp", "fsdp", None), check_vma=False
    )
```

time: 159 us -> 132 us (0.83)
  waiting for transfers between devices: 116 us -> 62.1 us
  starting transfers between devices: 7.38 us -> 55.6 us
  between operations: 13.6 us -> 0.72 us
  other arithmetic: 9 us -> 2.22 us
  Pallas kernels: 0 us -> 6.05 us
  matrix products: 6.25 us -> 1.51 us
  local copies, waits for them, and re-layouts: 5.24 us -> 2.86 us
    all_gather x1 -> x0, waiting for transfers between devices: 103 us -> none  [encode(): gathered = lax.all_gather(blocks, 'fsdp', axis=1, tiled=True)]
    ppermute x2 -> x24, waiting for transfers between devices: 13.3 us -> 62.1 us  [the longest x15 52.9 us: hop(): return lax.ppermute(value, ('dp', 'fsdp'), hops)]
    ppermute x2 -> x24, starting transfers between devices: 7.35 us -> 55.6 us  [the longest x15 32.5 us: hop(): return lax.ppermute(value, ('dp', 'fsdp'), hops)]
    pallas_call x0 -> x1, Pallas kernels: none -> 6.05 us  [encode(): pl.pallas_call(encode_kernel, in_specs=[pl.BlockSpec(memory_space=pltpu.S...]
    dot_general x3 -> x1, matrix products: 6.25 us -> 1.51 us  [folded(): weight = jnp.dot(weight, moved, preferred_element_type=jnp.bfloat16)]
    reduce_sum x4 -> x2, other arithmetic: 5.79 us -> 1.19 us  [the longest x1 0.82 us: picked(): jnp.sum(jnp.where(filling & which[None, :], values[None, :], 0), axis=1)]
    gather x4 -> x2, local copies, waits for them, and re-layouts: 5.2 us -> 2.49 us  [the longest x1 1.84 us: rebalance(): patches[picked(~staying, positions)]]
  transfers between devices with their start and end apart: 3 -> 24, of which waited for: 2 -> 16; matrix products, arithmetic and copies ran while one was open for 2% -> 2% of each run, Pallas kernels for 0% -> 0%
where the time goes in v3:
time: 132 us; the launch traced here: 131 us
  waiting for transfers between devices  62.1 us (47%)
  starting transfers between devices  55.6 us (42%)
  Pallas kernels  6.05 us (5%)
  local copies, waits for them, and re-layouts  2.86 us (2%)
  other arithmetic  2.22 us (2%)
  matrix products  1.51 us (1%)
    ppermute x15, waiting for transfers between devices, hop(): return lax.ppermute(value, ('dp', 'fsdp'), hops)  52.9 us
    ppermute x15, starting transfers between devices, hop(): return lax.ppermute(value, ('dp', 'fsdp'), hops)  32.5 us
    ppermute x8, starting transfers between devices, swap(): return lax.ppermute(value, 'dp', swaps)  18 us
    ppermute x1, waiting for transfers between devices, rebalance(): arrived = lax.ppermute(message, 'dp', pairs)  9.2 us
    pallas_call x1, Pallas kernels, encode(): pl.pallas_call(encode_kernel, in_specs=[pl.BlockSpec(memory_space=pltpu.S...  6.05 us
    ppermute x1, starting transfers between devices, rebalance(): arrived = lax.ppermute(message, 'dp', pairs)  5.1 us
  transfers between devices with their start and end apart: 24, of which 16 were waited for; matrix products, arithmetic and copies ran while one was open for 2% of the time, Pallas kernels for 0%

profile of v3, /device:TPU:6, one launch (start us, length us, event | category | flops | bytes accessed | tf_op | source)
XLA Modules:
  0.0 131.0 jit_solution(14476758005230094838)
XLA Ops:
  0.0 0.7 not_bitcast_fusion
  0.8 0.8 select_reduce_fusion
  1.6 1.8 %gather_fusion = bf16[24,80,128]{2,1,0:T(8,128)(2,1)S(1)} fusion(bf16[48,80,128]{2,1,0:T(8,128)(2,1)} %param.8, s32[1024]{0:T(1024)S(1)} %pad_clamp_fusion.1), kind=kCustom, calls=%fused_computation | custom fusion | bytes 983136 | tf_op jit(solution)/shard_map/gather | solution.py:117
  3.5 5.1 %collective-permute-start = (bf16[25,80,128]{2,1,0:T(8,128)(2,1)S(1)}, bf16[25,80,128]{2,1,0:T(8,128)(2,1)S(1)}, u32[]{:S(2)}, u32[]{:S(2)}) collective-permute-start(bf16[25,80,128]{2,1,0:T(8,128)(2,1)S(1)} %fusion.6), channel_id=1, source_target_pairs={{0,256},{16,272},{32,288},{48,304},{64,320},{80,336},{96,352},{112... | collective-permute-start | bytes 1536008 | tf_op jit(solution)/shard_map/ppermute | solution.py:119
  9.1 0.4 convert_reduce_fusion
  9.6 1.5 %fusion.weight = bf16[256,1280]{1,0:T(8,128)(2,1)S(1)} fusion(s32[1280]{0:T(1024)S(1)} %add.141, bf16[240,1280]{1,0:T(8,128)(2,1)S(1)} %get-tuple-element.52), kind=kOutput, calls=%fused_computation.3 | convolution fusion | flops 840499200 | bytes 1274880 | tf_op jit(solution)/shard_map/dot_general | solution.py:73
  11.1 9.2 %collective-permute-done = bf16[25,80,128]{2,1,0:T(8,128)(2,1)S(1)} collective-permute-done((bf16[25,80,128]{2,1,0:T(8,128)(2,1)S(1)}, bf16[25,80,128]{2,1,0:T(8,128)(2,1)S(1)}, u32[]{:S(2)}, u32[]{:S(2)}) %collective-permute-start) | collective-permute-done | bytes 512032 | tf_op jit(solution)/shard_map/ppermute | solution.py:119
  20.5 0.1 pad_maximum_fusion
  20.7 0.6 gather_fusion.1
  21.3 1.9 %collective-permute-start.2 = (bf16[24,80,128]{2,1,0:T(8,128)(2,1)S(1)}, bf16[24,80,128]{2,1,0:T(8,128)(2,1)S(1)}, u32[]{:S(2)}, u32[]{:S(2)}) collective-permute-start(bf16[24,80,128]{2,1,0:T(8,128)(2,1)S(1)} %gather_fusion.1), channel_id=1, source_target_pairs={{0,16},{16,0},{32,48},{48,32},{64,80},{80,64},{96,112},{112,96},{1... | collective-permute-start | bytes 1474568 | tf_op jit(solution)/shard_map/ppermute | solution.py:138
  23.3 3.8 %collective-permute-start.1 = (bf16[24,80,128]{2,1,0:T(8,128)(2,1)S(1)}, bf16[24,80,128]{2,1,0:T(8,128)(2,1)S(1)}, u32[]{:S(2)}, u32[]{:S(2)}) collective-permute-start(bf16[24,80,128]{2,1,0:T(8,128)(2,1)S(1)} %gather_fusion.1), channel_id=1, source_target_pairs={{0,1},{1,2},{2,3},{3,4},{4,5},{5,6},{6,7},{7,8},{8,9},{9,10},{10,1... | collective-permute-start | bytes 1474568 | tf_op jit(solution)/shard_map/ppermute | solution.py:141
  27.1 3.8 %collective-permute-start.3 = (bf16[24,80,128]{2,1,0:T(8,128)(2,1)S(1)}, bf16[24,80,128]{2,1,0:T(8,128)(2,1)S(1)}, u32[]{:S(2)}, u32[]{:S(2)}) collective-permute-start(bf16[24,80,128]{2,1,0:T(8,128)(2,1)S(1)} %collective-permute-done.2), channel_id=1, source_target_pairs={{0,1},{1,2},{2,3},{3,4},{4,5},{5,6},{6,7},{7,8},{8,9},{9,10},{10,1... | collective-permute-start | bytes 1474568 | tf_op jit(solution)/shard_map/ppermute | solution.py:141
  30.9 10.5 %collective-permute-done.1.refs_1_ = bf16[24,80,128]{2,1,0:T(8,128)(2,1)S(1)} collective-permute-done((bf16[24,80,128]{2,1,0:T(8,128)(2,1)S(1)}, bf16[24,80,128]{2,1,0:T(8,128)(2,1)S(1)}, u32[]{:S(2)}, u32[]{:S(2)}) %collective-permute-start.1) | collective-permute-done | bytes 491552 | tf_op jit(solution)/shard_map/ppermute | solution.py:141
  41.5 1.9 %collective-permute-start.7 = (bf16[24,80,128]{2,1,0:T(8,128)(2,1)S(1)}, bf16[24,80,128]{2,1,0:T(8,128)(2,1)S(1)}, u32[]{:S(2)}, u32[]{:S(2)}) collective-permute-start(bf16[24,80,128]{2,1,0:T(8,128)(2,1)S(1)} %collective-permute-done.1.refs_1_), channel_id=1, source_target_pairs={{0,1},{1,2},{2,3},{3,4},{4,5},{5,6},{6,7},{7,8},{8,9},{9,10},{10,1... | collective-permute-start | bytes 1474568 | tf_op jit(solution)/shard_map/ppermute | solution.py:141
  43.4 3.3 %collective-permute-done.3 = bf16[24,80,128]{2,1,0:T(8,128)(2,1)S(1)} collective-permute-done((bf16[24,80,128]{2,1,0:T(8,128)(2,1)S(1)}, bf16[24,80,128]{2,1,0:T(8,128)(2,1)S(1)}, u32[]{:S(2)}, u32[]{:S(2)}) %collective-permute-start.3) | collective-permute-done | bytes 491552 | tf_op jit(solution)/shard_map/ppermute | solution.py:141
  46.7 1.9 %collective-permute-start.4 = (bf16[24,80,128]{2,1,0:T(8,128)(2,1)S(1)}, bf16[24,80,128]{2,1,0:T(8,128)(2,1)S(1)}, u32[]{:S(2)}, u32[]{:S(2)}) collective-permute-start(bf16[24,80,128]{2,1,0:T(8,128)(2,1)S(1)} %collective-permute-done.3), channel_id=1, source_target_pairs={{0,1},{1,2},{2,3},{3,4},{4,5},{5,6},{6,7},{7,8},{8,9},{9,10},{10,1... | collective-permute-start | bytes 1474568 | tf_op jit(solution)/shard_map/ppermute | solution.py:141
  48.7 4.7 %collective-permute-done.7.refs_3_ = bf16[24,80,128]{2,1,0:T(8,128)(2,1)S(1)} collective-permute-done((bf16[24,80,128]{2,1,0:T(8,128)(2,1)S(1)}, bf16[24,80,128]{2,1,0:T(8,128)(2,1)S(1)}, u32[]{:S(2)}, u32[]{:S(2)}) %collective-permute-start.7) | collective-permute-done | bytes 491552 | tf_op jit(solution)/shard_map/ppermute | solution.py:141
  53.4 1.9 %collective-permute-start.10 = (bf16[24,80,128]{2,1,0:T(8,128)(2,1)S(1)}, bf16[24,80,128]{2,1,0:T(8,128)(2,1)S(1)}, u32[]{:S(2)}, u32[]{:S(2)}) collective-permute-start(bf16[24,80,128]{2,1,0:T(8,128)(2,1)S(1)} %collective-permute-done.7.refs_3_), channel_id=1, source_target_pairs={{0,1},{1,2},{2,3},{3,4},{4,5},{5,6},{6,7},{7,8},{8,9},{9,10},{10,1... | collective-permute-start | bytes 1474568 | tf_op jit(solution)/shard_map/ppermute | solution.py:141
  55.3 3.0 %collective-permute-start.6 = (bf16[24,80,128]{2,1,0:T(8,128)(2,1)S(1)}, bf16[24,80,128]{2,1,0:T(8,128)(2,1)S(1)}, u32[]{:S(2)}, u32[]{:S(2)}) collective-permute-start(bf16[24,80,128]{2,1,0:T(8,128)(2,1)S(1)} %collective-permute-done.3), channel_id=1, source_target_pairs={{0,16},{16,0},{32,48},{48,32},{64,80},{80,64},{96,112},{112,96},{1... | collective-permute-start | bytes 1474568 | tf_op jit(solution)/shard_map/ppermute | solution.py:138
  58.4 0.3 collective-permute-done.4
  58.7 1.9 %collective-permute-start.5 = (bf16[24,80,128]{2,1,0:T(8,128)(2,1)S(1)}, bf16[24,80,128]{2,1,0:T(8,128)(2,1)S(1)}, u32[]{:S(2)}, u32[]{:S(2)}) collective-permute-start(bf16[24,80,128]{2,1,0:T(8,128)(2,1)S(1)} %collective-permute-done.4), channel_id=1, source_target_pairs={{0,1},{1,2},{2,3},{3,4},{4,5},{5,6},{6,7},{7,8},{8,9},{9,10},{10,1... | collective-permute-start | bytes 1474568 | tf_op jit(solution)/shard_map/ppermute | solution.py:141
  60.6 4.7 %collective-permute-done.10.refs_5_ = bf16[24,80,128]{2,1,0:T(8,128)(2,1)S(1)} collective-permute-done((bf16[24,80,128]{2,1,0:T(8,128)(2,1)S(1)}, bf16[24,80,128]{2,1,0:T(8,128)(2,1)S(1)}, u32[]{:S(2)}, u32[]{:S(2)}) %collective-permute-start.10) | collective-permute-done | bytes 491552 | tf_op jit(solution)/shard_map/ppermute | solution.py:141
  65.3 1.9 %collective-permute-start.13 = (bf16[24,80,128]{2,1,0:T(8,128)(2,1)S(1)}, bf16[24,80,128]{2,1,0:T(8,128)(2,1)S(1)}, u32[]{:S(2)}, u32[]{:S(2)}) collective-permute-start(bf16[24,80,128]{2,1,0:T(8,128)(2,1)S(1)} %collective-permute-done.10.refs_5_), channel_id=1, source_target_pairs={{0,1},{1,2},{2,3},{3,4},{4,5},{5,6},{6,7},{7,8},{8,9},{9,10},{10,1... | collective-permute-start | bytes 1474568 | tf_op jit(solution)/shard_map/ppermute | solution.py:141
  67.2 1.9 %collective-permute-start.9 = (bf16[24,80,128]{2,1,0:T(8,128)(2,1)S(1)}, bf16[24,80,128]{2,1,0:T(8,128)(2,1)S(1)}, u32[]{:S(2)}, u32[]{:S(2)}) collective-permute-start(bf16[24,80,128]{2,1,0:T(8,128)(2,1)S(1)} %collective-permute-done.4), channel_id=1, source_target_pairs={{0,16},{16,0},{32,48},{48,32},{64,80},{80,64},{96,112},{112,96},{1... | collective-permute-start | bytes 1474568 | tf_op jit(solution)/shard_map/ppermute | solution.py:138
  69.2 1.4 %collective-permute-done.5 = bf16[24,80,128]{2,1,0:T(8,128)(2,1)S(1)} collective-permute-done((bf16[24,80,128]{2,1,0:T(8,128)(2,1)S(1)}, bf16[24,80,128]{2,1,0:T(8,128)(2,1)S(1)}, u32[]{:S(2)}, u32[]{:S(2)}) %collective-permute-start.5) | collective-permute-done | bytes 491552 | tf_op jit(solution)/shard_map/ppermute | solution.py:141
  70.6 1.9 %collective-permute-start.8 = (bf16[24,80,128]{2,1,0:T(8,128)(2,1)S(1)}, bf16[24,80,128]{2,1,0:T(8,128)(2,1)S(1)}, u32[]{:S(2)}, u32[]{:S(2)}) collective-permute-start(bf16[24,80,128]{2,1,0:T(8,128)(2,1)S(1)} %collective-permute-done.5), channel_id=1, source_target_pairs={{0,1},{1,2},{2,3},{3,4},{4,5},{5,6},{6,7},{7,8},{8,9},{9,10},{10,1... | collective-permute-start | bytes 1474568 | tf_op jit(solution)/shard_map/ppermute | solution.py:141
  72.5 4.7 %collective-permute-done.13.refs_7_ = bf16[24,80,128]{2,1,0:T(8,128)(2,1)S(1)} collective-permute-done((bf16[24,80,128]{2,1,0:T(8,128)(2,1)S(1)}, bf16[24,80,128]{2,1,0:T(8,128)(2,1)S(1)}, u32[]{:S(2)}, u32[]{:S(2)}) %collective-permute-start.13) | collective-permute-done | bytes 491552 | tf_op jit(solution)/shard_map/ppermute | solution.py:141
  77.2 1.9 %collective-permute-start.16 = (bf16[24,80,128]{2,1,0:T(8,128)(2,1)S(1)}, bf16[24,80,128]{2,1,0:T(8,128)(2,1)S(1)}, u32[]{:S(2)}, u32[]{:S(2)}) collective-permute-start(bf16[24,80,128]{2,1,0:T(8,128)(2,1)S(1)} %collective-permute-done.13.refs_7_), channel_id=1, source_target_pairs={{0,1},{1,2},{2,3},{3,4},{4,5},{5,6},{6,7},{7,8},{8,9},{9,10},{10,1... | collective-permute-start | bytes 1474568 | tf_op jit(solution)/shard_map/ppermute | solution.py:141
  79.2 1.9 %collective-permute-start.12 = (bf16[24,80,128]{2,1,0:T(8,128)(2,1)S(1)}, bf16[24,80,128]{2,1,0:T(8,128)(2,1)S(1)}, u32[]{:S(2)}, u32[]{:S(2)}) collective-permute-start(bf16[24,80,128]{2,1,0:T(8,128)(2,1)S(1)} %collective-permute-done.5), channel_id=1, source_target_pairs={{0,16},{16,0},{32,48},{48,32},{64,80},{80,64},{96,112},{112,96},{1... | collective-permute-start | bytes 1474568 | tf_op jit(solution)/shard_map/ppermute | solution.py:138
  81.1 1.4 %collective-permute-done.8 = bf16[24,80,128]{2,1,0:T(8,128)(2,1)S(1)} collective-permute-done((bf16[24,80,128]{2,1,0:T(8,128)(2,1)S(1)}, bf16[24,80,128]{2,1,0:T(8,128)(2,1)S(1)}, u32[]{:S(2)}, u32[]{:S(2)}) %collective-permute-start.8) | collective-permute-done | bytes 491552 | tf_op jit(solution)/shard_map/ppermute | solution.py:141
  82.5 1.9 %collective-permute-start.11 = (bf16[24,80,128]{2,1,0:T(8,128)(2,1)S(1)}, bf16[24,80,128]{2,1,0:T(8,128)(2,1)S(1)}, u32[]{:S(2)}, u32[]{:S(2)}) collective-permute-start(bf16[24,80,128]{2,1,0:T(8,128)(2,1)S(1)} %collective-permute-done.8), channel_id=1, source_target_pairs={{0,1},{1,2},{2,3},{3,4},{4,5},{5,6},{6,7},{7,8},{8,9},{9,10},{10,1... | collective-permute-start | bytes 1474568 | tf_op jit(solution)/shard_map/ppermute | solution.py:141
  84.4 4.7 %collective-permute-done.16.refs_9_ = bf16[24,80,128]{2,1,0:T(8,128)(2,1)S(1)} collective-permute-done((bf16[24,80,128]{2,1,0:T(8,128)(2,1)S(1)}, bf16[24,80,128]{2,1,0:T(8,128)(2,1)S(1)}, u32[]{:S(2)}, u32[]{:S(2)}) %collective-permute-start.16) | collective-permute-done | bytes 491552 | tf_op jit(solution)/shard_map/ppermute | solution.py:141
  89.2 1.9 %collective-permute-start.19 = (bf16[24,80,128]{2,1,0:T(8,128)(2,1)S(1)}, bf16[24,80,128]{2,1,0:T(8,128)(2,1)S(1)}, u32[]{:S(2)}, u32[]{:S(2)}) collective-permute-start(bf16[24,80,128]{2,1,0:T(8,128)(2,1)S(1)} %collective-permute-done.16.refs_9_), channel_id=1, source_target_pairs={{0,1},{1,2},{2,3},{3,4},{4,5},{5,6},{6,7},{7,8},{8,9},{9,10},{10,1... | collective-permute-start | bytes 1474568 | tf_op jit(solution)/shard_map/ppermute | solution.py:141
  91.1 1.9 %collective-permute-start.15 = (bf16[24,80,128]{2,1,0:T(8,128)(2,1)S(1)}, bf16[24,80,128]{2,1,0:T(8,128)(2,1)S(1)}, u32[]{:S(2)}, u32[]{:S(2)}) collective-permute-start(bf16[24,80,128]{2,1,0:T(8,128)(2,1)S(1)} %collective-permute-done.8), channel_id=1, source_target_pairs={{0,16},{16,0},{32,48},{48,32},{64,80},{80,64},{96,112},{112,96},{1... | collective-permute-start | bytes 1474568 | tf_op jit(solution)/shard_map/ppermute | solution.py:138
  93.0 1.4 %collective-permute-done.11 = bf16[24,80,128]{2,1,0:T(8,128)(2,1)S(1)} collective-permute-done((bf16[24,80,128]{2,1,0:T(8,128)(2,1)S(1)}, bf16[24,80,128]{2,1,0:T(8,128)(2,1)S(1)}, u32[]{:S(2)}, u32[]{:S(2)}) %collective-permute-start.11) | collective-permute-done | bytes 491552 | tf_op jit(solution)/shard_map/ppermute | solution.py:141
  94.4 1.9 %collective-permute-start.14 = (bf16[24,80,128]{2,1,0:T(8,128)(2,1)S(1)}, bf16[24,80,128]{2,1,0:T(8,128)(2,1)S(1)}, u32[]{:S(2)}, u32[]{:S(2)}) collective-permute-start(bf16[24,80,128]{2,1,0:T(8,128)(2,1)S(1)} %collective-permute-done.11), channel_id=1, source_target_pairs={{0,1},{1,2},{2,3},{3,4},{4,5},{5,6},{6,7},{7,8},{8,9},{9,10},{10,1... | collective-permute-start | bytes 1474568 | tf_op jit(solution)/shard_map/ppermute | solution.py:141
  96.3 4.7 %collective-permute-done.19.refs_11_ = bf16[24,80,128]{2,1,0:T(8,128)(2,1)S(1)} collective-permute-done((bf16[24,80,128]{2,1,0:T(8,128)(2,1)S(1)}, bf16[24,80,128]{2,1,0:T(8,128)(2,1)S(1)}, u32[]{:S(2)}, u32[]{:S(2)}) %collective-permute-start.19) | collective-permute-done | bytes 491552 | tf_op jit(solution)/shard_map/ppermute | solution.py:141
  101.1 1.9 %collective-permute-start.21 = (bf16[24,80,128]{2,1,0:T(8,128)(2,1)S(1)}, bf16[24,80,128]{2,1,0:T(8,128)(2,1)S(1)}, u32[]{:S(2)}, u32[]{:S(2)}) collective-permute-start(bf16[24,80,128]{2,1,0:T(8,128)(2,1)S(1)} %collective-permute-done.19.refs_11_), channel_id=1, source_target_pairs={{0,1},{1,2},{2,3},{3,4},{4,5},{5,6},{6,7},{7,8},{8,9},{9,10},{10,1... | collective-permute-start | bytes 1474568 | tf_op jit(solution)/shard_map/ppermute | solution.py:141
  103.0 3.3 %collective-permute-done.14 = bf16[24,80,128]{2,1,0:T(8,128)(2,1)S(1)} collective-permute-done((bf16[24,80,128]{2,1,0:T(8,128)(2,1)S(1)}, bf16[24,80,128]{2,1,0:T(8,128)(2,1)S(1)}, u32[]{:S(2)}, u32[]{:S(2)}) %collective-permute-start.14) | collective-permute-done | bytes 491552 | tf_op jit(solution)/shard_map/ppermute | solution.py:141
  106.4 1.9 %collective-permute-start.17 = (bf16[24,80,128]{2,1,0:T(8,128)(2,1)S(1)}, bf16[24,80,128]{2,1,0:T(8,128)(2,1)S(1)}, u32[]{:S(2)}, u32[]{:S(2)}) collective-permute-start(bf16[24,80,128]{2,1,0:T(8,128)(2,1)S(1)} %collective-permute-done.14), channel_id=1, source_target_pairs={{0,1},{1,2},{2,3},{3,4},{4,5},{5,6},{6,7},{7,8},{8,9},{9,10},{10,1... | collective-permute-start | bytes 1474568 | tf_op jit(solution)/shard_map/ppermute | solution.py:141
  108.3 2.8 %collective-permute-start.18 = (bf16[24,80,128]{2,1,0:T(8,128)(2,1)S(1)}, bf16[24,80,128]{2,1,0:T(8,128)(2,1)S(1)}, u32[]{:S(2)}, u32[]{:S(2)}) collective-permute-start(bf16[24,80,128]{2,1,0:T(8,128)(2,1)S(1)} %collective-permute-done.11), channel_id=1, source_target_pairs={{0,16},{16,0},{32,48},{48,32},{64,80},{80,64},{96,112},{112,96},{1... | collective-permute-start | bytes 1474568 | tf_op jit(solution)/shard_map/ppermute | solution.py:138
  111.1 1.9 %collective-permute-done.21.refs_13_ = bf16[24,80,128]{2,1,0:T(8,128)(2,1)S(1)} collective-permute-done((bf16[24,80,128]{2,1,0:T(8,128)(2,1)S(1)}, bf16[24,80,128]{2,1,0:T(8,128)(2,1)S(1)}, u32[]{:S(2)}, u32[]{:S(2)}) %collective-permute-start.21) | collective-permute-done | bytes 491552 | tf_op jit(solution)/shard_map/ppermute | solution.py:141
  113.0 1.9 %collective-permute-start.23 = (bf16[24,80,128]{2,1,0:T(8,128)(2,1)S(1)}, bf16[24,80,128]{2,1,0:T(8,128)(2,1)S(1)}, u32[]{:S(2)}, u32[]{:S(2)}) collective-permute-start(bf16[24,80,128]{2,1,0:T(8,128)(2,1)S(1)} %collective-permute-done.21.refs_13_), channel_id=1, source_target_pairs={{0,1},{1,2},{2,3},{3,4},{4,5},{5,6},{6,7},{7,8},{8,9},{9,10},{10,1... | collective-permute-start | bytes 1474568 | tf_op jit(solution)/shard_map/ppermute | solution.py:141
  114.9 2.5 %collective-permute-start.20 = (bf16[24,80,128]{2,1,0:T(8,128)(2,1)S(1)}, bf16[24,80,128]{2,1,0:T(8,128)(2,1)S(1)}, u32[]{:S(2)}, u32[]{:S(2)}) collective-permute-start(bf16[24,80,128]{2,1,0:T(8,128)(2,1)S(1)} %collective-permute-done.14), channel_id=1, source_target_pairs={{0,16},{16,0},{32,48},{48,32},{64,80},{80,64},{96,112},{112,96},{1... | collective-permute-start | bytes 1474568 | tf_op jit(solution)/shard_map/ppermute | solution.py:138
  117.5 0.8 collective-permute-done.17
  118.3 1.9 %collective-permute-start.22 = (bf16[24,80,128]{2,1,0:T(8,128)(2,1)S(1)}, bf16[24,80,128]{2,1,0:T(8,128)(2,1)S(1)}, u32[]{:S(2)}, u32[]{:S(2)}) collective-permute-start(bf16[24,80,128]{2,1,0:T(8,128)(2,1)S(1)} %collective-permute-done.17), channel_id=1, source_target_pairs={{0,16},{16,0},{32,48},{48,32},{64,80},{80,64},{96,112},{112,96},{1... | collective-permute-start | bytes 1474568 | tf_op jit(solution)/shard_map/ppermute | solution.py:138
  120.2 4.7 %collective-permute-done.23.refs_15_ = bf16[24,80,128]{2,1,0:T(8,128)(2,1)S(1)} collective-permute-done((bf16[24,80,128]{2,1,0:T(8,128)(2,1)S(1)}, bf16[24,80,128]{2,1,0:T(8,128)(2,1)S(1)}, u32[]{:S(2)}, u32[]{:S(2)}) %collective-permute-start.23) | collective-permute-done | bytes 491552 | tf_op jit(solution)/shard_map/ppermute | solution.py:141
  124.9 6.1 %shard_map.82 = bf16[24,80,128]{2,1,0:T(8,128)(2,1)} custom-call(s32[24]{0:T(128)S(1)} %compare_select_fusion.2.counts, bf16[256,1280]{1,0:T(8,128)(2,1)S(1)} %fusion.weight, f32[240,128]{1,0:T(8,128)S(1)} %broadcast_in_dim.66.column_sum, f32[240,128]{1,0:T(8,128)S(1)} %broadcast_in_dim.67.shift, bf16[24,80,128]{2,1,0:T(8,128)(2,1)S(1)} %gather_fusion.1, ...), custom_call_target="tpu_custom_call" | custom-call | flops 2013265920 | bytes 7864320 | tf_op jit(solution)/shard_map/pallas_call | solution.py:84
  (33 shorter events, 0.5 us)
Async XLA Ops:
  0.0 9.1 %copy-start.1 = (bf16[240,1280]{1,0:T(8,128)(2,1)S(1)}, bf16[240,1280]{1,0:T(8,128)(2,1)}, u32[]{:S(2)}) copy-start(bf16[240,1280]{1,0:T(8,128)(2,1)} %param.14) | copy-start | bytes 1843204
  0.0 9.1 %copy-start.3 = (f32[1280]{0:T(1024)S(1)}, f32[1280]{0:T(1024)}, u32[]{:S(2)}) copy-start(f32[1280]{0:T(1024)} %param.13) | copy-start | bytes 15364
  0.0 9.1 %copy-start.2 = (f32[1280]{0:T(1024)S(1)}, f32[1280]{0:T(1024)}, u32[]{:S(2)}) copy-start(f32[1280]{0:T(1024)} %param.12) | copy-start | bytes 15364
  3.5 6.1 %copy-start.4 = (bf16[240]{0:T(256)(128)(2,1)S(1)}, bf16[240]{0:T(256)(128)(2,1)}, u32[]{:S(2)}) copy-start(bf16[240]{0:T(256)(128)(2,1)} %param.15) | copy-start | bytes 1444
  3.5 16.8 %collective-permute-start = (bf16[25,80,128]{2,1,0:T(8,128)(2,1)S(1)}, bf16[25,80,128]{2,1,0:T(8,128)(2,1)S(1)}, u32[]{:S(2)}, u32[]{:S(2)}) collective-permute-start(bf16[25,80,128]{2,1,0:T(8,128)(2,1)S(1)} %fusion.6), channel_id=1, source_target_pairs={{0,256},{16,272},{32,288},{48,304},{64,320},{80,336},{96,352},{112... | collective-permute-start | bytes 1536008 | tf_op jit(solution)/shard_map/ppermute | solution.py:119
  9.6 10.9 %copy-start = (bf16[48,80,128]{2,1,0:T(8,128)(2,1)S(1)}, bf16[48,80,128]{2,1,0:T(8,128)(2,1)}, u32[]{:S(2)}) copy-start(bf16[48,80,128]{2,1,0:T(8,128)(2,1)} %param.8) | copy-start | bytes 2949124
  21.3 5.8 %collective-permute-start.2 = (bf16[24,80,128]{2,1,0:T(8,128)(2,1)S(1)}, bf16[24,80,128]{2,1,0:T(8,128)(2,1)S(1)}, u32[]{:S(2)}, u32[]{:S(2)}) collective-permute-start(bf16[24,80,128]{2,1,0:T(8,128)(2,1)S(1)} %gather_fusion.1), channel_id=1, source_target_pairs={{0,16},{16,0},{32,48},{48,32},{64,80},{80,64},{96,112},{112,96},{1... | collective-permute-start | bytes 1474568 | tf_op jit(solution)/shard_map/ppermute | solution.py:138
  23.3 18.2 %collective-permute-start.1 = (bf16[24,80,128]{2,1,0:T(8,128)(2,1)S(1)}, bf16[24,80,128]{2,1,0:T(8,128)(2,1)S(1)}, u32[]{:S(2)}, u32[]{:S(2)}) collective-permute-start(bf16[24,80,128]{2,1,0:T(8,128)(2,1)S(1)} %gather_fusion.1), channel_id=1, source_target_pairs={{0,1},{1,2},{2,3},{3,4},{4,5},{5,6},{6,7},{7,8},{8,9},{9,10},{10,1... | collective-permute-start | bytes 1474568 | tf_op jit(solution)/shard_map/ppermute | solution.py:141
  27.1 19.6 %collective-permute-start.3 = (bf16[24,80,128]{2,1,0:T(8,128)(2,1)S(1)}, bf16[24,80,128]{2,1,0:T(8,128)(2,1)S(1)}, u32[]{:S(2)}, u32[]{:S(2)}) collective-permute-start(bf16[24,80,128]{2,1,0:T(8,128)(2,1)S(1)} %collective-permute-done.2), channel_id=1, source_target_pairs={{0,1},{1,2},{2,3},{3,4},{4,5},{5,6},{6,7},{7,8},{8,9},{9,10},{10,1... | collective-permute-start | bytes 1474568 | tf_op jit(solution)/shard_map/ppermute | solution.py:141
  41.5 11.9 %collective-permute-start.7 = (bf16[24,80,128]{2,1,0:T(8,128)(2,1)S(1)}, bf16[24,80,128]{2,1,0:T(8,128)(2,1)S(1)}, u32[]{:S(2)}, u32[]{:S(2)}) collective-permute-start(bf16[24,80,128]{2,1,0:T(8,128)(2,1)S(1)} %collective-permute-done.1.refs_1_), channel_id=1, source_target_pairs={{0,1},{1,2},{2,3},{3,4},{4,5},{5,6},{6,7},{7,8},{8,9},{9,10},{10,1... | collective-permute-start | bytes 1474568 | tf_op jit(solution)/shard_map/ppermute | solution.py:141
  46.7 11.9 %collective-permute-start.4 = (bf16[24,80,128]{2,1,0:T(8,128)(2,1)S(1)}, bf16[24,80,128]{2,1,0:T(8,128)(2,1)S(1)}, u32[]{:S(2)}, u32[]{:S(2)}) collective-permute-start(bf16[24,80,128]{2,1,0:T(8,128)(2,1)S(1)} %collective-permute-done.3), channel_id=1, source_target_pairs={{0,1},{1,2},{2,3},{3,4},{4,5},{5,6},{6,7},{7,8},{8,9},{9,10},{10,1... | collective-permute-start | bytes 1474568 | tf_op jit(solution)/shard_map/ppermute | solution.py:141
  53.4 11.9 %collective-permute-start.10 = (bf16[24,80,128]{2,1,0:T(8,128)(2,1)S(1)}, bf16[24,80,128]{2,1,0:T(8,128)(2,1)S(1)}, u32[]{:S(2)}, u32[]{:S(2)}) collective-permute-start(bf16[24,80,128]{2,1,0:T(8,128)(2,1)S(1)} %collective-permute-done.7.refs_3_), channel_id=1, source_target_pairs={{0,1},{1,2},{2,3},{3,4},{4,5},{5,6},{6,7},{7,8},{8,9},{9,10},{10,1... | collective-permute-start | bytes 1474568 | tf_op jit(solution)/shard_map/ppermute | solution.py:141
  55.3 13.9 %collective-permute-start.6 = (bf16[24,80,128]{2,1,0:T(8,128)(2,1)S(1)}, bf16[24,80,128]{2,1,0:T(8,128)(2,1)S(1)}, u32[]{:S(2)}, u32[]{:S(2)}) collective-permute-start(bf16[24,80,128]{2,1,0:T(8,128)(2,1)S(1)} %collective-permute-done.3), channel_id=1, source_target_pairs={{0,16},{16,0},{32,48},{48,32},{64,80},{80,64},{96,112},{112,96},{1... | collective-permute-start | bytes 1474568 | tf_op jit(solution)/shard_map/ppermute | solution.py:138
  58.7 11.9 %collective-permute-start.5 = (bf16[24,80,128]{2,1,0:T(8,128)(2,1)S(1)}, bf16[24,80,128]{2,1,0:T(8,128)(2,1)S(1)}, u32[]{:S(2)}, u32[]{:S(2)}) collective-permute-start(bf16[24,80,128]{2,1,0:T(8,128)(2,1)S(1)} %collective-permute-done.4), channel_id=1, source_target_pairs={{0,1},{1,2},{2,3},{3,4},{4,5},{5,6},{6,7},{7,8},{8,9},{9,10},{10,1... | collective-permute-start | bytes 1474568 | tf_op jit(solution)/shard_map/ppermute | solution.py:141
  65.3 11.9 %collective-permute-start.13 = (bf16[24,80,128]{2,1,0:T(8,128)(2,1)S(1)}, bf16[24,80,128]{2,1,0:T(8,128)(2,1)S(1)}, u32[]{:S(2)}, u32[]{:S(2)}) collective-permute-start(bf16[24,80,128]{2,1,0:T(8,128)(2,1)S(1)} %collective-permute-done.10.refs_5_), channel_id=1, source_target_pairs={{0,1},{1,2},{2,3},{3,4},{4,5},{5,6},{6,7},{7,8},{8,9},{9,10},{10,1... | collective-permute-start | bytes 1474568 | tf_op jit(solution)/shard_map/ppermute | solution.py:141
  67.2 13.9 %collective-permute-start.9 = (bf16[24,80,128]{2,1,0:T(8,128)(2,1)S(1)}, bf16[24,80,128]{2,1,0:T(8,128)(2,1)S(1)}, u32[]{:S(2)}, u32[]{:S(2)}) collective-permute-start(bf16[24,80,128]{2,1,0:T(8,128)(2,1)S(1)} %collective-permute-done.4), channel_id=1, source_target_pairs={{0,16},{16,0},{32,48},{48,32},{64,80},{80,64},{96,112},{112,96},{1... | collective-permute-start | bytes 1474568 | tf_op jit(solution)/shard_map/ppermute | solution.py:138
  70.6 11.9 %collective-permute-start.8 = (bf16[24,80,128]{2,1,0:T(8,128)(2,1)S(1)}, bf16[24,80,128]{2,1,0:T(8,128)(2,1)S(1)}, u32[]{:S(2)}, u32[]{:S(2)}) collective-permute-start(bf16[24,80,128]{2,1,0:T(8,128)(2,1)S(1)} %collective-permute-done.5), channel_id=1, source_target_pairs={{0,1},{1,2},{2,3},{3,4},{4,5},{5,6},{6,7},{7,8},{8,9},{9,10},{10,1... | collective-permute-start | bytes 1474568 | tf_op jit(solution)/shard_map/ppermute | solution.py:141
  77.2 11.9 %collective-permute-start.16 = (bf16[24,80,128]{2,1,0:T(8,128)(2,1)S(1)}, bf16[24,80,128]{2,1,0:T(8,128)(2,1)S(1)}, u32[]{:S(2)}, u32[]{:S(2)}) collective-permute-start(bf16[24,80,128]{2,1,0:T(8,128)(2,1)S(1)} %collective-permute-done.13.refs_7_), channel_id=1, source_target_pairs={{0,1},{1,2},{2,3},{3,4},{4,5},{5,6},{6,7},{7,8},{8,9},{9,10},{10,1... | collective-permute-start | bytes 1474568 | tf_op jit(solution)/shard_map/ppermute | solution.py:141
  79.2 13.9 %collective-permute-start.12 = (bf16[24,80,128]{2,1,0:T(8,128)(2,1)S(1)}, bf16[24,80,128]{2,1,0:T(8,128)(2,1)S(1)}, u32[]{:S(2)}, u32[]{:S(2)}) collective-permute-start(bf16[24,80,128]{2,1,0:T(8,128)(2,1)S(1)} %collective-permute-done.5), channel_id=1, source_target_pairs={{0,16},{16,0},{32,48},{48,32},{64,80},{80,64},{96,112},{112,96},{1... | collective-permute-start | bytes 1474568 | tf_op jit(solution)/shard_map/ppermute | solution.py:138
  82.5 11.9 %collective-permute-start.11 = (bf16[24,80,128]{2,1,0:T(8,128)(2,1)S(1)}, bf16[24,80,128]{2,1,0:T(8,128)(2,1)S(1)}, u32[]{:S(2)}, u32[]{:S(2)}) collective-permute-start(bf16[24,80,128]{2,1,0:T(8,128)(2,1)S(1)} %collective-permute-done.8), channel_id=1, source_target_pairs={{0,1},{1,2},{2,3},{3,4},{4,5},{5,6},{6,7},{7,8},{8,9},{9,10},{10,1... | collective-permute-start | bytes 1474568 | tf_op jit(solution)/shard_map/ppermute | solution.py:141
  89.2 11.9 %collective-permute-start.19 = (bf16[24,80,128]{2,1,0:T(8,128)(2,1)S(1)}, bf16[24,80,128]{2,1,0:T(8,128)(2,1)S(1)}, u32[]{:S(2)}, u32[]{:S(2)}) collective-permute-start(bf16[24,80,128]{2,1,0:T(8,128)(2,1)S(1)} %collective-permute-done.16.refs_9_), channel_id=1, source_target_pairs={{0,1},{1,2},{2,3},{3,4},{4,5},{5,6},{6,7},{7,8},{8,9},{9,10},{10,1... | collective-permute-start | bytes 1474568 | tf_op jit(solution)/shard_map/ppermute | solution.py:141
  91.1 11.9 %collective-permute-start.15 = (bf16[24,80,128]{2,1,0:T(8,128)(2,1)S(1)}, bf16[24,80,128]{2,1,0:T(8,128)(2,1)S(1)}, u32[]{:S(2)}, u32[]{:S(2)}) collective-permute-start(bf16[24,80,128]{2,1,0:T(8,128)(2,1)S(1)} %collective-permute-done.8), channel_id=1, source_target_pairs={{0,16},{16,0},{32,48},{48,32},{64,80},{80,64},{96,112},{112,96},{1... | collective-permute-start | bytes 1474568 | tf_op jit(solution)/shard_map/ppermute | solution.py:138
  94.4 11.9 %collective-permute-start.14 = (bf16[24,80,128]{2,1,0:T(8,128)(2,1)S(1)}, bf16[24,80,128]{2,1,0:T(8,128)(2,1)S(1)}, u32[]{:S(2)}, u32[]{:S(2)}) collective-permute-start(bf16[24,80,128]{2,1,0:T(8,128)(2,1)S(1)} %collective-permute-done.11), channel_id=1, source_target_pairs={{0,1},{1,2},{2,3},{3,4},{4,5},{5,6},{6,7},{7,8},{8,9},{9,10},{10,1... | collective-permute-start | bytes 1474568 | tf_op jit(solution)/shard_map/ppermute | solution.py:141
  101.1 11.9 %collective-permute-start.21 = (bf16[24,80,128]{2,1,0:T(8,128)(2,1)S(1)}, bf16[24,80,128]{2,1,0:T(8,128)(2,1)S(1)}, u32[]{:S(2)}, u32[]{:S(2)}) collective-permute-start(bf16[24,80,128]{2,1,0:T(8,128)(2,1)S(1)} %collective-permute-done.19.refs_11_), channel_id=1, source_target_pairs={{0,1},{1,2},{2,3},{3,4},{4,5},{5,6},{6,7},{7,8},{8,9},{9,10},{10,1... | collective-permute-start | bytes 1474568 | tf_op jit(solution)/shard_map/ppermute | solution.py:141
  106.4 11.9 %collective-permute-start.17 = (bf16[24,80,128]{2,1,0:T(8,128)(2,1)S(1)}, bf16[24,80,128]{2,1,0:T(8,128)(2,1)S(1)}, u32[]{:S(2)}, u32[]{:S(2)}) collective-permute-start(bf16[24,80,128]{2,1,0:T(8,128)(2,1)S(1)} %collective-permute-done.14), channel_id=1, source_target_pairs={{0,1},{1,2},{2,3},{3,4},{4,5},{5,6},{6,7},{7,8},{8,9},{9,10},{10,1... | collective-permute-start | bytes 1474568 | tf_op jit(solution)/shard_map/ppermute | solution.py:141
  108.3 11.9 %collective-permute-start.18 = (bf16[24,80,128]{2,1,0:T(8,128)(2,1)S(1)}, bf16[24,80,128]{2,1,0:T(8,128)(2,1)S(1)}, u32[]{:S(2)}, u32[]{:S(2)}) collective-permute-start(bf16[24,80,128]{2,1,0:T(8,128)(2,1)S(1)} %collective-permute-done.11), channel_id=1, source_target_pairs={{0,16},{16,0},{32,48},{48,32},{64,80},{80,64},{96,112},{112,96},{1... | collective-permute-start | bytes 1474568 | tf_op jit(solution)/shard_map/ppermute | solution.py:138
  113.0 11.9 %collective-permute-start.23 = (bf16[24,80,128]{2,1,0:T(8,128)(2,1)S(1)}, bf16[24,80,128]{2,1,0:T(8,128)(2,1)S(1)}, u32[]{:S(2)}, u32[]{:S(2)}) collective-permute-start(bf16[24,80,128]{2,1,0:T(8,128)(2,1)S(1)} %collective-permute-done.21.refs_13_), channel_id=1, source_target_pairs={{0,1},{1,2},{2,3},{3,4},{4,5},{5,6},{6,7},{7,8},{8,9},{9,10},{10,1... | collective-permute-start | bytes 1474568 | tf_op jit(solution)/shard_map/ppermute | solution.py:141
  114.9 5.3 %collective-permute-start.20 = (bf16[24,80,128]{2,1,0:T(8,128)(2,1)S(1)}, bf16[24,80,128]{2,1,0:T(8,128)(2,1)S(1)}, u32[]{:S(2)}, u32[]{:S(2)}) collective-permute-start(bf16[24,80,128]{2,1,0:T(8,128)(2,1)S(1)} %collective-permute-done.14), channel_id=1, source_target_pairs={{0,16},{16,0},{32,48},{48,32},{64,80},{80,64},{96,112},{112,96},{1... | collective-permute-start | bytes 1474568 | tf_op jit(solution)/shard_map/ppermute | solution.py:138
  118.3 6.7 %collective-permute-start.22 = (bf16[24,80,128]{2,1,0:T(8,128)(2,1)S(1)}, bf16[24,80,128]{2,1,0:T(8,128)(2,1)S(1)}, u32[]{:S(2)}, u32[]{:S(2)}) collective-permute-start(bf16[24,80,128]{2,1,0:T(8,128)(2,1)S(1)} %collective-permute-done.17), channel_id=1, source_target_pairs={{0,16},{16,0},{32,48},{48,32},{64,80},{80,64},{96,112},{112,96},{1... | collective-permute-start | bytes 1474568 | tf_op jit(solution)/shard_map/ppermute | solution.py:138

commit v4 on v3

--- a/solution.py
+++ b/solution.py
@@ -1,3 +1,4 @@
+import functools
 import math
 
 import jax
@@ -8,31 +9,50 @@
 from jax.sharding import PartitionSpec as P
 
 HEAD_DIM = 80
-GROUP = 8
+GROUP = 12
 SUMS = 16
 
 
-def encode_kernel(counts, weight, column_sum, shift, *refs):
+def project_group(weight, pieces, first):
+    _, feat_share, block_rows = pieces[0].shape
+    feat_total = feat_share * len(pieces)
+    blocks, squares = [], []
+    for block in range(GROUP):
+        raw = jnp.concatenate([piece[first + block] for piece in pieces], axis=0)
+        values = raw.astype(jnp.float32)
+        squares.append(jnp.sum((values * values).reshape(feat_total // 8, 8, block_rows), axis=0))
+        blocks.append(raw)
+    product = jnp.dot(
+        weight[...], jnp.concatenate(blocks, axis=1), preferred_element_type=jnp.float32
+    )
+    return product[:-8], jnp.concatenate(squares, axis=1)
+
+
+def project_kernel(weight, *refs):
+    pieces, out = refs[:-1], refs[-1]
+
+    @pl.loop(0, out.shape[0])
+    def _(index):
+        product, squares = project_group(weight, pieces, index * GROUP)
+        out[index, :-8] = product
+        out[index, -8:] = squares
+
+
+def attend_kernel(feat_total, counts, weight, column_sum, shift, before, *refs):
     pieces, out = refs[:-1], refs[-1]
     blocks_n, feat_share, block_rows = out.shape
     columns_n = column_sum.shape[0]
-    feat_total = feat_share * len(pieces)
     key_place = lax.broadcasted_iota(jnp.int32, (block_rows, block_rows), 0)
     row_place = lax.broadcasted_iota(jnp.int32, (feat_share, block_rows), 1)
 
-    def encode_group(first):
-        blocks, squares = [], []
-        for block in range(GROUP):
-            raw = jnp.concatenate([piece[first + block] for piece in pieces], axis=0)
-            values = raw.astype(jnp.float32)
-            square = jnp.sum((values * values).reshape(feat_total // 8, 8, block_rows), axis=0)
-            squares.append(jnp.sum(square, axis=0, keepdims=True))
-            blocks.append(raw)
-        product = jnp.dot(
-            weight[...], jnp.concatenate(blocks, axis=1), preferred_element_type=jnp.float32
-        )
+    @pl.loop(0, blocks_n // GROUP)
+    def _(index):
+        first = index * GROUP
+        product, squares = project_group(weight, pieces, first)
+        product = product + before[index, :-8]
+        squares = jnp.sum(squares + before[index, -8:], axis=0, keepdims=True)
         center = product[columns_n : columns_n + 1] / feat_total
-        spread = jnp.concatenate(squares, axis=1) / feat_total - center * center
+        spread = squares / feat_total - center * center
         scale = lax.rsqrt(spread + 1e-06)
         for block in range(GROUP):
             columns = slice(block * block_rows, (block + 1) * block_rows)
@@ -52,10 +72,6 @@
             mixed = jnp.dot(qkv[2 * HEAD_DIM :], weights, preferred_element_type=jnp.float32)
             out[first + block] = jnp.where(row_place < count, mixed, 0.0).astype(jnp.bfloat16)
 
-    @pl.loop(0, blocks_n // GROUP)
-    def _(index):
-        encode_group(index * GROUP)
-
 
 def folded(ln_gain, ln_bias, w_qkv, b_qkv, origins, block_rows):
     columns_n, feat_total = w_qkv.shape
@@ -76,24 +92,40 @@
     return weight, column_sum, shift
 
 
-def encode(pieces, counts, weight, column_sum, shift):
-    blocks_n, feat_share, block_rows = pieces[0].shape
-    feat_total = feat_share * len(pieces)
+def encode(early, late, counts, weight, column_sum, shift):
+    blocks_n, feat_share, block_rows = late[0].shape
+    feat_total = weight.shape[1]
+    cut = feat_share * len(early)
     rows_n = blocks_n * block_rows
     vmem = pl.BlockSpec(memory_space=pltpu.VMEM)
+    params = pltpu.CompilerParams(vmem_limit_bytes=24 * 2**20)
+    wide = jax.ShapeDtypeStruct(
+        (blocks_n // GROUP, weight.shape[0], GROUP * block_rows), jnp.float32
+    )
+    before = pl.pallas_call(
+        project_kernel,
+        in_specs=[vmem] * (1 + len(early)),
+        out_specs=vmem,
+        out_shape=wide,
+        compiler_params=params,
+        cost_estimate=pl.CostEstimate(
+            flops=2 * rows_n * weight.shape[0] * cut,
+            bytes_accessed=rows_n * (2 * cut + 4 * weight.shape[0]),
+            transcendentals=0,
+        ),
+    )(weight[:, :cut], *early)
     return pl.pallas_call(
-        encode_kernel,
-        in_specs=[pl.BlockSpec(memory_space=pltpu.SMEM), vmem, vmem, vmem]
-        + [vmem] * len(pieces),
+        functools.partial(attend_kernel, feat_total),
+        in_specs=[pl.BlockSpec(memory_space=pltpu.SMEM)] + [vmem] * (4 + len(late)),
         out_specs=vmem,
         out_shape=jax.ShapeDtypeStruct((blocks_n, feat_share, block_rows), jnp.bfloat16),
-        compiler_params=pltpu.CompilerParams(vmem_limit_bytes=24 * 2**20),
+        compiler_params=params,
         cost_estimate=pl.CostEstimate(
-            flops=2 * rows_n * weight.shape[0] * feat_total,
-            bytes_accessed=2 * feat_total * rows_n,
-            transcendentals=blocks_n * block_rows * block_rows,
+            flops=2 * rows_n * weight.shape[0] * (feat_total - cut),
+            bytes_accessed=rows_n * 4 * weight.shape[0],
+            transcendentals=rows_n * block_rows,
         ),
-    )(counts, weight, column_sum, shift, *pieces)
+    )(counts, weight[:, cut:], column_sum, shift, before, *late)
 
 
 def rebalance(patches, counts, dest_ranks, dest_slots, ready):
@@ -125,11 +157,17 @@
     return pool[sources], work_counts, ready
 
 
+def sense_of(rank):
+    return 1 - 2 * (rank % 2)
+
+
 def gather_pieces(own):
     rank_total, ring = lax.axis_size("dp"), lax.axis_size("fsdp")
+    half = ring // 2
+
     swaps = [(rank, rank ^ 1) for rank in range(rank_total)]
     hops = [
-        (rank * ring + place, rank * ring + (place + 1 - 2 * (rank % 2)) % ring)
+        (rank * ring + place, rank * ring + (place + sense_of(rank)) % ring)
         for rank in range(rank_total)
         for place in range(ring)
     ]
@@ -140,7 +178,6 @@
     def hop(value):
         return lax.ppermute(value, ("dp", "fsdp"), hops)
 
-    half = ring // 2
     mine, other, swapped = [own, hop(own)], [swap(own)], {}
     for step in range(1, half):
         received = hop(other[-1])
@@ -148,33 +185,29 @@
         mine[-1], other[-2] = lax.optimization_barrier((mine[-1], other[-2]))
         if step > 2:
             other[-1], swapped[step - 2] = lax.optimization_barrier((received, swapped[step - 2]))
+        if step == half - 2:
+            other[-1], swapped[step - 1] = lax.optimization_barrier((other[-1], swapped[step - 1]))
         mine.append(hop(mine[-1]))
         swapped[step] = swap(received)
-
-    pieces = [own]
-    for step in range(1, half + 1):
-        pieces.append(mine[step])
-        if step < half:
-            pieces.append(swapped[step])
-    return pieces
+    early = mine[:half] + [swapped[step] for step in range(1, half - 1)]
+    return early, [mine[half], swapped[half - 1]]
 
 
 def shards(patches, patch_count, dest_rank, dest_slot, ln_gain, ln_bias, w_qkv, b_qkv):
     ring = lax.axis_size("fsdp")
+    half = ring // 2
     place = lax.axis_index("fsdp")
-    sense = 1 - 2 * (lax.axis_index("dp") % 2)
-    origins = [place]
-    for step in range(1, ring // 2 + 1):
-        origins.append((place - sense * step) % ring)
-        if step < ring // 2:
-            origins.append((place + sense * step) % ring)
+    sense = sense_of(lax.axis_index("dp"))
+    origins = [(place - sense * step) % ring for step in range(half)]
+    origins += [(place + sense * step) % ring for step in range(1, half - 1)]
+    origins += [(place - sense * half) % ring, (place + sense * (half - 1)) % ring]
     weight, column_sum, shift = folded(
         ln_gain, ln_bias, w_qkv, b_qkv, origins, patches.shape[2]
     )
     own, counts, ready = rebalance(
         patches, patch_count[0], dest_rank[0], dest_slot[0], (weight, column_sum, shift)
     )
-    return encode(gather_pieces(own), counts, *ready)
+    return encode(*gather_pieces(own), counts, *ready)
 
 
 def solution(mesh):

time: 132 us -> 130 us (0.985)
  waiting for transfers between devices: 62.1 us -> 58.1 us
  starting transfers between devices: 55.6 us -> 57 us
    ppermute x15, waiting for transfers between devices: 52.9 us -> 48.9 us  [hop(): return lax.ppermute(value, ('dp', 'fsdp'), hops)]
    ppermute x8, starting transfers between devices: 18 us -> 19.4 us  [swap(): return lax.ppermute(value, 'dp', swaps)]
    pallas_call x1 -> x2, Pallas kernels: 6.05 us -> 6.83 us  [the longest x1 4.44 us: encode(): pl.pallas_call(functools.partial(attend_kernel, feat_total), in_specs=[pl...]
  transfers between devices with their start and end apart: 24 -> 24, of which waited for: 16 -> 16; matrix products, arithmetic and copies ran while one was open for 2% -> 2% of each run, Pallas kernels for 0% -> 2%
where the time goes in v4:
time: 130 us; the launch traced here: 129 us
  waiting for transfers between devices  58.1 us (45%)
  starting transfers between devices  57 us (44%)
  Pallas kernels  6.83 us (5%)
  local copies, waits for them, and re-layouts  3 us (2%)
  other arithmetic  2.22 us (2%)
  matrix products  1.51 us (1%)
    ppermute x15, waiting for transfers between devices, hop(): return lax.ppermute(value, ('dp', 'fsdp'), hops)  48.9 us
    ppermute x15, starting transfers between devices, hop(): return lax.ppermute(value, ('dp', 'fsdp'), hops)  32.5 us
    ppermute x8, starting transfers between devices, swap(): return lax.ppermute(value, 'dp', swaps)  19.4 us
    ppermute x1, waiting for transfers between devices, rebalance(): arrived = lax.ppermute(message, 'dp', pairs)  9.18 us
    ppermute x1, starting transfers between devices, rebalance(): arrived = lax.ppermute(message, 'dp', pairs)  5.1 us
    pallas_call x1, Pallas kernels, encode(): pl.pallas_call(functools.partial(attend_kernel, feat_total), in_specs=[pl...  4.44 us
  transfers between devices with their start and end apart: 24, of which 16 were waited for; matrix products, arithmetic and copies ran while one was open for 2% of the time, Pallas kernels for 2%

profile of v4, /device:TPU:6, one launch (start us, length us, event | category | flops | bytes accessed | tf_op | source)
XLA Modules:
  0.0 129.4 jit_solution(7943768361806364110)
XLA Ops:
  0.0 0.7 not_bitcast_fusion
  0.8 0.8 select_reduce_fusion
  1.6 1.8 %gather_fusion = bf16[24,80,128]{2,1,0:T(8,128)(2,1)S(1)} fusion(bf16[48,80,128]{2,1,0:T(8,128)(2,1)} %param.8, s32[1024]{0:T(1024)S(1)} %pad_clamp_fusion.1), kind=kCustom, calls=%fused_computation | custom fusion | bytes 983136 | tf_op jit(solution)/shard_map/gather | solution.py:149
  3.5 5.1 %collective-permute-start = (bf16[25,80,128]{2,1,0:T(8,128)(2,1)S(1)}, bf16[25,80,128]{2,1,0:T(8,128)(2,1)S(1)}, u32[]{:S(2)}, u32[]{:S(2)}) collective-permute-start(bf16[25,80,128]{2,1,0:T(8,128)(2,1)S(1)} %fusion.6), channel_id=1, source_target_pairs={{0,256},{16,272},{32,288},{48,304},{64,320},{80,336},{96,352},{112... | collective-permute-start | bytes 1536008 | tf_op jit(solution)/shard_map/ppermute | solution.py:151
  9.1 0.4 convert_reduce_fusion
  9.6 1.5 %fusion = bf16[256,1280]{1,0:T(8,128)(2,1)S(1)} fusion(s32[1280]{0:T(1024)S(1)} %add.145, bf16[240,1280]{1,0:T(8,128)(2,1)S(1)} %get-tuple-element.56), kind=kOutput, calls=%fused_computation.3 | convolution fusion | flops 840499200 | bytes 1274880 | tf_op jit(solution)/shard_map/dot_general | solution.py:89
  11.1 9.2 %collective-permute-done = bf16[25,80,128]{2,1,0:T(8,128)(2,1)S(1)} collective-permute-done((bf16[25,80,128]{2,1,0:T(8,128)(2,1)S(1)}, bf16[25,80,128]{2,1,0:T(8,128)(2,1)S(1)}, u32[]{:S(2)}, u32[]{:S(2)}) %collective-permute-start) | collective-permute-done | bytes 512032 | tf_op jit(solution)/shard_map/ppermute | solution.py:151
  20.7 0.6 gather_fusion.1
  21.3 1.9 %collective-permute-start.2 = (bf16[24,80,128]{2,1,0:T(8,128)(2,1)S(1)}, bf16[24,80,128]{2,1,0:T(8,128)(2,1)S(1)}, u32[]{:S(2)}, u32[]{:S(2)}) collective-permute-start(bf16[24,80,128]{2,1,0:T(8,128)(2,1)S(1)} %gather_fusion.1), channel_id=1, source_target_pairs={{0,16},{16,0},{32,48},{48,32},{64,80},{80,64},{96,112},{112,96},{1... | collective-permute-start | bytes 1474568 | tf_op jit(solution)/shard_map/ppermute | solution.py:176
  23.3 3.8 %collective-permute-start.1 = (bf16[24,80,128]{2,1,0:T(8,128)(2,1)S(1)}, bf16[24,80,128]{2,1,0:T(8,128)(2,1)S(1)}, u32[]{:S(2)}, u32[]{:S(2)}) collective-permute-start(bf16[24,80,128]{2,1,0:T(8,128)(2,1)S(1)} %gather_fusion.1), channel_id=1, source_target_pairs={{0,1},{1,2},{2,3},{3,4},{4,5},{5,6},{6,7},{7,8},{8,9},{9,10},{10,1... | collective-permute-start | bytes 1474568 | tf_op jit(solution)/shard_map/ppermute | solution.py:179
  27.1 3.8 %collective-permute-start.4 = (bf16[24,80,128]{2,1,0:T(8,128)(2,1)S(1)}, bf16[24,80,128]{2,1,0:T(8,128)(2,1)S(1)}, u32[]{:S(2)}, u32[]{:S(2)}) collective-permute-start(bf16[24,80,128]{2,1,0:T(8,128)(2,1)S(1)} %collective-permute-done.2), channel_id=1, source_target_pairs={{0,1},{1,2},{2,3},{3,4},{4,5},{5,6},{6,7},{7,8},{8,9},{9,10},{10,1... | collective-permute-start | bytes 1474568 | tf_op jit(solution)/shard_map/ppermute | solution.py:179
  30.9 10.5 %collective-permute-done.1.refs_1_ = bf16[24,80,128]{2,1,0:T(8,128)(2,1)S(1)} collective-permute-done((bf16[24,80,128]{2,1,0:T(8,128)(2,1)S(1)}, bf16[24,80,128]{2,1,0:T(8,128)(2,1)S(1)}, u32[]{:S(2)}, u32[]{:S(2)}) %collective-permute-start.1) | collective-permute-done | bytes 491552 | tf_op jit(solution)/shard_map/ppermute | solution.py:179
  41.5 1.9 %collective-permute-start.3 = (bf16[24,80,128]{2,1,0:T(8,128)(2,1)S(1)}, bf16[24,80,128]{2,1,0:T(8,128)(2,1)S(1)}, u32[]{:S(2)}, u32[]{:S(2)}) collective-permute-start(bf16[24,80,128]{2,1,0:T(8,128)(2,1)S(1)} %collective-permute-done.1.refs_1_), channel_id=1, source_target_pairs={{0,1},{1,2},{2,3},{3,4},{4,5},{5,6},{6,7},{7,8},{8,9},{9,10},{10,1... | collective-permute-start | bytes 1474568 | tf_op jit(solution)/shard_map/ppermute | solution.py:179
  43.4 3.3 %collective-permute-done.4 = bf16[24,80,128]{2,1,0:T(8,128)(2,1)S(1)} collective-permute-done((bf16[24,80,128]{2,1,0:T(8,128)(2,1)S(1)}, bf16[24,80,128]{2,1,0:T(8,128)(2,1)S(1)}, u32[]{:S(2)}, u32[]{:S(2)}) %collective-permute-start.4) | collective-permute-done | bytes 491552 | tf_op jit(solution)/shard_map/ppermute | solution.py:179
  46.7 1.9 %collective-permute-start.6 = (bf16[24,80,128]{2,1,0:T(8,128)(2,1)S(1)}, bf16[24,80,128]{2,1,0:T(8,128)(2,1)S(1)}, u32[]{:S(2)}, u32[]{:S(2)}) collective-permute-start(bf16[24,80,128]{2,1,0:T(8,128)(2,1)S(1)} %collective-permute-done.4), channel_id=1, source_target_pairs={{0,1},{1,2},{2,3},{3,4},{4,5},{5,6},{6,7},{7,8},{8,9},{9,10},{10,1... | collective-permute-start | bytes 1474568 | tf_op jit(solution)/shard_map/ppermute | solution.py:179
  48.7 4.7 %collective-permute-done.3.refs_2_ = bf16[24,80,128]{2,1,0:T(8,128)(2,1)S(1)} collective-permute-done((bf16[24,80,128]{2,1,0:T(8,128)(2,1)S(1)}, bf16[24,80,128]{2,1,0:T(8,128)(2,1)S(1)}, u32[]{:S(2)}, u32[]{:S(2)}) %collective-permute-start.3) | collective-permute-done | bytes 491552 | tf_op jit(solution)/shard_map/ppermute | solution.py:179
  53.4 1.9 %collective-permute-start.5 = (bf16[24,80,128]{2,1,0:T(8,128)(2,1)S(1)}, bf16[24,80,128]{2,1,0:T(8,128)(2,1)S(1)}, u32[]{:S(2)}, u32[]{:S(2)}) collective-permute-start(bf16[24,80,128]{2,1,0:T(8,128)(2,1)S(1)} %collective-permute-done.3.refs_2_), channel_id=1, source_target_pairs={{0,1},{1,2},{2,3},{3,4},{4,5},{5,6},{6,7},{7,8},{8,9},{9,10},{10,1... | collective-permute-start | bytes 1474568 | tf_op jit(solution)/shard_map/ppermute | solution.py:179
  55.3 3.0 %collective-permute-start.9 = (bf16[24,80,128]{2,1,0:T(8,128)(2,1)S(1)}, bf16[24,80,128]{2,1,0:T(8,128)(2,1)S(1)}, u32[]{:S(2)}, u32[]{:S(2)}) collective-permute-start(bf16[24,80,128]{2,1,0:T(8,128)(2,1)S(1)} %collective-permute-done.4), channel_id=1, source_target_pairs={{0,16},{16,0},{32,48},{48,32},{64,80},{80,64},{96,112},{112,96},{1... | collective-permute-start | bytes 1474568 | tf_op jit(solution)/shard_map/ppermute | solution.py:176
  58.4 0.3 collective-permute-done.6
  58.7 1.9 %collective-permute-start.8 = (bf16[24,80,128]{2,1,0:T(8,128)(2,1)S(1)}, bf16[24,80,128]{2,1,0:T(8,128)(2,1)S(1)}, u32[]{:S(2)}, u32[]{:S(2)}) collective-permute-start(bf16[24,80,128]{2,1,0:T(8,128)(2,1)S(1)} %collective-permute-done.6), channel_id=1, source_target_pairs={{0,1},{1,2},{2,3},{3,4},{4,5},{5,6},{6,7},{7,8},{8,9},{9,10},{10,1... | collective-permute-start | bytes 1474568 | tf_op jit(solution)/shard_map/ppermute | solution.py:179
  60.6 4.7 %collective-permute-done.5.refs_3_ = bf16[24,80,128]{2,1,0:T(8,128)(2,1)S(1)} collective-permute-done((bf16[24,80,128]{2,1,0:T(8,128)(2,1)S(1)}, bf16[24,80,128]{2,1,0:T(8,128)(2,1)S(1)}, u32[]{:S(2)}, u32[]{:S(2)}) %collective-permute-start.5) | collective-permute-done | bytes 491552 | tf_op jit(solution)/shard_map/ppermute | solution.py:179
  65.3 1.9 %collective-permute-start.7 = (bf16[24,80,128]{2,1,0:T(8,128)(2,1)S(1)}, bf16[24,80,128]{2,1,0:T(8,128)(2,1)S(1)}, u32[]{:S(2)}, u32[]{:S(2)}) collective-permute-start(bf16[24,80,128]{2,1,0:T(8,128)(2,1)S(1)} %collective-permute-done.5.refs_3_), channel_id=1, source_target_pairs={{0,1},{1,2},{2,3},{3,4},{4,5},{5,6},{6,7},{7,8},{8,9},{9,10},{10,1... | collective-permute-start | bytes 1474568 | tf_op jit(solution)/shard_map/ppermute | solution.py:179
  67.2 1.9 %collective-permute-start.12 = (bf16[24,80,128]{2,1,0:T(8,128)(2,1)S(1)}, bf16[24,80,128]{2,1,0:T(8,128)(2,1)S(1)}, u32[]{:S(2)}, u32[]{:S(2)}) collective-permute-start(bf16[24,80,128]{2,1,0:T(8,128)(2,1)S(1)} %collective-permute-done.6), channel_id=1, source_target_pairs={{0,16},{16,0},{32,48},{48,32},{64,80},{80,64},{96,112},{112,96},{1... | collective-permute-start | bytes 1474568 | tf_op jit(solution)/shard_map/ppermute | solution.py:176
  69.2 1.4 %collective-permute-done.8 = bf16[24,80,128]{2,1,0:T(8,128)(2,1)S(1)} collective-permute-done((bf16[24,80,128]{2,1,0:T(8,128)(2,1)S(1)}, bf16[24,80,128]{2,1,0:T(8,128)(2,1)S(1)}, u32[]{:S(2)}, u32[]{:S(2)}) %collective-permute-start.8) | collective-permute-done | bytes 491552 | tf_op jit(solution)/shard_map/ppermute | solution.py:179
  70.6 1.9 %collective-permute-start.11 = (bf16[24,80,128]{2,1,0:T(8,128)(2,1)S(1)}, bf16[24,80,128]{2,1,0:T(8,128)(2,1)S(1)}, u32[]{:S(2)}, u32[]{:S(2)}) collective-permute-start(bf16[24,80,128]{2,1,0:T(8,128)(2,1)S(1)} %collective-permute-done.8), channel_id=1, source_target_pairs={{0,1},{1,2},{2,3},{3,4},{4,5},{5,6},{6,7},{7,8},{8,9},{9,10},{10,1... | collective-permute-start | bytes 1474568 | tf_op jit(solution)/shard_map/ppermute | solution.py:179
  72.5 4.7 %collective-permute-done.7.refs_4_ = bf16[24,80,128]{2,1,0:T(8,128)(2,1)S(1)} collective-permute-done((bf16[24,80,128]{2,1,0:T(8,128)(2,1)S(1)}, bf16[24,80,128]{2,1,0:T(8,128)(2,1)S(1)}, u32[]{:S(2)}, u32[]{:S(2)}) %collective-permute-start.7) | collective-permute-done | bytes 491552 | tf_op jit(solution)/shard_map/ppermute | solution.py:179
  77.2 1.9 %collective-permute-start.10 = (bf16[24,80,128]{2,1,0:T(8,128)(2,1)S(1)}, bf16[24,80,128]{2,1,0:T(8,128)(2,1)S(1)}, u32[]{:S(2)}, u32[]{:S(2)}) collective-permute-start(bf16[24,80,128]{2,1,0:T(8,128)(2,1)S(1)} %collective-permute-done.7.refs_4_), channel_id=1, source_target_pairs={{0,1},{1,2},{2,3},{3,4},{4,5},{5,6},{6,7},{7,8},{8,9},{9,10},{10,1... | collective-permute-start | bytes 1474568 | tf_op jit(solution)/shard_map/ppermute | solution.py:179
  79.2 1.9 %collective-permute-start.15 = (bf16[24,80,128]{2,1,0:T(8,128)(2,1)S(1)}, bf16[24,80,128]{2,1,0:T(8,128)(2,1)S(1)}, u32[]{:S(2)}, u32[]{:S(2)}) collective-permute-start(bf16[24,80,128]{2,1,0:T(8,128)(2,1)S(1)} %collective-permute-done.8), channel_id=1, source_target_pairs={{0,16},{16,0},{32,48},{48,32},{64,80},{80,64},{96,112},{112,96},{1... | collective-permute-start | bytes 1474568 | tf_op jit(solution)/shard_map/ppermute | solution.py:176
  81.1 1.4 %collective-permute-done.11 = bf16[24,80,128]{2,1,0:T(8,128)(2,1)S(1)} collective-permute-done((bf16[24,80,128]{2,1,0:T(8,128)(2,1)S(1)}, bf16[24,80,128]{2,1,0:T(8,128)(2,1)S(1)}, u32[]{:S(2)}, u32[]{:S(2)}) %collective-permute-start.11) | collective-permute-done | bytes 491552 | tf_op jit(solution)/shard_map/ppermute | solution.py:179
  82.5 1.9 %collective-permute-start.14 = (bf16[24,80,128]{2,1,0:T(8,128)(2,1)S(1)}, bf16[24,80,128]{2,1,0:T(8,128)(2,1)S(1)}, u32[]{:S(2)}, u32[]{:S(2)}) collective-permute-start(bf16[24,80,128]{2,1,0:T(8,128)(2,1)S(1)} %collective-permute-done.11), channel_id=1, source_target_pairs={{0,1},{1,2},{2,3},{3,4},{4,5},{5,6},{6,7},{7,8},{8,9},{9,10},{10,1... | collective-permute-start | bytes 1474568 | tf_op jit(solution)/shard_map/ppermute | solution.py:179
  84.4 4.7 %collective-permute-done.10.refs_5_ = bf16[24,80,128]{2,1,0:T(8,128)(2,1)S(1)} collective-permute-done((bf16[24,80,128]{2,1,0:T(8,128)(2,1)S(1)}, bf16[24,80,128]{2,1,0:T(8,128)(2,1)S(1)}, u32[]{:S(2)}, u32[]{:S(2)}) %collective-permute-start.10) | collective-permute-done | bytes 491552 | tf_op jit(solution)/shard_map/ppermute | solution.py:179
  89.2 1.9 %collective-permute-start.13 = (bf16[24,80,128]{2,1,0:T(8,128)(2,1)S(1)}, bf16[24,80,128]{2,1,0:T(8,128)(2,1)S(1)}, u32[]{:S(2)}, u32[]{:S(2)}) collective-permute-start(bf16[24,80,128]{2,1,0:T(8,128)(2,1)S(1)} %collective-permute-done.10.refs_5_), channel_id=1, source_target_pairs={{0,1},{1,2},{2,3},{3,4},{4,5},{5,6},{6,7},{7,8},{8,9},{9,10},{10,1... | collective-permute-start | bytes 1474568 | tf_op jit(solution)/shard_map/ppermute | solution.py:179
  91.1 1.9 %collective-permute-start.18 = (bf16[24,80,128]{2,1,0:T(8,128)(2,1)S(1)}, bf16[24,80,128]{2,1,0:T(8,128)(2,1)S(1)}, u32[]{:S(2)}, u32[]{:S(2)}) collective-permute-start(bf16[24,80,128]{2,1,0:T(8,128)(2,1)S(1)} %collective-permute-done.11), channel_id=1, source_target_pairs={{0,16},{16,0},{32,48},{48,32},{64,80},{80,64},{96,112},{112,96},{1... | collective-permute-start | bytes 1474568 | tf_op jit(solution)/shard_map/ppermute | solution.py:176
  93.0 1.4 %collective-permute-done.14 = bf16[24,80,128]{2,1,0:T(8,128)(2,1)S(1)} collective-permute-done((bf16[24,80,128]{2,1,0:T(8,128)(2,1)S(1)}, bf16[24,80,128]{2,1,0:T(8,128)(2,1)S(1)}, u32[]{:S(2)}, u32[]{:S(2)}) %collective-permute-start.14) | collective-permute-done | bytes 491552 | tf_op jit(solution)/shard_map/ppermute | solution.py:179
  94.4 1.9 %collective-permute-start.17 = (bf16[24,80,128]{2,1,0:T(8,128)(2,1)S(1)}, bf16[24,80,128]{2,1,0:T(8,128)(2,1)S(1)}, u32[]{:S(2)}, u32[]{:S(2)}) collective-permute-start(bf16[24,80,128]{2,1,0:T(8,128)(2,1)S(1)} %collective-permute-done.14), channel_id=1, source_target_pairs={{0,1},{1,2},{2,3},{3,4},{4,5},{5,6},{6,7},{7,8},{8,9},{9,10},{10,1... | collective-permute-start | bytes 1474568 | tf_op jit(solution)/shard_map/ppermute | solution.py:179
  96.3 3.9 %collective-permute-start.19 = (bf16[24,80,128]{2,1,0:T(8,128)(2,1)S(1)}, bf16[24,80,128]{2,1,0:T(8,128)(2,1)S(1)}, u32[]{:S(2)}, u32[]{:S(2)}) collective-permute-start(bf16[24,80,128]{2,1,0:T(8,128)(2,1)S(1)} %collective-permute-done.14), channel_id=1, source_target_pairs={{0,16},{16,0},{32,48},{48,32},{64,80},{80,64},{96,112},{112,96},{1... | collective-permute-start | bytes 1474568 | tf_op jit(solution)/shard_map/ppermute | solution.py:176
  100.3 0.8 collective-permute-done.13.refs_6_
  101.1 1.9 %collective-permute-start.16 = (bf16[24,80,128]{2,1,0:T(8,128)(2,1)S(1)}, bf16[24,80,128]{2,1,0:T(8,128)(2,1)S(1)}, u32[]{:S(2)}, u32[]{:S(2)}) collective-permute-start(bf16[24,80,128]{2,1,0:T(8,128)(2,1)S(1)} %collective-permute-done.13.refs_6_), channel_id=1, source_target_pairs={{0,1},{1,2},{2,3},{3,4},{4,5},{5,6},{6,7},{7,8},{8,9},{9,10},{10,1... | collective-permute-start | bytes 1474568 | tf_op jit(solution)/shard_map/ppermute | solution.py:179
  103.0 3.3 %collective-permute-done.17 = bf16[24,80,128]{2,1,0:T(8,128)(2,1)S(1)} collective-permute-done((bf16[24,80,128]{2,1,0:T(8,128)(2,1)S(1)}, bf16[24,80,128]{2,1,0:T(8,128)(2,1)S(1)}, u32[]{:S(2)}, u32[]{:S(2)}) %collective-permute-start.17) | collective-permute-done | bytes 491552 | tf_op jit(solution)/shard_map/ppermute | solution.py:179
  106.4 1.9 %collective-permute-start.20 = (bf16[24,80,128]{2,1,0:T(8,128)(2,1)S(1)}, bf16[24,80,128]{2,1,0:T(8,128)(2,1)S(1)}, u32[]{:S(2)}, u32[]{:S(2)}) collective-permute-start(bf16[24,80,128]{2,1,0:T(8,128)(2,1)S(1)} %collective-permute-done.17), channel_id=1, source_target_pairs={{0,1},{1,2},{2,3},{3,4},{4,5},{5,6},{6,7},{7,8},{8,9},{9,10},{10,1... | collective-permute-start | bytes 1474568 | tf_op jit(solution)/shard_map/ppermute | solution.py:179
  108.3 2.8 %collective-permute-start.21 = (bf16[24,80,128]{2,1,0:T(8,128)(2,1)S(1)}, bf16[24,80,128]{2,1,0:T(8,128)(2,1)S(1)}, u32[]{:S(2)}, u32[]{:S(2)}) collective-permute-start(bf16[24,80,128]{2,1,0:T(8,128)(2,1)S(1)} %collective-permute-done.17), channel_id=1, source_target_pairs={{0,16},{16,0},{32,48},{48,32},{64,80},{80,64},{96,112},{112,96},{1... | collective-permute-start | bytes 1474568 | tf_op jit(solution)/shard_map/ppermute | solution.py:176
  111.1 1.9 %collective-permute-done.16.refs_7_ = bf16[24,80,128]{2,1,0:T(8,128)(2,1)S(1)} collective-permute-done((bf16[24,80,128]{2,1,0:T(8,128)(2,1)S(1)}, bf16[24,80,128]{2,1,0:T(8,128)(2,1)S(1)}, u32[]{:S(2)}, u32[]{:S(2)}) %collective-permute-start.16) | collective-permute-done | bytes 491552 | tf_op jit(solution)/shard_map/ppermute | solution.py:179
  113.0 1.9 %collective-permute-start.22 = (bf16[24,80,128]{2,1,0:T(8,128)(2,1)S(1)}, bf16[24,80,128]{2,1,0:T(8,128)(2,1)S(1)}, u32[]{:S(2)}, u32[]{:S(2)}) collective-permute-start(bf16[24,80,128]{2,1,0:T(8,128)(2,1)S(1)} %collective-permute-done.16.refs_7_), channel_id=1, source_target_pairs={{0,1},{1,2},{2,3},{3,4},{4,5},{5,6},{6,7},{7,8},{8,9},{9,10},{10,1... | collective-permute-start | bytes 1474568 | tf_op jit(solution)/shard_map/ppermute | solution.py:179
  114.9 3.4 %collective-permute-done.20 = bf16[24,80,128]{2,1,0:T(8,128)(2,1)S(1)} collective-permute-done((bf16[24,80,128]{2,1,0:T(8,128)(2,1)S(1)}, bf16[24,80,128]{2,1,0:T(8,128)(2,1)S(1)}, u32[]{:S(2)}, u32[]{:S(2)}) %collective-permute-start.20) | collective-permute-done | bytes 491552 | tf_op jit(solution)/shard_map/ppermute | solution.py:179
  118.3 1.9 %collective-permute-start.23 = (bf16[24,80,128]{2,1,0:T(8,128)(2,1)S(1)}, bf16[24,80,128]{2,1,0:T(8,128)(2,1)S(1)}, u32[]{:S(2)}, u32[]{:S(2)}) collective-permute-start(bf16[24,80,128]{2,1,0:T(8,128)(2,1)S(1)} %collective-permute-done.20), channel_id=1, source_target_pairs={{0,16},{16,0},{32,48},{48,32},{64,80},{80,64},{96,112},{112,96},{1... | collective-permute-start | bytes 1474568 | tf_op jit(solution)/shard_map/ppermute | solution.py:176
  120.4 2.4 %shard_map.82.before = f32[2,256,1536]{2,1,0:T(8,128)S(1)} custom-call(bf16[256,1120]{1,0:T(8,128)(2,1)S(1)} %slice.11.weight, bf16[24,80,128]{2,1,0:T(8,128)(2,1)S(1)} %gather_fusion.1, bf16[24,80,128]{2,1,0:T(8,128)(2,1)S(1)} %collective-permute-done.1.refs_1_, bf16[24,80,128]{2,1,0:T(8,128)(2,1)S(1)} %collective-permute-done.3.refs_2_, ...), custom_call_target="tpu_custom_call" | custom-call | flops 1761607680 | bytes 10027008 | tf_op jit(solution)/shard_map/pallas_call | solution.py:105
  122.8 2.1 %collective-permute-done.22.refs_0_ = bf16[24,80,128]{2,1,0:T(8,128)(2,1)S(1)} collective-permute-done((bf16[24,80,128]{2,1,0:T(8,128)(2,1)S(1)}, bf16[24,80,128]{2,1,0:T(8,128)(2,1)S(1)}, u32[]{:S(2)}, u32[]{:S(2)}) %collective-permute-start.22) | collective-permute-done | bytes 491552 | tf_op jit(solution)/shard_map/ppermute | solution.py:179
  124.9 4.4 %shard_map.83 = bf16[24,80,128]{2,1,0:T(8,128)(2,1)} custom-call(s32[24]{0:T(128)S(1)} %compare_select_fusion.2.counts, bf16[256,160]{1,0:T(8,128)(2,1)S(1)} %slice.10.weight, f32[240,128]{1,0:T(8,128)S(1)} %broadcast_in_dim.66.column_sum, f32[240,128]{1,0:T(8,128)S(1)} %broadcast_in_dim.67.shift, f32[2,256,1536]{2,1,0:T(8,128)S(1)} %shard_map.82.before, ...), custom_call_target="tpu_custom_call" | custom-call | flops 251658240 | bytes 3145728 | tf_op jit(solution)/shard_map/pallas_call | solution.py:117
  (36 shorter events, 0.8 us)
Async XLA Ops:
  0.0 9.1 %copy-start.1 = (bf16[240,1280]{1,0:T(8,128)(2,1)S(1)}, bf16[240,1280]{1,0:T(8,128)(2,1)}, u32[]{:S(2)}) copy-start(bf16[240,1280]{1,0:T(8,128)(2,1)} %param.14) | copy-start | bytes 1843204
  0.0 9.1 %copy-start.3 = (f32[1280]{0:T(1024)S(1)}, f32[1280]{0:T(1024)}, u32[]{:S(2)}) copy-start(f32[1280]{0:T(1024)} %param.13) | copy-start | bytes 15364
  0.0 9.1 %copy-start.2 = (f32[1280]{0:T(1024)S(1)}, f32[1280]{0:T(1024)}, u32[]{:S(2)}) copy-start(f32[1280]{0:T(1024)} %param.12) | copy-start | bytes 15364
  3.5 6.1 %copy-start.4 = (bf16[240]{0:T(256)(128)(2,1)S(1)}, bf16[240]{0:T(256)(128)(2,1)}, u32[]{:S(2)}) copy-start(bf16[240]{0:T(256)(128)(2,1)} %param.15) | copy-start | bytes 1444
  3.5 16.8 %collective-permute-start = (bf16[25,80,128]{2,1,0:T(8,128)(2,1)S(1)}, bf16[25,80,128]{2,1,0:T(8,128)(2,1)S(1)}, u32[]{:S(2)}, u32[]{:S(2)}) collective-permute-start(bf16[25,80,128]{2,1,0:T(8,128)(2,1)S(1)} %fusion.6), channel_id=1, source_target_pairs={{0,256},{16,272},{32,288},{48,304},{64,320},{80,336},{96,352},{112... | collective-permute-start | bytes 1536008 | tf_op jit(solution)/shard_map/ppermute | solution.py:151
  9.6 10.9 %copy-start = (bf16[48,80,128]{2,1,0:T(8,128)(2,1)S(1)}, bf16[48,80,128]{2,1,0:T(8,128)(2,1)}, u32[]{:S(2)}) copy-start(bf16[48,80,128]{2,1,0:T(8,128)(2,1)} %param.8) | copy-start | bytes 2949124
  21.3 5.8 %collective-permute-start.2 = (bf16[24,80,128]{2,1,0:T(8,128)(2,1)S(1)}, bf16[24,80,128]{2,1,0:T(8,128)(2,1)S(1)}, u32[]{:S(2)}, u32[]{:S(2)}) collective-permute-start(bf16[24,80,128]{2,1,0:T(8,128)(2,1)S(1)} %gather_fusion.1), channel_id=1, source_target_pairs={{0,16},{16,0},{32,48},{48,32},{64,80},{80,64},{96,112},{112,96},{1... | collective-permute-start | bytes 1474568 | tf_op jit(solution)/shard_map/ppermute | solution.py:176
  23.3 18.2 %collective-permute-start.1 = (bf16[24,80,128]{2,1,0:T(8,128)(2,1)S(1)}, bf16[24,80,128]{2,1,0:T(8,128)(2,1)S(1)}, u32[]{:S(2)}, u32[]{:S(2)}) collective-permute-start(bf16[24,80,128]{2,1,0:T(8,128)(2,1)S(1)} %gather_fusion.1), channel_id=1, source_target_pairs={{0,1},{1,2},{2,3},{3,4},{4,5},{5,6},{6,7},{7,8},{8,9},{9,10},{10,1... | collective-permute-start | bytes 1474568 | tf_op jit(solution)/shard_map/ppermute | solution.py:179
  27.1 19.6 %collective-permute-start.4 = (bf16[24,80,128]{2,1,0:T(8,128)(2,1)S(1)}, bf16[24,80,128]{2,1,0:T(8,128)(2,1)S(1)}, u32[]{:S(2)}, u32[]{:S(2)}) collective-permute-start(bf16[24,80,128]{2,1,0:T(8,128)(2,1)S(1)} %collective-permute-done.2), channel_id=1, source_target_pairs={{0,1},{1,2},{2,3},{3,4},{4,5},{5,6},{6,7},{7,8},{8,9},{9,10},{10,1... | collective-permute-start | bytes 1474568 | tf_op jit(solution)/shard_map/ppermute | solution.py:179
  41.5 11.9 %collective-permute-start.3 = (bf16[24,80,128]{2,1,0:T(8,128)(2,1)S(1)}, bf16[24,80,128]{2,1,0:T(8,128)(2,1)S(1)}, u32[]{:S(2)}, u32[]{:S(2)}) collective-permute-start(bf16[24,80,128]{2,1,0:T(8,128)(2,1)S(1)} %collective-permute-done.1.refs_1_), channel_id=1, source_target_pairs={{0,1},{1,2},{2,3},{3,4},{4,5},{5,6},{6,7},{7,8},{8,9},{9,10},{10,1... | collective-permute-start | bytes 1474568 | tf_op jit(solution)/shard_map/ppermute | solution.py:179
  46.7 11.9 %collective-permute-start.6 = (bf16[24,80,128]{2,1,0:T(8,128)(2,1)S(1)}, bf16[24,80,128]{2,1,0:T(8,128)(2,1)S(1)}, u32[]{:S(2)}, u32[]{:S(2)}) collective-permute-start(bf16[24,80,128]{2,1,0:T(8,128)(2,1)S(1)} %collective-permute-done.4), channel_id=1, source_target_pairs={{0,1},{1,2},{2,3},{3,4},{4,5},{5,6},{6,7},{7,8},{8,9},{9,10},{10,1... | collective-permute-start | bytes 1474568 | tf_op jit(solution)/shard_map/ppermute | solution.py:179
  53.4 11.9 %collective-permute-start.5 = (bf16[24,80,128]{2,1,0:T(8,128)(2,1)S(1)}, bf16[24,80,128]{2,1,0:T(8,128)(2,1)S(1)}, u32[]{:S(2)}, u32[]{:S(2)}) collective-permute-start(bf16[24,80,128]{2,1,0:T(8,128)(2,1)S(1)} %collective-permute-done.3.refs_2_), channel_id=1, source_target_pairs={{0,1},{1,2},{2,3},{3,4},{4,5},{5,6},{6,7},{7,8},{8,9},{9,10},{10,1... | collective-permute-start | bytes 1474568 | tf_op jit(solution)/shard_map/ppermute | solution.py:179
  55.3 13.9 %collective-permute-start.9 = (bf16[24,80,128]{2,1,0:T(8,128)(2,1)S(1)}, bf16[24,80,128]{2,1,0:T(8,128)(2,1)S(1)}, u32[]{:S(2)}, u32[]{:S(2)}) collective-permute-start(bf16[24,80,128]{2,1,0:T(8,128)(2,1)S(1)} %collective-permute-done.4), channel_id=1, source_target_pairs={{0,16},{16,0},{32,48},{48,32},{64,80},{80,64},{96,112},{112,96},{1... | collective-permute-start | bytes 1474568 | tf_op jit(solution)/shard_map/ppermute | solution.py:176
  58.7 11.9 %collective-permute-start.8 = (bf16[24,80,128]{2,1,0:T(8,128)(2,1)S(1)}, bf16[24,80,128]{2,1,0:T(8,128)(2,1)S(1)}, u32[]{:S(2)}, u32[]{:S(2)}) collective-permute-start(bf16[24,80,128]{2,1,0:T(8,128)(2,1)S(1)} %collective-permute-done.6), channel_id=1, source_target_pairs={{0,1},{1,2},{2,3},{3,4},{4,5},{5,6},{6,7},{7,8},{8,9},{9,10},{10,1... | collective-permute-start | bytes 1474568 | tf_op jit(solution)/shard_map/ppermute | solution.py:179
  65.3 11.9 %collective-permute-start.7 = (bf16[24,80,128]{2,1,0:T(8,128)(2,1)S(1)}, bf16[24,80,128]{2,1,0:T(8,128)(2,1)S(1)}, u32[]{:S(2)}, u32[]{:S(2)}) collective-permute-start(bf16[24,80,128]{2,1,0:T(8,128)(2,1)S(1)} %collective-permute-done.5.refs_3_), channel_id=1, source_target_pairs={{0,1},{1,2},{2,3},{3,4},{4,5},{5,6},{6,7},{7,8},{8,9},{9,10},{10,1... | collective-permute-start | bytes 1474568 | tf_op jit(solution)/shard_map/ppermute | solution.py:179
  67.2 13.9 %collective-permute-start.12 = (bf16[24,80,128]{2,1,0:T(8,128)(2,1)S(1)}, bf16[24,80,128]{2,1,0:T(8,128)(2,1)S(1)}, u32[]{:S(2)}, u32[]{:S(2)}) collective-permute-start(bf16[24,80,128]{2,1,0:T(8,128)(2,1)S(1)} %collective-permute-done.6), channel_id=1, source_target_pairs={{0,16},{16,0},{32,48},{48,32},{64,80},{80,64},{96,112},{112,96},{1... | collective-permute-start | bytes 1474568 | tf_op jit(solution)/shard_map/ppermute | solution.py:176
  70.6 11.9 %collective-permute-start.11 = (bf16[24,80,128]{2,1,0:T(8,128)(2,1)S(1)}, bf16[24,80,128]{2,1,0:T(8,128)(2,1)S(1)}, u32[]{:S(2)}, u32[]{:S(2)}) collective-permute-start(bf16[24,80,128]{2,1,0:T(8,128)(2,1)S(1)} %collective-permute-done.8), channel_id=1, source_target_pairs={{0,1},{1,2},{2,3},{3,4},{4,5},{5,6},{6,7},{7,8},{8,9},{9,10},{10,1... | collective-permute-start | bytes 1474568 | tf_op jit(solution)/shard_map/ppermute | solution.py:179
  77.2 11.9 %collective-permute-start.10 = (bf16[24,80,128]{2,1,0:T(8,128)(2,1)S(1)}, bf16[24,80,128]{2,1,0:T(8,128)(2,1)S(1)}, u32[]{:S(2)}, u32[]{:S(2)}) collective-permute-start(bf16[24,80,128]{2,1,0:T(8,128)(2,1)S(1)} %collective-permute-done.7.refs_4_), channel_id=1, source_target_pairs={{0,1},{1,2},{2,3},{3,4},{4,5},{5,6},{6,7},{7,8},{8,9},{9,10},{10,1... | collective-permute-start | bytes 1474568 | tf_op jit(solution)/shard_map/ppermute | solution.py:179
  79.2 13.9 %collective-permute-start.15 = (bf16[24,80,128]{2,1,0:T(8,128)(2,1)S(1)}, bf16[24,80,128]{2,1,0:T(8,128)(2,1)S(1)}, u32[]{:S(2)}, u32[]{:S(2)}) collective-permute-start(bf16[24,80,128]{2,1,0:T(8,128)(2,1)S(1)} %collective-permute-done.8), channel_id=1, source_target_pairs={{0,16},{16,0},{32,48},{48,32},{64,80},{80,64},{96,112},{112,96},{1... | collective-permute-start | bytes 1474568 | tf_op jit(solution)/shard_map/ppermute | solution.py:176
  82.5 11.9 %collective-permute-start.14 = (bf16[24,80,128]{2,1,0:T(8,128)(2,1)S(1)}, bf16[24,80,128]{2,1,0:T(8,128)(2,1)S(1)}, u32[]{:S(2)}, u32[]{:S(2)}) collective-permute-start(bf16[24,80,128]{2,1,0:T(8,128)(2,1)S(1)} %collective-permute-done.11), channel_id=1, source_target_pairs={{0,1},{1,2},{2,3},{3,4},{4,5},{5,6},{6,7},{7,8},{8,9},{9,10},{10,1... | collective-permute-start | bytes 1474568 | tf_op jit(solution)/shard_map/ppermute | solution.py:179
  89.2 11.9 %collective-permute-start.13 = (bf16[24,80,128]{2,1,0:T(8,128)(2,1)S(1)}, bf16[24,80,128]{2,1,0:T(8,128)(2,1)S(1)}, u32[]{:S(2)}, u32[]{:S(2)}) collective-permute-start(bf16[24,80,128]{2,1,0:T(8,128)(2,1)S(1)} %collective-permute-done.10.refs_5_), channel_id=1, source_target_pairs={{0,1},{1,2},{2,3},{3,4},{4,5},{5,6},{6,7},{7,8},{8,9},{9,10},{10,1... | collective-permute-start | bytes 1474568 | tf_op jit(solution)/shard_map/ppermute | solution.py:179
  91.1 11.9 %collective-permute-start.18 = (bf16[24,80,128]{2,1,0:T(8,128)(2,1)S(1)}, bf16[24,80,128]{2,1,0:T(8,128)(2,1)S(1)}, u32[]{:S(2)}, u32[]{:S(2)}) collective-permute-start(bf16[24,80,128]{2,1,0:T(8,128)(2,1)S(1)} %collective-permute-done.11), channel_id=1, source_target_pairs={{0,16},{16,0},{32,48},{48,32},{64,80},{80,64},{96,112},{112,96},{1... | collective-permute-start | bytes 1474568 | tf_op jit(solution)/shard_map/ppermute | solution.py:176
  94.4 11.9 %collective-permute-start.17 = (bf16[24,80,128]{2,1,0:T(8,128)(2,1)S(1)}, bf16[24,80,128]{2,1,0:T(8,128)(2,1)S(1)}, u32[]{:S(2)}, u32[]{:S(2)}) collective-permute-start(bf16[24,80,128]{2,1,0:T(8,128)(2,1)S(1)} %collective-permute-done.14), channel_id=1, source_target_pairs={{0,1},{1,2},{2,3},{3,4},{4,5},{5,6},{6,7},{7,8},{8,9},{9,10},{10,1... | collective-permute-start | bytes 1474568 | tf_op jit(solution)/shard_map/ppermute | solution.py:179
  96.3 10.0 %collective-permute-start.19 = (bf16[24,80,128]{2,1,0:T(8,128)(2,1)S(1)}, bf16[24,80,128]{2,1,0:T(8,128)(2,1)S(1)}, u32[]{:S(2)}, u32[]{:S(2)}) collective-permute-start(bf16[24,80,128]{2,1,0:T(8,128)(2,1)S(1)} %collective-permute-done.14), channel_id=1, source_target_pairs={{0,16},{16,0},{32,48},{48,32},{64,80},{80,64},{96,112},{112,96},{1... | collective-permute-start | bytes 1474568 | tf_op jit(solution)/shard_map/ppermute | solution.py:176
  101.1 11.9 %collective-permute-start.16 = (bf16[24,80,128]{2,1,0:T(8,128)(2,1)S(1)}, bf16[24,80,128]{2,1,0:T(8,128)(2,1)S(1)}, u32[]{:S(2)}, u32[]{:S(2)}) collective-permute-start(bf16[24,80,128]{2,1,0:T(8,128)(2,1)S(1)} %collective-permute-done.13.refs_6_), channel_id=1, source_target_pairs={{0,1},{1,2},{2,3},{3,4},{4,5},{5,6},{6,7},{7,8},{8,9},{9,10},{10,1... | collective-permute-start | bytes 1474568 | tf_op jit(solution)/shard_map/ppermute | solution.py:179
  106.4 11.9 %collective-permute-start.20 = (bf16[24,80,128]{2,1,0:T(8,128)(2,1)S(1)}, bf16[24,80,128]{2,1,0:T(8,128)(2,1)S(1)}, u32[]{:S(2)}, u32[]{:S(2)}) collective-permute-start(bf16[24,80,128]{2,1,0:T(8,128)(2,1)S(1)} %collective-permute-done.17), channel_id=1, source_target_pairs={{0,1},{1,2},{2,3},{3,4},{4,5},{5,6},{6,7},{7,8},{8,9},{9,10},{10,1... | collective-permute-start | bytes 1474568 | tf_op jit(solution)/shard_map/ppermute | solution.py:179
  108.3 12.1 %collective-permute-start.21 = (bf16[24,80,128]{2,1,0:T(8,128)(2,1)S(1)}, bf16[24,80,128]{2,1,0:T(8,128)(2,1)S(1)}, u32[]{:S(2)}, u32[]{:S(2)}) collective-permute-start(bf16[24,80,128]{2,1,0:T(8,128)(2,1)S(1)} %collective-permute-done.17), channel_id=1, source_target_pairs={{0,16},{16,0},{32,48},{48,32},{64,80},{80,64},{96,112},{112,96},{1... | collective-permute-start | bytes 1474568 | tf_op jit(solution)/shard_map/ppermute | solution.py:176
  113.0 11.9 %collective-permute-start.22 = (bf16[24,80,128]{2,1,0:T(8,128)(2,1)S(1)}, bf16[24,80,128]{2,1,0:T(8,128)(2,1)S(1)}, u32[]{:S(2)}, u32[]{:S(2)}) collective-permute-start(bf16[24,80,128]{2,1,0:T(8,128)(2,1)S(1)} %collective-permute-done.16.refs_7_), channel_id=1, source_target_pairs={{0,1},{1,2},{2,3},{3,4},{4,5},{5,6},{6,7},{7,8},{8,9},{9,10},{10,1... | collective-permute-start | bytes 1474568 | tf_op jit(solution)/shard_map/ppermute | solution.py:179
  118.3 6.7 %collective-permute-start.23 = (bf16[24,80,128]{2,1,0:T(8,128)(2,1)S(1)}, bf16[24,80,128]{2,1,0:T(8,128)(2,1)S(1)}, u32[]{:S(2)}, u32[]{:S(2)}) collective-permute-start(bf16[24,80,128]{2,1,0:T(8,128)(2,1)S(1)} %collective-permute-done.20), channel_id=1, source_target_pairs={{0,16},{16,0},{32,48},{48,32},{64,80},{80,64},{96,112},{112,96},{1... | collective-permute-start | bytes 1474568 | tf_op jit(solution)/shard_map/ppermute | solution.py:176

commit v5 on v4

--- a/solution.py
+++ b/solution.py
@@ -188,9 +188,12 @@
         if step == half - 2:
             other[-1], swapped[step - 1] = lax.optimization_barrier((other[-1], swapped[step - 1]))
         mine.append(hop(mine[-1]))
-        swapped[step] = swap(received)
-    early = mine[:half] + [swapped[step] for step in range(1, half - 1)]
-    return early, [mine[half], swapped[half - 1]]
+        if step != half - 2:
+            swapped[step] = swap(received)
+    before_last = lax.optimization_barrier((other[half - 2], other[half - 1]))[0]
+    swapped[half - 2] = swap(before_last)
+    early = mine[:half] + [swapped[step] for step in range(1, half - 2)]
+    return early, [mine[half], swapped[half - 2], swapped[half - 1]]
 
 
 def shards(patches, patch_count, dest_rank, dest_slot, ln_gain, ln_bias, w_qkv, b_qkv):
@@ -199,8 +202,9 @@
     place = lax.axis_index("fsdp")
     sense = sense_of(lax.axis_index("dp"))
     origins = [(place - sense * step) % ring for step in range(half)]
-    origins += [(place + sense * step) % ring for step in range(1, half - 1)]
-    origins += [(place - sense * half) % ring, (place + sense * (half - 1)) % ring]
+    origins += [(place + sense * step) % ring for step in range(1, half - 2)]
+    origins += [(place - sense * half) % ring]
+    origins += [(place + sense * step) % ring for step in range(half - 2, half)]
     weight, column_sum, shift = folded(
         ln_gain, ln_bias, w_qkv, b_qkv, origins, patches.shape[2]
     )

time: 130 us -> 132 us (1.015)
  waiting for transfers between devices: 58.1 us -> 60.9 us
    ppermute x15, waiting for transfers between devices: 48.9 us -> 51.7 us  [hop(): return lax.ppermute(value, ('dp', 'fsdp'), hops)]
where the time goes in v5:
time: 132 us; the launch traced here: 131 us
  waiting for transfers between devices  60.9 us (46%)
  starting transfers between devices  56.1 us (42%)
  Pallas kernels  6.92 us (5%)
  local copies, waits for them, and re-layouts  3 us (2%)
  other arithmetic  2.22 us (2%)
  matrix products  1.51 us (1%)
    ppermute x15, waiting for transfers between devices, hop(): return lax.ppermute(value, ('dp', 'fsdp'), hops)  51.7 us
    ppermute x15, starting transfers between devices, hop(): return lax.ppermute(value, ('dp', 'fsdp'), hops)  32.5 us
    ppermute x8, starting transfers between devices, swap(): return lax.ppermute(value, 'dp', swaps)  18.5 us
    ppermute x1, waiting for transfers between devices, rebalance(): arrived = lax.ppermute(message, 'dp', pairs)  9.18 us
    ppermute x1, starting transfers between devices, rebalance(): arrived = lax.ppermute(message, 'dp', pairs)  5.1 us
    pallas_call x1, Pallas kernels, encode(): pl.pallas_call(functools.partial(attend_kernel, feat_total), in_specs=[pl...  4.5 us
  transfers between devices with their start and end apart: 24, of which 16 were waited for; matrix products, arithmetic and copies ran while one was open for 2% of the time, Pallas kernels for 2%

profile of v5, /device:TPU:6, one launch (start us, length us, event | category | flops | bytes accessed | tf_op | source)
XLA Modules:
  0.0 131.4 jit_solution(8489954379866680786)
XLA Ops:
  0.0 0.7 not_bitcast_fusion
  0.8 0.8 select_reduce_fusion
  1.6 1.8 %gather_fusion = bf16[24,80,128]{2,1,0:T(8,128)(2,1)S(1)} fusion(bf16[48,80,128]{2,1,0:T(8,128)(2,1)} %param.8, s32[1024]{0:T(1024)S(1)} %pad_clamp_fusion.1), kind=kCustom, calls=%fused_computation | custom fusion | bytes 983136 | tf_op jit(solution)/shard_map/gather | solution.py:149
  3.5 5.1 %collective-permute-start = (bf16[25,80,128]{2,1,0:T(8,128)(2,1)S(1)}, bf16[25,80,128]{2,1,0:T(8,128)(2,1)S(1)}, u32[]{:S(2)}, u32[]{:S(2)}) collective-permute-start(bf16[25,80,128]{2,1,0:T(8,128)(2,1)S(1)} %fusion.6), channel_id=1, source_target_pairs={{0,256},{16,272},{32,288},{48,304},{64,320},{80,336},{96,352},{112... | collective-permute-start | bytes 1536008 | tf_op jit(solution)/shard_map/ppermute | solution.py:151
  9.1 0.4 convert_reduce_fusion
  9.6 1.5 %fusion = bf16[256,1280]{1,0:T(8,128)(2,1)S(1)} fusion(s32[1280]{0:T(1024)S(1)} %add.145, bf16[240,1280]{1,0:T(8,128)(2,1)S(1)} %get-tuple-element.58), kind=kOutput, calls=%fused_computation.3 | convolution fusion | flops 840499200 | bytes 1274880 | tf_op jit(solution)/shard_map/dot_general | solution.py:89
  11.1 9.2 %collective-permute-done = bf16[25,80,128]{2,1,0:T(8,128)(2,1)S(1)} collective-permute-done((bf16[25,80,128]{2,1,0:T(8,128)(2,1)S(1)}, bf16[25,80,128]{2,1,0:T(8,128)(2,1)S(1)}, u32[]{:S(2)}, u32[]{:S(2)}) %collective-permute-start) | collective-permute-done | bytes 512032 | tf_op jit(solution)/shard_map/ppermute | solution.py:151
  20.7 0.6 gather_fusion.1
  21.3 1.9 %collective-permute-start.2 = (bf16[24,80,128]{2,1,0:T(8,128)(2,1)S(1)}, bf16[24,80,128]{2,1,0:T(8,128)(2,1)S(1)}, u32[]{:S(2)}, u32[]{:S(2)}) collective-permute-start(bf16[24,80,128]{2,1,0:T(8,128)(2,1)S(1)} %gather_fusion.1), channel_id=1, source_target_pairs={{0,16},{16,0},{32,48},{48,32},{64,80},{80,64},{96,112},{112,96},{1... | collective-permute-start | bytes 1474568 | tf_op jit(solution)/shard_map/ppermute | solution.py:176
  23.3 3.8 %collective-permute-start.1 = (bf16[24,80,128]{2,1,0:T(8,128)(2,1)S(1)}, bf16[24,80,128]{2,1,0:T(8,128)(2,1)S(1)}, u32[]{:S(2)}, u32[]{:S(2)}) collective-permute-start(bf16[24,80,128]{2,1,0:T(8,128)(2,1)S(1)} %gather_fusion.1), channel_id=1, source_target_pairs={{0,1},{1,2},{2,3},{3,4},{4,5},{5,6},{6,7},{7,8},{8,9},{9,10},{10,1... | collective-permute-start | bytes 1474568 | tf_op jit(solution)/shard_map/ppermute | solution.py:179
  27.1 3.8 %collective-permute-start.4 = (bf16[24,80,128]{2,1,0:T(8,128)(2,1)S(1)}, bf16[24,80,128]{2,1,0:T(8,128)(2,1)S(1)}, u32[]{:S(2)}, u32[]{:S(2)}) collective-permute-start(bf16[24,80,128]{2,1,0:T(8,128)(2,1)S(1)} %collective-permute-done.2), channel_id=1, source_target_pairs={{0,1},{1,2},{2,3},{3,4},{4,5},{5,6},{6,7},{7,8},{8,9},{9,10},{10,1... | collective-permute-start | bytes 1474568 | tf_op jit(solution)/shard_map/ppermute | solution.py:179
  30.9 10.5 %collective-permute-done.1.refs_1_ = bf16[24,80,128]{2,1,0:T(8,128)(2,1)S(1)} collective-permute-done((bf16[24,80,128]{2,1,0:T(8,128)(2,1)S(1)}, bf16[24,80,128]{2,1,0:T(8,128)(2,1)S(1)}, u32[]{:S(2)}, u32[]{:S(2)}) %collective-permute-start.1) | collective-permute-done | bytes 491552 | tf_op jit(solution)/shard_map/ppermute | solution.py:179
  41.5 1.9 %collective-permute-start.3 = (bf16[24,80,128]{2,1,0:T(8,128)(2,1)S(1)}, bf16[24,80,128]{2,1,0:T(8,128)(2,1)S(1)}, u32[]{:S(2)}, u32[]{:S(2)}) collective-permute-start(bf16[24,80,128]{2,1,0:T(8,128)(2,1)S(1)} %collective-permute-done.1.refs_1_), channel_id=1, source_target_pairs={{0,1},{1,2},{2,3},{3,4},{4,5},{5,6},{6,7},{7,8},{8,9},{9,10},{10,1... | collective-permute-start | bytes 1474568 | tf_op jit(solution)/shard_map/ppermute | solution.py:179
  43.4 3.3 %collective-permute-done.4 = bf16[24,80,128]{2,1,0:T(8,128)(2,1)S(1)} collective-permute-done((bf16[24,80,128]{2,1,0:T(8,128)(2,1)S(1)}, bf16[24,80,128]{2,1,0:T(8,128)(2,1)S(1)}, u32[]{:S(2)}, u32[]{:S(2)}) %collective-permute-start.4) | collective-permute-done | bytes 491552 | tf_op jit(solution)/shard_map/ppermute | solution.py:179
  46.7 1.9 %collective-permute-start.6 = (bf16[24,80,128]{2,1,0:T(8,128)(2,1)S(1)}, bf16[24,80,128]{2,1,0:T(8,128)(2,1)S(1)}, u32[]{:S(2)}, u32[]{:S(2)}) collective-permute-start(bf16[24,80,128]{2,1,0:T(8,128)(2,1)S(1)} %collective-permute-done.4), channel_id=1, source_target_pairs={{0,1},{1,2},{2,3},{3,4},{4,5},{5,6},{6,7},{7,8},{8,9},{9,10},{10,1... | collective-permute-start | bytes 1474568 | tf_op jit(solution)/shard_map/ppermute | solution.py:179
  48.7 4.7 %collective-permute-done.3.refs_2_ = bf16[24,80,128]{2,1,0:T(8,128)(2,1)S(1)} collective-permute-done((bf16[24,80,128]{2,1,0:T(8,128)(2,1)S(1)}, bf16[24,80,128]{2,1,0:T(8,128)(2,1)S(1)}, u32[]{:S(2)}, u32[]{:S(2)}) %collective-permute-start.3) | collective-permute-done | bytes 491552 | tf_op jit(solution)/shard_map/ppermute | solution.py:179
  53.4 1.9 %collective-permute-start.5 = (bf16[24,80,128]{2,1,0:T(8,128)(2,1)S(1)}, bf16[24,80,128]{2,1,0:T(8,128)(2,1)S(1)}, u32[]{:S(2)}, u32[]{:S(2)}) collective-permute-start(bf16[24,80,128]{2,1,0:T(8,128)(2,1)S(1)} %collective-permute-done.3.refs_2_), channel_id=1, source_target_pairs={{0,1},{1,2},{2,3},{3,4},{4,5},{5,6},{6,7},{7,8},{8,9},{9,10},{10,1... | collective-permute-start | bytes 1474568 | tf_op jit(solution)/shard_map/ppermute | solution.py:179
  55.3 3.0 %collective-permute-start.9 = (bf16[24,80,128]{2,1,0:T(8,128)(2,1)S(1)}, bf16[24,80,128]{2,1,0:T(8,128)(2,1)S(1)}, u32[]{:S(2)}, u32[]{:S(2)}) collective-permute-start(bf16[24,80,128]{2,1,0:T(8,128)(2,1)S(1)} %collective-permute-done.4), channel_id=1, source_target_pairs={{0,16},{16,0},{32,48},{48,32},{64,80},{80,64},{96,112},{112,96},{1... | collective-permute-start | bytes 1474568 | tf_op jit(solution)/shard_map/ppermute | solution.py:176
  58.4 0.3 collective-permute-done.6
  58.7 1.9 %collective-permute-start.8 = (bf16[24,80,128]{2,1,0:T(8,128)(2,1)S(1)}, bf16[24,80,128]{2,1,0:T(8,128)(2,1)S(1)}, u32[]{:S(2)}, u32[]{:S(2)}) collective-permute-start(bf16[24,80,128]{2,1,0:T(8,128)(2,1)S(1)} %collective-permute-done.6), channel_id=1, source_target_pairs={{0,1},{1,2},{2,3},{3,4},{4,5},{5,6},{6,7},{7,8},{8,9},{9,10},{10,1... | collective-permute-start | bytes 1474568 | tf_op jit(solution)/shard_map/ppermute | solution.py:179
  60.6 4.7 %collective-permute-done.5.refs_3_ = bf16[24,80,128]{2,1,0:T(8,128)(2,1)S(1)} collective-permute-done((bf16[24,80,128]{2,1,0:T(8,128)(2,1)S(1)}, bf16[24,80,128]{2,1,0:T(8,128)(2,1)S(1)}, u32[]{:S(2)}, u32[]{:S(2)}) %collective-permute-start.5) | collective-permute-done | bytes 491552 | tf_op jit(solution)/shard_map/ppermute | solution.py:179
  65.3 1.9 %collective-permute-start.7 = (bf16[24,80,128]{2,1,0:T(8,128)(2,1)S(1)}, bf16[24,80,128]{2,1,0:T(8,128)(2,1)S(1)}, u32[]{:S(2)}, u32[]{:S(2)}) collective-permute-start(bf16[24,80,128]{2,1,0:T(8,128)(2,1)S(1)} %collective-permute-done.5.refs_3_), channel_id=1, source_target_pairs={{0,1},{1,2},{2,3},{3,4},{4,5},{5,6},{6,7},{7,8},{8,9},{9,10},{10,1... | collective-permute-start | bytes 1474568 | tf_op jit(solution)/shard_map/ppermute | solution.py:179
  67.2 1.9 %collective-permute-start.12 = (bf16[24,80,128]{2,1,0:T(8,128)(2,1)S(1)}, bf16[24,80,128]{2,1,0:T(8,128)(2,1)S(1)}, u32[]{:S(2)}, u32[]{:S(2)}) collective-permute-start(bf16[24,80,128]{2,1,0:T(8,128)(2,1)S(1)} %collective-permute-done.6), channel_id=1, source_target_pairs={{0,16},{16,0},{32,48},{48,32},{64,80},{80,64},{96,112},{112,96},{1... | collective-permute-start | bytes 1474568 | tf_op jit(solution)/shard_map/ppermute | solution.py:176
  69.2 1.4 %collective-permute-done.8 = bf16[24,80,128]{2,1,0:T(8,128)(2,1)S(1)} collective-permute-done((bf16[24,80,128]{2,1,0:T(8,128)(2,1)S(1)}, bf16[24,80,128]{2,1,0:T(8,128)(2,1)S(1)}, u32[]{:S(2)}, u32[]{:S(2)}) %collective-permute-start.8) | collective-permute-done | bytes 491552 | tf_op jit(solution)/shard_map/ppermute | solution.py:179
  70.6 1.9 %collective-permute-start.11 = (bf16[24,80,128]{2,1,0:T(8,128)(2,1)S(1)}, bf16[24,80,128]{2,1,0:T(8,128)(2,1)S(1)}, u32[]{:S(2)}, u32[]{:S(2)}) collective-permute-start(bf16[24,80,128]{2,1,0:T(8,128)(2,1)S(1)} %collective-permute-done.8), channel_id=1, source_target_pairs={{0,1},{1,2},{2,3},{3,4},{4,5},{5,6},{6,7},{7,8},{8,9},{9,10},{10,1... | collective-permute-start | bytes 1474568 | tf_op jit(solution)/shard_map/ppermute | solution.py:179
  72.5 4.7 %collective-permute-done.7.refs_4_ = bf16[24,80,128]{2,1,0:T(8,128)(2,1)S(1)} collective-permute-done((bf16[24,80,128]{2,1,0:T(8,128)(2,1)S(1)}, bf16[24,80,128]{2,1,0:T(8,128)(2,1)S(1)}, u32[]{:S(2)}, u32[]{:S(2)}) %collective-permute-start.7) | collective-permute-done | bytes 491552 | tf_op jit(solution)/shard_map/ppermute | solution.py:179
  77.2 1.9 %collective-permute-start.10 = (bf16[24,80,128]{2,1,0:T(8,128)(2,1)S(1)}, bf16[24,80,128]{2,1,0:T(8,128)(2,1)S(1)}, u32[]{:S(2)}, u32[]{:S(2)}) collective-permute-start(bf16[24,80,128]{2,1,0:T(8,128)(2,1)S(1)} %collective-permute-done.7.refs_4_), channel_id=1, source_target_pairs={{0,1},{1,2},{2,3},{3,4},{4,5},{5,6},{6,7},{7,8},{8,9},{9,10},{10,1... | collective-permute-start | bytes 1474568 | tf_op jit(solution)/shard_map/ppermute | solution.py:179
  79.2 1.9 %collective-permute-start.15 = (bf16[24,80,128]{2,1,0:T(8,128)(2,1)S(1)}, bf16[24,80,128]{2,1,0:T(8,128)(2,1)S(1)}, u32[]{:S(2)}, u32[]{:S(2)}) collective-permute-start(bf16[24,80,128]{2,1,0:T(8,128)(2,1)S(1)} %collective-permute-done.8), channel_id=1, source_target_pairs={{0,16},{16,0},{32,48},{48,32},{64,80},{80,64},{96,112},{112,96},{1... | collective-permute-start | bytes 1474568 | tf_op jit(solution)/shard_map/ppermute | solution.py:176
  81.1 1.4 %collective-permute-done.11 = bf16[24,80,128]{2,1,0:T(8,128)(2,1)S(1)} collective-permute-done((bf16[24,80,128]{2,1,0:T(8,128)(2,1)S(1)}, bf16[24,80,128]{2,1,0:T(8,128)(2,1)S(1)}, u32[]{:S(2)}, u32[]{:S(2)}) %collective-permute-start.11) | collective-permute-done | bytes 491552 | tf_op jit(solution)/shard_map/ppermute | solution.py:179
  82.5 1.9 %collective-permute-start.14 = (bf16[24,80,128]{2,1,0:T(8,128)(2,1)S(1)}, bf16[24,80,128]{2,1,0:T(8,128)(2,1)S(1)}, u32[]{:S(2)}, u32[]{:S(2)}) collective-permute-start(bf16[24,80,128]{2,1,0:T(8,128)(2,1)S(1)} %collective-permute-done.11), channel_id=1, source_target_pairs={{0,1},{1,2},{2,3},{3,4},{4,5},{5,6},{6,7},{7,8},{8,9},{9,10},{10,1... | collective-permute-start | bytes 1474568 | tf_op jit(solution)/shard_map/ppermute | solution.py:179
  84.4 4.7 %collective-permute-done.10.refs_5_ = bf16[24,80,128]{2,1,0:T(8,128)(2,1)S(1)} collective-permute-done((bf16[24,80,128]{2,1,0:T(8,128)(2,1)S(1)}, bf16[24,80,128]{2,1,0:T(8,128)(2,1)S(1)}, u32[]{:S(2)}, u32[]{:S(2)}) %collective-permute-start.10) | collective-permute-done | bytes 491552 | tf_op jit(solution)/shard_map/ppermute | solution.py:179
  89.2 1.9 %collective-permute-start.13 = (bf16[24,80,128]{2,1,0:T(8,128)(2,1)S(1)}, bf16[24,80,128]{2,1,0:T(8,128)(2,1)S(1)}, u32[]{:S(2)}, u32[]{:S(2)}) collective-permute-start(bf16[24,80,128]{2,1,0:T(8,128)(2,1)S(1)} %collective-permute-done.10.refs_5_), channel_id=1, source_target_pairs={{0,1},{1,2},{2,3},{3,4},{4,5},{5,6},{6,7},{7,8},{8,9},{9,10},{10,1... | collective-permute-start | bytes 1474568 | tf_op jit(solution)/shard_map/ppermute | solution.py:179
  91.1 1.9 %collective-permute-start.18 = (bf16[24,80,128]{2,1,0:T(8,128)(2,1)S(1)}, bf16[24,80,128]{2,1,0:T(8,128)(2,1)S(1)}, u32[]{:S(2)}, u32[]{:S(2)}) collective-permute-start(bf16[24,80,128]{2,1,0:T(8,128)(2,1)S(1)} %collective-permute-done.11), channel_id=1, source_target_pairs={{0,16},{16,0},{32,48},{48,32},{64,80},{80,64},{96,112},{112,96},{1... | collective-permute-start | bytes 1474568 | tf_op jit(solution)/shard_map/ppermute | solution.py:176
  93.0 1.4 %collective-permute-done.14 = bf16[24,80,128]{2,1,0:T(8,128)(2,1)S(1)} collective-permute-done((bf16[24,80,128]{2,1,0:T(8,128)(2,1)S(1)}, bf16[24,80,128]{2,1,0:T(8,128)(2,1)S(1)}, u32[]{:S(2)}, u32[]{:S(2)}) %collective-permute-start.14) | collective-permute-done | bytes 491552 | tf_op jit(solution)/shard_map/ppermute | solution.py:179
  94.4 1.9 %collective-permute-start.17 = (bf16[24,80,128]{2,1,0:T(8,128)(2,1)S(1)}, bf16[24,80,128]{2,1,0:T(8,128)(2,1)S(1)}, u32[]{:S(2)}, u32[]{:S(2)}) collective-permute-start(bf16[24,80,128]{2,1,0:T(8,128)(2,1)S(1)} %collective-permute-done.14), channel_id=1, source_target_pairs={{0,1},{1,2},{2,3},{3,4},{4,5},{5,6},{6,7},{7,8},{8,9},{9,10},{10,1... | collective-permute-start | bytes 1474568 | tf_op jit(solution)/shard_map/ppermute | solution.py:179
  96.3 3.9 %collective-permute-start.19 = (bf16[24,80,128]{2,1,0:T(8,128)(2,1)S(1)}, bf16[24,80,128]{2,1,0:T(8,128)(2,1)S(1)}, u32[]{:S(2)}, u32[]{:S(2)}) collective-permute-start(bf16[24,80,128]{2,1,0:T(8,128)(2,1)S(1)} %collective-permute-done.14), channel_id=1, source_target_pairs={{0,16},{16,0},{32,48},{48,32},{64,80},{80,64},{96,112},{112,96},{1... | collective-permute-start | bytes 1474568 | tf_op jit(solution)/shard_map/ppermute | solution.py:176
  100.3 0.8 collective-permute-done.13.refs_6_
  101.1 1.9 %collective-permute-start.16 = (bf16[24,80,128]{2,1,0:T(8,128)(2,1)S(1)}, bf16[24,80,128]{2,1,0:T(8,128)(2,1)S(1)}, u32[]{:S(2)}, u32[]{:S(2)}) collective-permute-start(bf16[24,80,128]{2,1,0:T(8,128)(2,1)S(1)} %collective-permute-done.13.refs_6_), channel_id=1, source_target_pairs={{0,1},{1,2},{2,3},{3,4},{4,5},{5,6},{6,7},{7,8},{8,9},{9,10},{10,1... | collective-permute-start | bytes 1474568 | tf_op jit(solution)/shard_map/ppermute | solution.py:179
  103.0 3.3 %collective-permute-done.17 = bf16[24,80,128]{2,1,0:T(8,128)(2,1)S(1)} collective-permute-done((bf16[24,80,128]{2,1,0:T(8,128)(2,1)S(1)}, bf16[24,80,128]{2,1,0:T(8,128)(2,1)S(1)}, u32[]{:S(2)}, u32[]{:S(2)}) %collective-permute-start.17) | collective-permute-done | bytes 491552 | tf_op jit(solution)/shard_map/ppermute | solution.py:179
  106.4 1.9 %collective-permute-start.20 = (bf16[24,80,128]{2,1,0:T(8,128)(2,1)S(1)}, bf16[24,80,128]{2,1,0:T(8,128)(2,1)S(1)}, u32[]{:S(2)}, u32[]{:S(2)}) collective-permute-start(bf16[24,80,128]{2,1,0:T(8,128)(2,1)S(1)} %collective-permute-done.17), channel_id=1, source_target_pairs={{0,1},{1,2},{2,3},{3,4},{4,5},{5,6},{6,7},{7,8},{8,9},{9,10},{10,1... | collective-permute-start | bytes 1474568 | tf_op jit(solution)/shard_map/ppermute | solution.py:179
  108.3 4.7 %collective-permute-done.16.refs_7_ = bf16[24,80,128]{2,1,0:T(8,128)(2,1)S(1)} collective-permute-done((bf16[24,80,128]{2,1,0:T(8,128)(2,1)S(1)}, bf16[24,80,128]{2,1,0:T(8,128)(2,1)S(1)}, u32[]{:S(2)}, u32[]{:S(2)}) %collective-permute-start.16) | collective-permute-done | bytes 491552 | tf_op jit(solution)/shard_map/ppermute | solution.py:179
  113.0 1.9 %collective-permute-start.22 = (bf16[24,80,128]{2,1,0:T(8,128)(2,1)S(1)}, bf16[24,80,128]{2,1,0:T(8,128)(2,1)S(1)}, u32[]{:S(2)}, u32[]{:S(2)}) collective-permute-start(bf16[24,80,128]{2,1,0:T(8,128)(2,1)S(1)} %collective-permute-done.17), channel_id=1, source_target_pairs={{0,16},{16,0},{32,48},{48,32},{64,80},{80,64},{96,112},{112,96},{1... | collective-permute-start | bytes 1474568 | tf_op jit(solution)/shard_map/ppermute | solution.py:176
  114.9 1.9 %collective-permute-start.21 = (bf16[24,80,128]{2,1,0:T(8,128)(2,1)S(1)}, bf16[24,80,128]{2,1,0:T(8,128)(2,1)S(1)}, u32[]{:S(2)}, u32[]{:S(2)}) collective-permute-start(bf16[24,80,128]{2,1,0:T(8,128)(2,1)S(1)} %collective-permute-done.16.refs_7_), channel_id=1, source_target_pairs={{0,1},{1,2},{2,3},{3,4},{4,5},{5,6},{6,7},{7,8},{8,9},{9,10},{10,1... | collective-permute-start | bytes 1474568 | tf_op jit(solution)/shard_map/ppermute | solution.py:179
  116.9 1.4 %collective-permute-done.20 = bf16[24,80,128]{2,1,0:T(8,128)(2,1)S(1)} collective-permute-done((bf16[24,80,128]{2,1,0:T(8,128)(2,1)S(1)}, bf16[24,80,128]{2,1,0:T(8,128)(2,1)S(1)}, u32[]{:S(2)}, u32[]{:S(2)}) %collective-permute-start.20) | collective-permute-done | bytes 491552 | tf_op jit(solution)/shard_map/ppermute | solution.py:179
  118.3 1.9 %collective-permute-start.23 = (bf16[24,80,128]{2,1,0:T(8,128)(2,1)S(1)}, bf16[24,80,128]{2,1,0:T(8,128)(2,1)S(1)}, u32[]{:S(2)}, u32[]{:S(2)}) collective-permute-start(bf16[24,80,128]{2,1,0:T(8,128)(2,1)S(1)} %collective-permute-done.20), channel_id=1, source_target_pairs={{0,16},{16,0},{32,48},{48,32},{64,80},{80,64},{96,112},{112,96},{1... | collective-permute-start | bytes 1474568 | tf_op jit(solution)/shard_map/ppermute | solution.py:176
  120.4 2.4 %shard_map.82.before = f32[2,256,1536]{2,1,0:T(8,128)S(1)} custom-call(bf16[256,1040]{1,0:T(8,128)(2,1)S(1)} %slice.11.weight, bf16[24,80,128]{2,1,0:T(8,128)(2,1)S(1)} %gather_fusion.1, bf16[24,80,128]{2,1,0:T(8,128)(2,1)S(1)} %collective-permute-done.1.refs_1_, bf16[24,80,128]{2,1,0:T(8,128)(2,1)S(1)} %collective-permute-done.3.refs_2_, ...), custom_call_target="tpu_custom_call" | custom-call | flops 1635778560 | bytes 9535488 | tf_op jit(solution)/shard_map/pallas_call | solution.py:105
  122.8 4.1 %collective-permute-done.21.refs_0_ = bf16[24,80,128]{2,1,0:T(8,128)(2,1)S(1)} collective-permute-done((bf16[24,80,128]{2,1,0:T(8,128)(2,1)S(1)}, bf16[24,80,128]{2,1,0:T(8,128)(2,1)S(1)}, u32[]{:S(2)}, u32[]{:S(2)}) %collective-permute-start.21) | collective-permute-done | bytes 491552 | tf_op jit(solution)/shard_map/ppermute | solution.py:179
  126.9 4.5 %shard_map.83 = bf16[24,80,128]{2,1,0:T(8,128)(2,1)} custom-call(s32[24]{0:T(128)S(1)} %compare_select_fusion.2.counts, bf16[256,240]{1,0:T(8,128)(2,1)S(1)} %slice.10.weight, f32[240,128]{1,0:T(8,128)S(1)} %broadcast_in_dim.66.column_sum, f32[240,128]{1,0:T(8,128)S(1)} %broadcast_in_dim.67.shift, f32[2,256,1536]{2,1,0:T(8,128)S(1)} %shard_map.82.before, ...), custom_call_target="tpu_custom_call" | custom-call | flops 377487360 | bytes 3145728 | tf_op jit(solution)/shard_map/pallas_call | solution.py:117
  (36 shorter events, 0.8 us)
Async XLA Ops:
  0.0 9.1 %copy-start.1 = (bf16[240,1280]{1,0:T(8,128)(2,1)S(1)}, bf16[240,1280]{1,0:T(8,128)(2,1)}, u32[]{:S(2)}) copy-start(bf16[240,1280]{1,0:T(8,128)(2,1)} %param.14) | copy-start | bytes 1843204
  0.0 9.1 %copy-start.3 = (f32[1280]{0:T(1024)S(1)}, f32[1280]{0:T(1024)}, u32[]{:S(2)}) copy-start(f32[1280]{0:T(1024)} %param.13) | copy-start | bytes 15364
  0.0 9.1 %copy-start.2 = (f32[1280]{0:T(1024)S(1)}, f32[1280]{0:T(1024)}, u32[]{:S(2)}) copy-start(f32[1280]{0:T(1024)} %param.12) | copy-start | bytes 15364
  3.5 6.1 %copy-start.4 = (bf16[240]{0:T(256)(128)(2,1)S(1)}, bf16[240]{0:T(256)(128)(2,1)}, u32[]{:S(2)}) copy-start(bf16[240]{0:T(256)(128)(2,1)} %param.15) | copy-start | bytes 1444
  3.5 16.8 %collective-permute-start = (bf16[25,80,128]{2,1,0:T(8,128)(2,1)S(1)}, bf16[25,80,128]{2,1,0:T(8,128)(2,1)S(1)}, u32[]{:S(2)}, u32[]{:S(2)}) collective-permute-start(bf16[25,80,128]{2,1,0:T(8,128)(2,1)S(1)} %fusion.6), channel_id=1, source_target_pairs={{0,256},{16,272},{32,288},{48,304},{64,320},{80,336},{96,352},{112... | collective-permute-start | bytes 1536008 | tf_op jit(solution)/shard_map/ppermute | solution.py:151
  9.6 10.9 %copy-start = (bf16[48,80,128]{2,1,0:T(8,128)(2,1)S(1)}, bf16[48,80,128]{2,1,0:T(8,128)(2,1)}, u32[]{:S(2)}) copy-start(bf16[48,80,128]{2,1,0:T(8,128)(2,1)} %param.8) | copy-start | bytes 2949124
  21.3 5.8 %collective-permute-start.2 = (bf16[24,80,128]{2,1,0:T(8,128)(2,1)S(1)}, bf16[24,80,128]{2,1,0:T(8,128)(2,1)S(1)}, u32[]{:S(2)}, u32[]{:S(2)}) collective-permute-start(bf16[24,80,128]{2,1,0:T(8,128)(2,1)S(1)} %gather_fusion.1), channel_id=1, source_target_pairs={{0,16},{16,0},{32,48},{48,32},{64,80},{80,64},{96,112},{112,96},{1... | collective-permute-start | bytes 1474568 | tf_op jit(solution)/shard_map/ppermute | solution.py:176
  23.3 18.2 %collective-permute-start.1 = (bf16[24,80,128]{2,1,0:T(8,128)(2,1)S(1)}, bf16[24,80,128]{2,1,0:T(8,128)(2,1)S(1)}, u32[]{:S(2)}, u32[]{:S(2)}) collective-permute-start(bf16[24,80,128]{2,1,0:T(8,128)(2,1)S(1)} %gather_fusion.1), channel_id=1, source_target_pairs={{0,1},{1,2},{2,3},{3,4},{4,5},{5,6},{6,7},{7,8},{8,9},{9,10},{10,1... | collective-permute-start | bytes 1474568 | tf_op jit(solution)/shard_map/ppermute | solution.py:179
  27.1 19.6 %collective-permute-start.4 = (bf16[24,80,128]{2,1,0:T(8,128)(2,1)S(1)}, bf16[24,80,128]{2,1,0:T(8,128)(2,1)S(1)}, u32[]{:S(2)}, u32[]{:S(2)}) collective-permute-start(bf16[24,80,128]{2,1,0:T(8,128)(2,1)S(1)} %collective-permute-done.2), channel_id=1, source_target_pairs={{0,1},{1,2},{2,3},{3,4},{4,5},{5,6},{6,7},{7,8},{8,9},{9,10},{10,1... | collective-permute-start | bytes 1474568 | tf_op jit(solution)/shard_map/ppermute | solution.py:179
  41.5 11.9 %collective-permute-start.3 = (bf16[24,80,128]{2,1,0:T(8,128)(2,1)S(1)}, bf16[24,80,128]{2,1,0:T(8,128)(2,1)S(1)}, u32[]{:S(2)}, u32[]{:S(2)}) collective-permute-start(bf16[24,80,128]{2,1,0:T(8,128)(2,1)S(1)} %collective-permute-done.1.refs_1_), channel_id=1, source_target_pairs={{0,1},{1,2},{2,3},{3,4},{4,5},{5,6},{6,7},{7,8},{8,9},{9,10},{10,1... | collective-permute-start | bytes 1474568 | tf_op jit(solution)/shard_map/ppermute | solution.py:179
  46.7 11.9 %collective-permute-start.6 = (bf16[24,80,128]{2,1,0:T(8,128)(2,1)S(1)}, bf16[24,80,128]{2,1,0:T(8,128)(2,1)S(1)}, u32[]{:S(2)}, u32[]{:S(2)}) collective-permute-start(bf16[24,80,128]{2,1,0:T(8,128)(2,1)S(1)} %collective-permute-done.4), channel_id=1, source_target_pairs={{0,1},{1,2},{2,3},{3,4},{4,5},{5,6},{6,7},{7,8},{8,9},{9,10},{10,1... | collective-permute-start | bytes 1474568 | tf_op jit(solution)/shard_map/ppermute | solution.py:179
  53.4 11.9 %collective-permute-start.5 = (bf16[24,80,128]{2,1,0:T(8,128)(2,1)S(1)}, bf16[24,80,128]{2,1,0:T(8,128)(2,1)S(1)}, u32[]{:S(2)}, u32[]{:S(2)}) collective-permute-start(bf16[24,80,128]{2,1,0:T(8,128)(2,1)S(1)} %collective-permute-done.3.refs_2_), channel_id=1, source_target_pairs={{0,1},{1,2},{2,3},{3,4},{4,5},{5,6},{6,7},{7,8},{8,9},{9,10},{10,1... | collective-permute-start | bytes 1474568 | tf_op jit(solution)/shard_map/ppermute | solution.py:179
  55.3 13.9 %collective-permute-start.9 = (bf16[24,80,128]{2,1,0:T(8,128)(2,1)S(1)}, bf16[24,80,128]{2,1,0:T(8,128)(2,1)S(1)}, u32[]{:S(2)}, u32[]{:S(2)}) collective-permute-start(bf16[24,80,128]{2,1,0:T(8,128)(2,1)S(1)} %collective-permute-done.4), channel_id=1, source_target_pairs={{0,16},{16,0},{32,48},{48,32},{64,80},{80,64},{96,112},{112,96},{1... | collective-permute-start | bytes 1474568 | tf_op jit(solution)/shard_map/ppermute | solution.py:176
  58.7 11.9 %collective-permute-start.8 = (bf16[24,80,128]{2,1,0:T(8,128)(2,1)S(1)}, bf16[24,80,128]{2,1,0:T(8,128)(2,1)S(1)}, u32[]{:S(2)}, u32[]{:S(2)}) collective-permute-start(bf16[24,80,128]{2,1,0:T(8,128)(2,1)S(1)} %collective-permute-done.6), channel_id=1, source_target_pairs={{0,1},{1,2},{2,3},{3,4},{4,5},{5,6},{6,7},{7,8},{8,9},{9,10},{10,1... | collective-permute-start | bytes 1474568 | tf_op jit(solution)/shard_map/ppermute | solution.py:179
  65.3 11.9 %collective-permute-start.7 = (bf16[24,80,128]{2,1,0:T(8,128)(2,1)S(1)}, bf16[24,80,128]{2,1,0:T(8,128)(2,1)S(1)}, u32[]{:S(2)}, u32[]{:S(2)}) collective-permute-start(bf16[24,80,128]{2,1,0:T(8,128)(2,1)S(1)} %collective-permute-done.5.refs_3_), channel_id=1, source_target_pairs={{0,1},{1,2},{2,3},{3,4},{4,5},{5,6},{6,7},{7,8},{8,9},{9,10},{10,1... | collective-permute-start | bytes 1474568 | tf_op jit(solution)/shard_map/ppermute | solution.py:179
  67.2 13.9 %collective-permute-start.12 = (bf16[24,80,128]{2,1,0:T(8,128)(2,1)S(1)}, bf16[24,80,128]{2,1,0:T(8,128)(2,1)S(1)}, u32[]{:S(2)}, u32[]{:S(2)}) collective-permute-start(bf16[24,80,128]{2,1,0:T(8,128)(2,1)S(1)} %collective-permute-done.6), channel_id=1, source_target_pairs={{0,16},{16,0},{32,48},{48,32},{64,80},{80,64},{96,112},{112,96},{1... | collective-permute-start | bytes 1474568 | tf_op jit(solution)/shard_map/ppermute | solution.py:176
  70.6 11.9 %collective-permute-start.11 = (bf16[24,80,128]{2,1,0:T(8,128)(2,1)S(1)}, bf16[24,80,128]{2,1,0:T(8,128)(2,1)S(1)}, u32[]{:S(2)}, u32[]{:S(2)}) collective-permute-start(bf16[24,80,128]{2,1,0:T(8,128)(2,1)S(1)} %collective-permute-done.8), channel_id=1, source_target_pairs={{0,1},{1,2},{2,3},{3,4},{4,5},{5,6},{6,7},{7,8},{8,9},{9,10},{10,1... | collective-permute-start | bytes 1474568 | tf_op jit(solution)/shard_map/ppermute | solution.py:179
  77.2 11.9 %collective-permute-start.10 = (bf16[24,80,128]{2,1,0:T(8,128)(2,1)S(1)}, bf16[24,80,128]{2,1,0:T(8,128)(2,1)S(1)}, u32[]{:S(2)}, u32[]{:S(2)}) collective-permute-start(bf16[24,80,128]{2,1,0:T(8,128)(2,1)S(1)} %collective-permute-done.7.refs_4_), channel_id=1, source_target_pairs={{0,1},{1,2},{2,3},{3,4},{4,5},{5,6},{6,7},{7,8},{8,9},{9,10},{10,1... | collective-permute-start | bytes 1474568 | tf_op jit(solution)/shard_map/ppermute | solution.py:179
  79.2 13.9 %collective-permute-start.15 = (bf16[24,80,128]{2,1,0:T(8,128)(2,1)S(1)}, bf16[24,80,128]{2,1,0:T(8,128)(2,1)S(1)}, u32[]{:S(2)}, u32[]{:S(2)}) collective-permute-start(bf16[24,80,128]{2,1,0:T(8,128)(2,1)S(1)} %collective-permute-done.8), channel_id=1, source_target_pairs={{0,16},{16,0},{32,48},{48,32},{64,80},{80,64},{96,112},{112,96},{1... | collective-permute-start | bytes 1474568 | tf_op jit(solution)/shard_map/ppermute | solution.py:176
  82.5 11.9 %collective-permute-start.14 = (bf16[24,80,128]{2,1,0:T(8,128)(2,1)S(1)}, bf16[24,80,128]{2,1,0:T(8,128)(2,1)S(1)}, u32[]{:S(2)}, u32[]{:S(2)}) collective-permute-start(bf16[24,80,128]{2,1,0:T(8,128)(2,1)S(1)} %collective-permute-done.11), channel_id=1, source_target_pairs={{0,1},{1,2},{2,3},{3,4},{4,5},{5,6},{6,7},{7,8},{8,9},{9,10},{10,1... | collective-permute-start | bytes 1474568 | tf_op jit(solution)/shard_map/ppermute | solution.py:179
  89.2 11.9 %collective-permute-start.13 = (bf16[24,80,128]{2,1,0:T(8,128)(2,1)S(1)}, bf16[24,80,128]{2,1,0:T(8,128)(2,1)S(1)}, u32[]{:S(2)}, u32[]{:S(2)}) collective-permute-start(bf16[24,80,128]{2,1,0:T(8,128)(2,1)S(1)} %collective-permute-done.10.refs_5_), channel_id=1, source_target_pairs={{0,1},{1,2},{2,3},{3,4},{4,5},{5,6},{6,7},{7,8},{8,9},{9,10},{10,1... | collective-permute-start | bytes 1474568 | tf_op jit(solution)/shard_map/ppermute | solution.py:179
  91.1 11.9 %collective-permute-start.18 = (bf16[24,80,128]{2,1,0:T(8,128)(2,1)S(1)}, bf16[24,80,128]{2,1,0:T(8,128)(2,1)S(1)}, u32[]{:S(2)}, u32[]{:S(2)}) collective-permute-start(bf16[24,80,128]{2,1,0:T(8,128)(2,1)S(1)} %collective-permute-done.11), channel_id=1, source_target_pairs={{0,16},{16,0},{32,48},{48,32},{64,80},{80,64},{96,112},{112,96},{1... | collective-permute-start | bytes 1474568 | tf_op jit(solution)/shard_map/ppermute | solution.py:176
  94.4 11.9 %collective-permute-start.17 = (bf16[24,80,128]{2,1,0:T(8,128)(2,1)S(1)}, bf16[24,80,128]{2,1,0:T(8,128)(2,1)S(1)}, u32[]{:S(2)}, u32[]{:S(2)}) collective-permute-start(bf16[24,80,128]{2,1,0:T(8,128)(2,1)S(1)} %collective-permute-done.14), channel_id=1, source_target_pairs={{0,1},{1,2},{2,3},{3,4},{4,5},{5,6},{6,7},{7,8},{8,9},{9,10},{10,1... | collective-permute-start | bytes 1474568 | tf_op jit(solution)/shard_map/ppermute | solution.py:179
  96.3 10.0 %collective-permute-start.19 = (bf16[24,80,128]{2,1,0:T(8,128)(2,1)S(1)}, bf16[24,80,128]{2,1,0:T(8,128)(2,1)S(1)}, u32[]{:S(2)}, u32[]{:S(2)}) collective-permute-start(bf16[24,80,128]{2,1,0:T(8,128)(2,1)S(1)} %collective-permute-done.14), channel_id=1, source_target_pairs={{0,16},{16,0},{32,48},{48,32},{64,80},{80,64},{96,112},{112,96},{1... | collective-permute-start | bytes 1474568 | tf_op jit(solution)/shard_map/ppermute | solution.py:176
  101.1 11.9 %collective-permute-start.16 = (bf16[24,80,128]{2,1,0:T(8,128)(2,1)S(1)}, bf16[24,80,128]{2,1,0:T(8,128)(2,1)S(1)}, u32[]{:S(2)}, u32[]{:S(2)}) collective-permute-start(bf16[24,80,128]{2,1,0:T(8,128)(2,1)S(1)} %collective-permute-done.13.refs_6_), channel_id=1, source_target_pairs={{0,1},{1,2},{2,3},{3,4},{4,5},{5,6},{6,7},{7,8},{8,9},{9,10},{10,1... | collective-permute-start | bytes 1474568 | tf_op jit(solution)/shard_map/ppermute | solution.py:179
  106.4 11.9 %collective-permute-start.20 = (bf16[24,80,128]{2,1,0:T(8,128)(2,1)S(1)}, bf16[24,80,128]{2,1,0:T(8,128)(2,1)S(1)}, u32[]{:S(2)}, u32[]{:S(2)}) collective-permute-start(bf16[24,80,128]{2,1,0:T(8,128)(2,1)S(1)} %collective-permute-done.17), channel_id=1, source_target_pairs={{0,1},{1,2},{2,3},{3,4},{4,5},{5,6},{6,7},{7,8},{8,9},{9,10},{10,1... | collective-permute-start | bytes 1474568 | tf_op jit(solution)/shard_map/ppermute | solution.py:179
  113.0 9.8 %collective-permute-start.22 = (bf16[24,80,128]{2,1,0:T(8,128)(2,1)S(1)}, bf16[24,80,128]{2,1,0:T(8,128)(2,1)S(1)}, u32[]{:S(2)}, u32[]{:S(2)}) collective-permute-start(bf16[24,80,128]{2,1,0:T(8,128)(2,1)S(1)} %collective-permute-done.17), channel_id=1, source_target_pairs={{0,16},{16,0},{32,48},{48,32},{64,80},{80,64},{96,112},{112,96},{1... | collective-permute-start | bytes 1474568 | tf_op jit(solution)/shard_map/ppermute | solution.py:176
  114.9 11.9 %collective-permute-start.21 = (bf16[24,80,128]{2,1,0:T(8,128)(2,1)S(1)}, bf16[24,80,128]{2,1,0:T(8,128)(2,1)S(1)}, u32[]{:S(2)}, u32[]{:S(2)}) collective-permute-start(bf16[24,80,128]{2,1,0:T(8,128)(2,1)S(1)} %collective-permute-done.16.refs_7_), channel_id=1, source_target_pairs={{0,1},{1,2},{2,3},{3,4},{4,5},{5,6},{6,7},{7,8},{8,9},{9,10},{10,1... | collective-permute-start | bytes 1474568 | tf_op jit(solution)/shard_map/ppermute | solution.py:179
  118.3 8.6 %collective-permute-start.23 = (bf16[24,80,128]{2,1,0:T(8,128)(2,1)S(1)}, bf16[24,80,128]{2,1,0:T(8,128)(2,1)S(1)}, u32[]{:S(2)}, u32[]{:S(2)}) collective-permute-start(bf16[24,80,128]{2,1,0:T(8,128)(2,1)S(1)} %collective-permute-done.20), channel_id=1, source_target_pairs={{0,16},{16,0},{32,48},{48,32},{64,80},{80,64},{96,112},{112,96},{1... | collective-permute-start | bytes 1474568 | tf_op jit(solution)/shard_map/ppermute | solution.py:176
